TPU v7x, 32 devices: a whole 2x2x4 slice. The times are simulated.
32 devices in a mesh: term: 4 (over z), pencil: 8 (over y, x, core).
Axes of the slice: x: 2, y: 2, z: 4, core: 2. Of those that a mesh axis runs over, the one named last changes fastest.
Arguments:
- present_acoustic: float32 [512, 16, 512], P('pencil'), may hold values from -6 to 6
- prior_acoustic: float32 [512, 16, 512], P('pencil'), may hold values from -6 to 6
- location_factor: float32 [16, 512, 16, 512], P('term', 'pencil'), may hold values from -1 to 1
- spectral_multiplier: float32 [16, 16, 512, 512], P('term', None, 'pencil'), may hold values from -6 to 6
- medium_kinds: int32 [512, 16, 512], P('pencil', 'term'), may hold values from 0 to 2
- organ_properties: float32 [3, 2], replicated, may hold values from 0.05 to 0.3
- thermal_increase: float32 [512, 16, 512], P('pencil', 'term'), may hold values from -6 to 6
Outputs:
- pressure_final: float32 [512, 16, 512], P('pencil', 'term')
- temperature_final: float32 [512, 16, 512], P('pencil', 'term')
Inputs may be any that keep to these rules, and one draw needn't show every extreme that they name: `medium_kinds`: tissue class of each cell: 0 bone, 1 brain, 2 water.
All inputs are finite; a program needn't handle non-finite values.
Results may differ from a plain program's by a relative error of at most 0.0001.
Values sent between devices are 32-bit elements; how exact they have to be, the bound alone decides.
No kernel may reach another device: no remote copies, remote signals or barrier semaphores. Data moves between devices by JAX's collectives and lax.ppermute only.
A program may use at most 192 MiB of HBM per device.

v0:
```python
import math

import jax
import jax.numpy as jnp
from jax import lax
from jax.sharding import PartitionSpec as P

WAVE_STEPS = 2
HEAT_STEPS = 2


DIFFUSION = 0.125


def padded_2(block, sides, width):
    for axis, dim in sides:
        count = lax.axis_size(axis)
        forward = [(i, i + 1) for i in range(count - 1)]
        backward = [(target, source) for source, target in forward]
        low = lax.ppermute(
            lax.slice_in_dim(block, block.shape[dim] - width, None, axis=dim), axis, forward
        )
        high = lax.ppermute(lax.slice_in_dim(block, 0, width, axis=dim), axis, backward)
        block = jnp.concatenate([low, block, high], axis=dim)
    return block


def matmul(left, right):
    return jnp.dot(left, right, precision=lax.Precision.HIGHEST, preferred_element_type=jnp.float32)


def contract(form, left, right):
    return jnp.einsum(
        form, left, right, precision=lax.Precision.HIGHEST, preferred_element_type=jnp.float32
    )


def cos_sin(row_freq, column_frequency, length):
    phase_index = row_freq[:, None] * column_frequency[None, :] % length
    phase_angles = phase_index.astype(jnp.float32) * (2.0 * math.pi / length)
    return (jnp.cos(phase_angles), jnp.sin(phase_angles))


def forward_rows(pressure, z_cosine, z_sine, y_cosine, y_sine):
    real_z = contract("rye,ec->ycr", pressure, z_cosine)
    imag_z = -contract("rye,ec->ycr", pressure, z_sine)
    real_part = contract("ky,ycr->kcr", y_cosine, real_z) + contract("ky,ycr->kcr", y_sine, imag_z)
    imag_part = contract("ky,ycr->kcr", y_cosine, imag_z) - contract("ky,ycr->kcr", y_sine, real_z)
    return jnp.stack([real_part, imag_part])


def forward_columns(spectrum, cosine_table, sine_table):
    length_x = spectrum.shape[3]
    flattened = spectrum.reshape(2, -1, length_x)
    real_part = matmul(flattened[0], cosine_table) + matmul(flattened[1], sine_table)
    imag_part = matmul(flattened[1], cosine_table) - matmul(flattened[0], sine_table)
    return jnp.stack([real_part, imag_part]).reshape(spectrum.shape)


def inverse_columns(weighted, cosine_table, sine_table):
    length_x = weighted.shape[4]
    real_in = weighted[:, 0].reshape(-1, length_x)
    imag_in = weighted[:, 1].reshape(-1, length_x)
    real_part = matmul(real_in, cosine_table) - matmul(imag_in, sine_table)
    imag_part = matmul(imag_in, cosine_table) + matmul(real_in, sine_table)
    inner_shape = (weighted.shape[0],) + weighted.shape[2:]
    return jnp.stack([real_part.reshape(inner_shape), imag_part.reshape(inner_shape)], axis=1)


def stencil_sum(padded):
    center = padded[1:-1, 1:-1, :]
    depth_pad = jnp.pad(center, ((0, 0), (0, 0), (1, 1)))
    near_sum = padded[2:, 1:-1, :] + padded[:-2, 1:-1, :]
    near_sum = near_sum + padded[1:-1, 2:, :] + padded[1:-1, :-2, :]
    near_sum = near_sum + depth_pad[:, :, 2:] + depth_pad[:, :, :-2]
    return (center, near_sum)


def heat_update(center, near_sum, perfuse, source):
    return center + DIFFUSION * (near_sum - 6.0 * center) - perfuse * center + source


def on_device(
    present_acoustic,
    prior_acoustic,
    location_factor,
    spectral_multiplier,
    medium_kinds,
    organ_properties,
    thermal_increase,
):
    term_count = lax.axis_size("term")
    pencil_count = lax.axis_size("pencil")
    rows_local = present_acoustic.shape[0]
    length_y = present_acoustic.shape[1]
    length_z = present_acoustic.shape[2]
    length_x = rows_local * pencil_count
    width_brick = length_y // term_count
    brick_start = lax.axis_index("term") * width_brick
    z_index = jnp.arange(length_z, dtype=jnp.int32)
    x_index = jnp.arange(length_x, dtype=jnp.int32)
    y_index = jnp.arange(length_y, dtype=jnp.int32)
    x_cos, x_sin = cos_sin(x_index, x_index, length_x)
    z_cos, z_sin = cos_sin(z_index, z_index, length_z)
    y_cos, y_sin = cos_sin(y_index, y_index, length_y)
    inverse_norm = 1.0 / (length_x * length_y * length_z)

    def to_brick(values):
        return lax.dynamic_slice_in_dim(values, brick_start, width_brick, 1)

    pick_cos, pick_sin = (z_cos, z_sin)
    previous = prior_acoustic
    current = present_acoustic
    dose_sum = jnp.zeros(medium_kinds.shape, jnp.float32)
    final_brick = dose_sum
    for turn_index in range(WAVE_STEPS):
        rows_spec = forward_rows(current, pick_cos, pick_sin, y_cos, y_sin)
        spectrum = lax.all_to_all(rows_spec, "pencil", split_axis=2, concat_axis=3, tiled=True)
        spectrum = forward_columns(spectrum, x_cos, x_sin)
        weighted = spectral_multiplier[:, None] * spectrum[None]
        term_restored = inverse_columns(weighted, x_cos, x_sin)
        restored = lax.all_to_all(term_restored, "pencil", split_axis=4, concat_axis=3, tiled=True)
        real_in = restored[:, 0]
        imag_in = restored[:, 1]
        real_y = contract("yk,nkzr->nyzr", y_cos, real_in) - contract(
            "yk,nkzr->nyzr", y_sin, imag_in
        )
        imag_y = contract("yk,nkzr->nyzr", y_cos, imag_in) + contract(
            "yk,nkzr->nyzr", y_sin, real_in
        )
        real_part = contract("nyzr,zw->nryw", real_y, z_cos) - contract(
            "nyzr,zw->nryw", imag_y, z_sin
        )
        fields = real_part * inverse_norm
        partial_value = jnp.sum(location_factor * fields, axis=0)
        if turn_index + 1 < WAVE_STEPS:
            summed = lax.psum(partial_value, "term")
            advanced = 2.0 * summed - previous
            advanced_brick = to_brick(advanced)
            dose_sum = advanced_brick * advanced_brick
            previous = current
            current = advanced
        else:
            shared = lax.psum_scatter(partial_value, "term", scatter_dimension=1, tiled=True)
            final_brick = 2.0 * shared - to_brick(previous)
            dose_sum = dose_sum + final_brick * final_brick
    absorb = jnp.where(
        medium_kinds == 0,
        organ_properties[0, 0],
        jnp.where(medium_kinds == 1, organ_properties[1, 0], organ_properties[2, 0]),
    )
    perfuse = jnp.where(
        medium_kinds == 0,
        organ_properties[0, 1],
        jnp.where(medium_kinds == 1, organ_properties[1, 1], organ_properties[2, 1]),
    )
    source = absorb * dose_sum
    present_thermal = thermal_increase
    for turn_index in range(HEAT_STEPS):
        padded = padded_2(present_thermal, (("term", 1), ("pencil", 0)), 1)
        center, near_sum = stencil_sum(padded)
        present_thermal = heat_update(center, near_sum, perfuse, source)
    return (final_brick, present_thermal)


def solution(mesh):
    return jax.shard_map(
        on_device,
        mesh=mesh,
        in_specs=(
            P("pencil", None, None),
            P("pencil", None, None),
            P("term", "pencil", None, None),
            P("term", None, "pencil", None),
            P("pencil", "term", None),
            P(),
            P("pencil", "term", None),
        ),
        out_specs=(P("pencil", "term", None), P("pencil", "term", None)),
        check_vma=False,
    )
```

profile of v0, /device:TPU:11, one launch (start us, length us, event | category | flops | bytes accessed | tf_op | source)
XLA Modules:
  0.0 1815.2 jit_solution(8365943608618644426)
XLA Ops:
  50.3 9.8 reshape.35
  60.1 52.7 %all_to_all.66 = f32[8,1,131072]{2,1,0:T(1,128)} all-to-all(f32[8,1,131072]{2,1,0:T(1,128)} %reshape.35), channel_id=1, replica_groups=mesh['term'=4,'pencil'=8] {'pencil'}, dimensions={0} | all-to-all | bytes 8388608 | tf_op jit(solution)/shard_map/all_to_all | solution.py:118
  113.4 13.7 reduce
  164.9 10.0 fusion.97
  174.8 10.6 convolution_add_fusion.3
  209.0 23.7 %fusion.95 = f32[4096,512]{1,0:T(8,128)} fusion(f32[4096,512]{1,0:T(8,128)S(1)} %bitcast.202), kind=kOutput, calls=%fused_computation.134 | convolution fusion | flops 12888571904 | bytes 16777216 | tf_op jit(solution)/shard_map/dot_general | solution.py:29
  232.7 23.4 %fusion.93 = f32[4096,512]{1,0:T(8,128)} fusion(f32[4096,512]{1,0:T(8,128)S(1)} %bitcast.206), kind=kOutput, calls=%fused_computation.133 | convolution fusion | flops 12888571904 | bytes 16777216 | tf_op jit(solution)/shard_map/dot_general | solution.py:29
  256.0 23.6 %convolution_subtract_fusion.1 = f32[4096,512]{1,0:T(8,128)} fusion(f32[4096,512]{1,0:T(8,128)S(1)} %bitcast.213, f32[4096,512]{1,0:T(8,128)S(1)} %bitcast.207), kind=kOutput, calls=%fused_computation.37 | convolution fusion | flops 12890669056 | bytes 25165824 | tf_op jit(solution)/shard_map/dot_general | solution.py:29
  279.6 16.2 copy.124
  295.9 27.1 %convolution_add_fusion.1 = f32[4096,512]{1,0:T(8,128)} fusion(f32[4096,512]{1,0:T(8,128)} %fusion.93, f32[4096,512]{1,0:T(8,128)} %bitcast.203), kind=kOutput, calls=%fused_computation.36 | convolution fusion | flops 12890669056 | bytes 25165824 | tf_op jit(solution)/shard_map/dot_general | solution.py:29
  323.0 16.4 copy.125
  339.4 23.3 %fusion.325 = f32[512,4,2,16,64]{4,3,2,1,0:T(8,128)} fusion(f32[4,1,16,64,512]{3,2,1,0,4:T(8,128)} %copy.125, f32[4,1,16,64,512]{3,2,1,0,4:T(8,128)} %copy.124), kind=kLoop, calls=%fused_computation.343 | loop fusion | flops 4194304 | bytes 33554432
  362.7 25.5 %reshape.37 = f32[8,1,524288]{2,1,0:T(1,128)} reshape(f32[512,4,2,16,64]{4,3,2,1,0:T(8,128)} %fusion.325) | data formatting | bytes 33554432
  388.3 191.4 %all_to_all.67 = f32[8,1,524288]{2,1,0:T(1,128)} all-to-all(f32[8,1,524288]{2,1,0:T(1,128)} %reshape.37), channel_id=1, replica_groups=mesh['term'=4,'pencil'=8] {'pencil'}, dimensions={0} | all-to-all | bytes 33554432 | tf_op jit(solution)/shard_map/all_to_all | solution.py:122
  579.6 50.3 %reduce.1 = f32[8,524288]{1,0:T(8,128)} reduce(f32[8,1,524288]{2,1,0:T(1,128)} %all_to_all.67, f32[]{:T(128)} %broadcast.200), dimensions={1}, to_apply=%all_to_all.51.reduce_sub_computation | reduce | bytes 33554436 | tf_op jit(solution)/shard_map/all_to_all | solution.py:122
  629.9 30.2 %reshape.38 = f32[512,4,2,16,64]{4,3,2,1,0:T(8,128)} reshape(f32[8,524288]{1,0:T(8,128)} %reduce.1) | data formatting | bytes 33554432
  660.1 31.9 %copy.171 = f32[4,2,16,8,64,64]{4,3,2,5,0,1:T(8,128)} copy(f32[4,2,16,8,64,64]{4,2,1,0,5,3:T(8,128)} %bitcast.210) | data formatting | bytes 33554432 | tf_op jit(solution)/shard_map/all_to_all | solution.py:122
  692.1 27.6 %reshape.33 = f32[4,2,16,512,64]{3,2,4,0,1:T(8,128)} reshape(f32[4,2,16,8,64,64]{4,3,2,5,0,1:T(8,128)} %copy.171) | data formatting | bytes 33554432 | tf_op jit(solution)/shard_map/all_to_all | solution.py:122
  719.7 12.1 fusion.11
  740.4 12.3 subtract_bitcast_fusion.1
  752.7 10.3 add_bitcast_fusion.1
  763.0 29.5 %fusion.6 = f32[512,4,16,64]{0,3,2,1:T(8,128)} fusion(f32[4,16,512,64]{2,1,3,0:T(8,128)} %add_bitcast_fusion.1), kind=kOutput, calls=%fused_computation.15 | convolution fusion | flops 12888571904 | bytes 16777216 | tf_op jit(solution)/shard_map/nyzr,zw->nryw/dot_general | solution.py:33
  792.6 35.6 %fusion.1 = f32[64,16,512]{2,0,1:T(8,128)} fusion(f32[512,4,16,64]{0,3,2,1:T(8,128)} %fusion.6, f32[4,64,16,512]{3,2,1,0:T(8,128)} %param.9, f32[4,16,512,64]{2,1,3,0:T(8,128)S(1)} %copy-done.4), kind=kOutput, calls=%fused_computation.9 | convolution fusion | flops 12896436224 | bytes 27262976 | tf_op jit(solution)/shard_map/nyzr,zw->nryw/dot_general | solution.py:33
  828.2 85.1 %all-reduce.4.cloned.1.call-done = f32[64,16,512]{2,0,1:T(8,128)} async-done(((f32[64,16,512]{2,0,1:T(8,128)}), f32[64,16,512]{2,0,1:T(8,128)}) %all-reduce.4.cloned.1.call-update) | async-done | bytes 2097168 | tf_op jit(solution)/shard_map/psum | solution.py:137
  956.5 9.8 reshape.39
  966.4 52.9 %all_to_all.68 = f32[8,1,131072]{2,1,0:T(1,128)} all-to-all(f32[8,1,131072]{2,1,0:T(1,128)} %reshape.39), channel_id=1, replica_groups=mesh['term'=4,'pencil'=8] {'pencil'}, dimensions={0} | all-to-all | bytes 8388608 | tf_op jit(solution)/shard_map/all_to_all | solution.py:118
  1019.3 13.7 reduce.2
  1071.1 10.0 fusion.86
  1081.0 10.6 convolution_add_fusion.2
  1115.1 23.5 %fusion.84 = f32[4096,512]{1,0:T(8,128)} fusion(f32[4096,512]{1,0:T(8,128)S(1)} %bitcast.204), kind=kOutput, calls=%fused_computation.129 | convolution fusion | flops 12888571904 | bytes 16777216 | tf_op jit(solution)/shard_map/dot_general | solution.py:29
  1138.6 23.6 %fusion.90 = f32[4096,512]{1,0:T(8,128)} fusion(f32[4096,512]{1,0:T(8,128)S(1)} %bitcast.208), kind=kOutput, calls=%fused_computation.132 | convolution fusion | flops 12888571904 | bytes 16777216 | tf_op jit(solution)/shard_map/dot_general | solution.py:29
  1162.2 23.6 %convolution_subtract_fusion = f32[4096,512]{1,0:T(8,128)} fusion(f32[4096,512]{1,0:T(8,128)S(1)} %bitcast.215, f32[4096,512]{1,0:T(8,128)S(1)} %bitcast.209), kind=kOutput, calls=%fused_computation.35 | convolution fusion | flops 12890669056 | bytes 25165824 | tf_op jit(solution)/shard_map/dot_general | solution.py:29
  1185.8 16.2 copy.140
  1202.0 26.9 %convolution_add_fusion = f32[4096,512]{1,0:T(8,128)} fusion(f32[4096,512]{1,0:T(8,128)} %fusion.90, f32[4096,512]{1,0:T(8,128)} %bitcast.205), kind=kOutput, calls=%fused_computation.34 | convolution fusion | flops 12890669056 | bytes 25165824 | tf_op jit(solution)/shard_map/dot_general | solution.py:29
  1228.9 16.6 copy.141
  1245.6 23.3 %fusion.324 = f32[512,4,2,16,64]{4,3,2,1,0:T(8,128)} fusion(f32[4,1,16,64,512]{3,2,1,0,4:T(8,128)} %copy.141, f32[4,1,16,64,512]{3,2,1,0,4:T(8,128)} %copy.140), kind=kLoop, calls=%fused_computation.342 | loop fusion | flops 4194304 | bytes 33554432
  1268.9 25.5 %reshape.41 = f32[8,1,524288]{2,1,0:T(1,128)} reshape(f32[512,4,2,16,64]{4,3,2,1,0:T(8,128)} %fusion.324) | data formatting | bytes 33554432
  1294.5 191.4 %all_to_all.69 = f32[8,1,524288]{2,1,0:T(1,128)} all-to-all(f32[8,1,524288]{2,1,0:T(1,128)} %reshape.41), channel_id=1, replica_groups=mesh['term'=4,'pencil'=8] {'pencil'}, dimensions={0} | all-to-all | bytes 33554432 | tf_op jit(solution)/shard_map/all_to_all | solution.py:122
  1485.8 50.2 %reduce.3 = f32[8,524288]{1,0:T(8,128)} reduce(f32[8,1,524288]{2,1,0:T(1,128)} %all_to_all.69, f32[]{:T(128)} %broadcast.200), dimensions={1}, to_apply=%all_to_all.58.reduce_sub_computation | reduce | bytes 33554436 | tf_op jit(solution)/shard_map/all_to_all | solution.py:122
  1536.1 30.0 %reshape.42 = f32[512,4,2,16,64]{4,3,2,1,0:T(8,128)} reshape(f32[8,524288]{1,0:T(8,128)} %reduce.3) | data formatting | bytes 33554432
  1566.1 31.9 %copy.173 = f32[4,2,16,8,64,64]{4,3,2,5,0,1:T(8,128)} copy(f32[4,2,16,8,64,64]{4,2,1,0,5,3:T(8,128)} %bitcast.211) | data formatting | bytes 33554432 | tf_op jit(solution)/shard_map/all_to_all | solution.py:122
  1598.0 27.6 %reshape.34 = f32[4,2,16,512,64]{3,2,4,0,1:T(8,128)} reshape(f32[4,2,16,8,64,64]{4,3,2,5,0,1:T(8,128)} %copy.173) | data formatting | bytes 33554432 | tf_op jit(solution)/shard_map/all_to_all | solution.py:122
  1625.7 12.3 fusion.15
  1646.6 12.2 subtract_bitcast_fusion
  1658.9 10.3 add_bitcast_fusion
  1669.2 29.5 %fusion.2 = f32[512,4,16,64]{0,3,2,1:T(8,128)} fusion(f32[4,16,512,64]{2,1,3,0:T(8,128)} %add_bitcast_fusion), kind=kOutput, calls=%fused_computation.10 | convolution fusion | flops 12888571904 | bytes 16777216 | tf_op jit(solution)/shard_map/nyzr,zw->nryw/dot_general | solution.py:33
  1698.6 35.2 %fusion = f32[64,16,512]{2,0,1:T(8,128)} fusion(f32[512,4,16,64]{0,3,2,1:T(8,128)} %fusion.2, f32[4,64,16,512]{3,2,1,0:T(8,128)} %param.9, f32[4,16,512,64]{2,1,3,0:T(8,128)S(1)} %copy-done.5), kind=kOutput, calls=%fused_computation.7 | convolution fusion | flops 12896436224 | bytes 27262976 | tf_op jit(solution)/shard_map/nyzr,zw->nryw/dot_general | solution.py:33
  1763.1 15.9 reduce-scatter.2.cloned.1.call-done
  (118 shorter events, 284.9 us)
Async XLA Ops:
  7.2 906.1 %all-reduce.4.cloned.1.call-start = ((), (), s32[]{:S(2)}) async-start(), calls=%async_computation.5 | async-start | bytes 4194304 | tf_op jit(solution)/shard_map/psum | solution.py:137
  174.8 19.8 %slice-start.4 = ((s8[8388608]{0:T(1024)(128)(4,1)}), s8[4194304]{0:T(1024)(128)(4,1)S(1)}, s32[]{:S(2)}) async-start(s8[8388608]{0:T(1024)(128)(4,1)} %bitcast.220), calls=%async_computation.11 | async-start | bytes 8388608
  185.5 9.2 slice-start.5
  208.9 23.7 %copy-start.2 = (f32[4,1,16,64,512]{4,3,2,1,0:T(8,128)}, f32[4,1,16,64,512]{4,3,2,1,0:T(8,128)S(1)}, u32[]{:S(2)}) copy-start(f32[4,1,16,64,512]{4,3,2,1,0:T(8,128)S(1)} %get-tuple-element.12) | copy-start | bytes 25165828
  232.7 23.4 %slice-start = ((s8[8388608]{0:T(1024)(128)(4,1)}), s8[4194304]{0:T(1024)(128)(4,1)S(1)}, s32[]{:S(2)}) async-start(s8[8388608]{0:T(1024)(128)(4,1)} %bitcast.212), calls=%async_computation.7 | async-start | bytes 8388608
  232.7 23.4 %slice-start.1 = ((s8[8388608]{0:T(1024)(128)(4,1)}), s8[4194304]{0:T(1024)(128)(4,1)S(1)}, s32[]{:S(2)}) async-start(s8[8388608]{0:T(1024)(128)(4,1)} %bitcast.212), calls=%async_computation.8 | async-start | bytes 8388608
  719.7 12.1 copy-start
  763.0 29.5 %copy-start.4 = (f32[4,16,512,64]{2,1,3,0:T(8,128)S(1)}, f32[4,16,512,64]{2,1,3,0:T(8,128)}, u32[]{:S(2)}) copy-start(f32[4,16,512,64]{2,1,3,0:T(8,128)} %subtract_bitcast_fusion.1) | copy-start | bytes 25165828
  792.5 120.8 %copy-start.8 = (f32[64,16,512]{2,1,0:T(8,128)S(1)}, f32[64,16,512]{2,1,0:T(8,128)}, u32[]{:S(2)}) copy-start(f32[64,16,512]{2,1,0:T(8,128)} %param.8) | copy-start | bytes 6291460
  828.2 950.9 %reduce-scatter.2.cloned.1.call-start = ((), (), s32[]{:S(2)}) async-start(), calls=%async_computation.6 | async-start | bytes 2621440 | tf_op jit(solution)/shard_map/reduce_scatter | solution.py:144
  916.3 8.3 copy-start.6
  1081.0 19.8 %slice-start.6 = ((s8[8388608]{0:T(1024)(128)(4,1)}), s8[4194304]{0:T(1024)(128)(4,1)S(1)}, s32[]{:S(2)}) async-start(s8[8388608]{0:T(1024)(128)(4,1)} %bitcast.222), calls=%async_computation.13 | async-start | bytes 8388608
  1091.6 9.2 slice-start.7
  1115.1 23.5 %copy-start.3 = (f32[4,1,16,64,512]{4,3,2,1,0:T(8,128)}, f32[4,1,16,64,512]{4,3,2,1,0:T(8,128)S(1)}, u32[]{:S(2)}) copy-start(f32[4,1,16,64,512]{4,3,2,1,0:T(8,128)S(1)} %get-tuple-element.10) | copy-start | bytes 25165828
  1138.6 23.6 %slice-start.2 = ((s8[8388608]{0:T(1024)(128)(4,1)}), s8[4194304]{0:T(1024)(128)(4,1)S(1)}, s32[]{:S(2)}) async-start(s8[8388608]{0:T(1024)(128)(4,1)} %bitcast.214), calls=%async_computation.9 | async-start | bytes 8388608
  1138.6 23.6 %slice-start.3 = ((s8[8388608]{0:T(1024)(128)(4,1)}), s8[4194304]{0:T(1024)(128)(4,1)S(1)}, s32[]{:S(2)}) async-start(s8[8388608]{0:T(1024)(128)(4,1)} %bitcast.214), calls=%async_computation.10 | async-start | bytes 8388608
  1625.7 12.3 copy-start.1
  1669.2 29.5 %copy-start.5 = (f32[4,16,512,64]{2,1,3,0:T(8,128)S(1)}, f32[4,16,512,64]{2,1,3,0:T(8,128)}, u32[]{:S(2)}) copy-start(f32[4,16,512,64]{2,1,3,0:T(8,128)} %subtract_bitcast_fusion) | copy-start | bytes 25165828
  1698.6 35.3 %copy-start.9 = (f32[64,4,512]{2,1,0:T(4,128)S(1)}, f32[64,4,512]{2,1,0:T(4,128)}, u32[]{:S(2)}) copy-start(f32[64,4,512]{2,1,0:T(4,128)} %param.13) | copy-start | bytes 1572868
  1698.6 59.7 %copy-start.11 = (f32[3,2]{0,1:T(2,128)S(1)}, f32[3,2]{0,1:T(2,128)}, u32[]{:S(2)}) copy-start(f32[3,2]{0,1:T(2,128)} %param.12) | copy-start | bytes 76
  1733.9 45.2 %copy-start.7 = (f32[64,16,512]{2,0,1:T(8,128)S(1)}, f32[64,16,512]{2,0,1:T(8,128)}, u32[]{:S(2)}) copy-start(f32[64,16,512]{2,0,1:T(8,128)} %copy-done.6) | copy-start | bytes 6291460
  1734.1 6.5 collective-permute-start
  1737.6 12.5 collective-permute-start.1
  1750.1 0.9 copy-start.10
  1751.1 12.1 collective-permute-start.2
  1755.6 7.5 collective-permute-start.3
  1785.3 6.3 collective-permute-start.4
  1788.8 6.2 collective-permute-start.5
  1795.0 7.6 collective-permute-start.6
  1798.5 4.1 collective-permute-start.7
Sparse Core Ops, SparseCore 0:
  828.3 84.9 all-reduce.3
  1734.0 45.0 reduce-scatter.1
where the time goes:
time: 1830 us; the launch traced here: 1820 us
  matrix products  547 us (30%)
  blocking collectives  488 us (27%)
  local copies, waits for them, and re-layouts  415 us (23%)
  other arithmetic  209 us (11%)
  waiting for transfers between devices  116 us (6%)
  starting transfers between devices  24.6 us (1%)
    all_to_all x2, blocking collectives, on_device(): lax.all_to_all(term_restored, 'pencil', split_axis=4, concat_axis=3, tile...  383 us
    dot_general x24, matrix products, contract(): jnp.einsum(form, left, right, precision=lax.Precision.HIGHEST, preferred_...  276 us
    dot_general x16, matrix products, matmul(): jnp.dot(left, right, precision=lax.Precision.HIGHEST, preferred_element_t...  271 us
    unnamed x54, local copies, waits for them, and re-layouts  156 us
    all_to_all x4, local copies, waits for them, and re-layouts, on_device(): lax.all_to_all(term_restored, 'pencil', split_axis=4, concat_axis=3, tile...  119 us
    all_to_all x2, blocking collectives, on_device(): lax.all_to_all(rows_spec, 'pencil', split_axis=2, concat_axis=3, tiled=True)  106 us
    all_to_all x2, other arithmetic, on_device(): lax.all_to_all(term_restored, 'pencil', split_axis=4, concat_axis=3, tile...  101 us
    psum x1, waiting for transfers between devices, on_device(): summed = lax.psum(partial_value, 'term')  85.1 us
  transfers between devices with their start and end apart: 10, of which 6 were waited for; matrix products, arithmetic and copies ran while one was open for 0% of the time, Pallas kernels for 0%

commit v1 on v0

v1 whole, which is shorter than its diff:
```python
import functools
import math

import jax
import jax.numpy as jnp
import ml_dtypes
import numpy as np
from jax import lax
from jax.experimental import pallas as pl
from jax.experimental.pallas import tpu as pltpu
from jax.sharding import PartitionSpec as P

WAVE_STEPS = 2
HEAT_STEPS = 2
DIFFUSION = 0.125
VMEM_BYTES = 56 * 1024 * 1024
F32 = jnp.float32
BF16 = jnp.bfloat16


def halves(table):
    high = table.astype(ml_dtypes.bfloat16)
    low = (table - high.astype(np.float64)).astype(ml_dtypes.bfloat16)
    return high, low


def angles(left, right, length):
    return (np.outer(left, right) % length) * (2.0 * math.pi / length)


def slot_wavenumbers(blocks, length_z):
    width = length_z // blocks
    half = width // 2
    slots = np.concatenate([[half], np.arange(1, half)])
    starts = np.arange(blocks) * width
    return starts[:, None] + slots[None, :], starts


def forward_z_table(blocks, length_z):
    main, first = slot_wavenumbers(blocks, length_z)
    z = np.arange(length_z)
    theta = angles(z, main.reshape(-1), length_z).reshape(length_z, blocks, -1)
    real, imag = np.cos(theta), -np.sin(theta)
    for q in range(blocks // 2):
        real[:, q, 0], imag[:, q, 0] = -imag[:, q, 0].copy(), real[:, q, 0].copy()
    theta = angles(z, first, length_z)
    real0, imag0 = np.cos(theta), -np.sin(theta)
    for q in range(blocks // 2 + 1, blocks):
        real0[:, q], imag0[:, q] = imag0[:, q].copy(), -real0[:, q].copy()
    table = np.concatenate(
        [np.stack([real, imag], 2).reshape(length_z, -1), np.stack([real0, imag0], 2).reshape(length_z, -1)], axis=1
    )
    spare = -table.shape[1] % 128
    return np.pad(table, ((0, 0), (0, spare)))


def inverse_z_table(blocks, length_z, scale):
    main, first = slot_wavenumbers(blocks, length_z)
    z = np.arange(length_z)
    theta = angles(main.reshape(-1), z, length_z).reshape(blocks, -1, length_z)
    real, imag = np.cos(theta), -np.sin(theta)
    for p in range(blocks):
        middle = theta[p, 0]
        imag[p, 0] = np.cos(middle) if p < blocks // 2 else -np.sin(middle)
        lowest = angles(first[p : p + 1], z, length_z)[0]
        real[p, 0] = np.cos(lowest) if p <= blocks // 2 else -np.sin(lowest)
    return scale * np.concatenate([real.reshape(-1, length_z), imag.reshape(-1, length_z)], axis=0)


def forward_x_table(length_x):
    x = np.arange(length_x)
    theta = angles(x, x, length_x)
    return np.concatenate([np.cos(theta), np.sin(theta)], axis=1)


def inverse_x_table(blocks, length_x):
    x = np.arange(length_x)
    theta = angles(x, x, length_x).reshape(length_x, blocks, -1)
    cosine, sine = np.cos(theta), np.sin(theta)
    real_rows = np.stack([cosine, sine], axis=2).reshape(length_x, -1)
    imag_rows = np.stack([-sine, cosine], axis=2).reshape(length_x, -1)
    return np.concatenate([real_rows, imag_rows], axis=0)


def mirror_table(length):
    x = np.arange(length)
    table = np.zeros((length, length), ml_dtypes.bfloat16)
    table[x, (-x) % length] = 1
    return table


def fourier(real, imag, sign):
    count = len(real)
    if count == 1:
        return real, imag
    if count % 2:
        out_real, out_imag = [], []
        for k in range(count):
            total_real, total_imag = real[0], imag[0]
            for n in range(1, count):
                angle = 2.0 * math.pi * (k * n % count) / count
                c, s = math.cos(angle), sign * math.sin(angle)
                total_real = total_real + (c * real[n] - s * imag[n])
                total_imag = total_imag + (c * imag[n] + s * real[n])
            out_real.append(total_real)
            out_imag.append(total_imag)
        return out_real, out_imag
    even_real, even_imag = fourier(real[::2], imag[::2], sign)
    odd_real, odd_imag = fourier(real[1::2], imag[1::2], sign)
    half = count // 2
    out_real, out_imag = [None] * count, [None] * count
    for k in range(half):
        a, b = odd_real[k], odd_imag[k]
        if k == 0:
            turned = (a, b)
        elif 4 * k == count:
            turned = (-b, a) if sign > 0 else (b, -a)
        else:
            angle = 2.0 * math.pi * k / count
            c, s = math.cos(angle), sign * math.sin(angle)
            if 8 * k == count or 8 * k == 3 * count:
                root = math.sqrt(0.5)
                sum_ab, less_ab = root * (a + b), root * (a - b)
                if c > 0:
                    turned = (less_ab, sum_ab) if s > 0 else (sum_ab, -less_ab)
                else:
                    turned = (-sum_ab, less_ab) if s > 0 else (-less_ab, -sum_ab)
            else:
                turned = (c * a - s * b, c * b + s * a)
        out_real[k] = even_real[k] + turned[0]
        out_imag[k] = even_imag[k] + turned[1]
        out_real[k + half] = even_real[k] - turned[0]
        out_imag[k + half] = even_imag[k] - turned[1]
    return out_real, out_imag


def split(values):
    high = values.astype(BF16)
    return high, (values - high.astype(F32)).astype(BF16)


def dot(left, right):
    return jnp.dot(left, right, preferred_element_type=F32)


def dot_three(high, low, table_high, table_low):
    return dot(high, table_high) + (dot(low, table_high) + dot(high, table_low))


def params(count=0):
    return pltpu.CompilerParams(vmem_limit_bytes=VMEM_BYTES, dimension_semantics=("arbitrary",) * count)


def cost(flops, moved):
    return pl.CostEstimate(flops=int(flops), bytes_accessed=int(moved), transcendentals=0)


def whole(shape, grid_rank):
    return pl.BlockSpec(shape, lambda *_: (0,) * len(shape), pipeline_mode=pl.Buffered(1)) if grid_rank else pl.BlockSpec(
        memory_space=pltpu.VMEM
    )


def forward_z_kernel(brick_ref, high_ref, low_ref, out_ref):
    width, rows, length_z = brick_ref.shape
    blocks = out_ref.shape[0]
    half = length_z // blocks // 2
    high, low = split(brick_ref[...].reshape(width * rows, length_z))
    result = dot_three(high, low, high_ref[...], low_ref[...])
    main = 2 * half
    out_ref[...] = jnp.zeros_like(out_ref)
    for q in range(blocks):
        for w in range(width):
            part = result[w * rows : (w + 1) * rows]
            out_ref[q, :, w * main : (w + 1) * main] = part[:, q * main : (q + 1) * main]
            at = blocks * main + 2 * q
            lane = width * main + w
            out_ref[q, :, lane : lane + 1] = part[:, at : at + 1]
            out_ref[q, :, lane + width : lane + width + 1] = part[:, at + 1 : at + 2]


def forward_z(brick, blocks):
    width, rows, length_z = brick.shape
    half = length_z // blocks // 2
    lanes = width * 2 * half + 2 * width
    lanes += -lanes % 128
    high, low = halves(forward_z_table(blocks, length_z))
    return pl.pallas_call(
        forward_z_kernel,
        out_shape=jax.ShapeDtypeStruct((blocks, rows, lanes), F32),
        compiler_params=params(),
        name="forward_z",
    )(brick, jnp.asarray(high), jnp.asarray(low))


def forward_x_kernel(data_ref, high_ref, low_ref, out_ref, *, width, half):
    length_x = data_ref.shape[0]
    main = width * 2 * half
    turned = data_ref[...].T
    high, low = split(turned[: out_ref.shape[0]])
    both = dot_three(high, low, high_ref[...], low_ref[...])
    by_cos, by_sin = both[:, :length_x], both[:, length_x:]
    for w in range(width):
        re, im = w * 2 * half, w * 2 * half + half
        out_ref[re : re + half] = by_cos[re : re + half] + by_sin[im : im + half]
        out_ref[im : im + half] = by_cos[im : im + half] - by_sin[re : re + half]
    re, im, end = main, main + width, main + 2 * width
    out_ref[re:im] = by_cos[re:im] + by_sin[im:end]
    out_ref[im:end] = by_cos[im:end] - by_sin[re:im]


def forward_x(data, width, half):
    length_x = data.shape[0]
    rows = width * 2 * half + 2 * width
    rows += -rows % 8
    high, low = halves(forward_x_table(length_x))
    return pl.pallas_call(
        functools.partial(forward_x_kernel, width=width, half=half),
        out_shape=jax.ShapeDtypeStruct((rows, length_x), F32),
        compiler_params=params(),
        name="forward_x",
    )(data, jnp.asarray(high), jnp.asarray(low))


def spread_kernel(
    f_ref, first_ref, own_ref, other_ref, high_ref, low_ref, out_ref,
    fk_ref, edge_ref, edge_out_ref, u_ref, u_high_ref, u_low_ref, *, width, first_term,
):
    length_y, _, half, length_x = fk_ref.shape
    lanes_out = out_ref.shape[-1]
    rows_x = lanes_out // 2
    main = width * 2 * half
    step = pl.program_id(0)
    tiles = [slice(at, at + 128) for at in range(0, length_x, 128)]

    @pl.when(step == 0)
    def _():
        @pl.loop(0, half // 8)
        def _(tile):
            for lanes in tiles:
                real, imag = [], []
                for y in range(length_y):
                    row = (y % width) * 2 * half + tile * 8
                    real.append(f_ref[y // width, pl.ds(pl.multiple_of(row, 8), 8), lanes])
                    imag.append(f_ref[y // width, pl.ds(pl.multiple_of(row + half, 8), 8), lanes])
                real, imag = fourier(real, imag, -1)
                at = pl.ds(pl.multiple_of(tile * 8, 8), 8)
                for y in range(length_y):
                    fk_ref[y, 0, at, lanes] = real[y]
                    fk_ref[y, 1, at, lanes] = imag[y]

        for index, lanes in enumerate(tiles):
            real = [f_ref[y // width, main + y % width : main + y % width + 1, lanes] for y in range(length_y)]
            imag = [
                f_ref[y // width, main + width + y % width : main + width + y % width + 1, lanes]
                for y in range(length_y)
            ]
            real, imag = fourier(real, imag, -1)
            factors = [first_ref[y, :, lanes] for y in range(length_y)]
            real = [factors[y] * real[y] for y in range(length_y)]
            imag = [factors[y] * imag[y] for y in range(length_y)]
            real, imag = fourier(real, imag, 1)
            for y in range(length_y):
                edge_ref[y, :, index * 128 : index * 128 + 128] = real[y]
                edge_ref[y, :, length_x + index * 128 : length_x + index * 128 + 128] = imag[y]
        high, low = split(edge_ref[...].reshape(-1, 2 * length_x))
        edge_out_ref[...] = dot_three(high, low, high_ref[...], low_ref[...])

    row_index = lax.broadcasted_iota(jnp.int32, (8, 128), 0)

    @pl.loop(0, half // 8)
    def _(tile):
        at = pl.ds(pl.multiple_of(tile * 8, 8), 8)
        swapped = jnp.logical_and(row_index == 0, tile == 0)
        for index, lanes in enumerate(tiles):
            real, imag = [], []
            for y in range(length_y):
                own = jnp.where(swapped, own_ref[0, y, half : half + 1, lanes], own_ref[0, y, at, lanes])
                factor = own + other_ref[0, y, at, lanes]
                real.append(factor * fk_ref[y, 0, at, lanes])
                imag.append(factor * fk_ref[y, 1, at, lanes])
            real, imag = fourier(real, imag, 1)
            for y in range(length_y):
                rows = pl.ds(pl.multiple_of(y * half + tile * 8, 8), 8)
                u_ref[rows, index * 128 : index * 128 + 128] = real[y]
                u_ref[rows, length_x + index * 128 : length_x + index * 128 + 128] = imag[y]

    @pl.loop(0, length_y * half // 64)
    def _(part):
        rows = pl.ds(pl.multiple_of(part * 64, 64), 64)
        high, low = split(u_ref[rows, :])
        u_high_ref[rows, :] = high
        u_low_ref[rows, :] = low

    term = first_term + step
    lane_index = lax.broadcasted_iota(jnp.int32, (8, lanes_out), 1)
    row_index = lax.broadcasted_iota(jnp.int32, (8, lanes_out), 0)
    swapped = jnp.logical_and(row_index == 0, lane_index < rows_x)
    count = 256 // lanes_out
    for part in range(2 * length_x // 256):
        cols = slice(part * 256, part * 256 + 256)
        result = dot_three(u_high_ref[...], u_low_ref[...], high_ref[:, cols], low_ref[:, cols])
        edges = [edge_out_ref[pl.ds(y * first_ref.shape[1] + term, 1), cols] for y in range(length_y)]
        for k in range(count):
            q = part * count + k
            inside = slice(k * lanes_out, (k + 1) * lanes_out)
            piece = result[:, inside]
            for y in range(length_y):
                top = piece[y * half : y * half + 8]
                out_ref[q, 0, y, :8, :] = jnp.where(swapped, edges[y][:, inside], top)
                out_ref[q, 0, y, 8:, :] = piece[y * half + 8 : (y + 1) * half]


def spread(f, first, own, other, blocks, width, first_term, terms):
    length_y, length_x = own.shape[1], own.shape[3]
    half = other.shape[2]
    rows_x = length_x // blocks
    high, low = halves(inverse_x_table(blocks, length_x))
    high, low = jnp.asarray(high), jnp.asarray(low)
    rows = length_y * half
    return pl.pallas_call(
        functools.partial(spread_kernel, width=width, first_term=first_term),
        grid=(terms,),
        in_specs=[
            whole(f.shape, 1),
            whole(first.shape, 1),
            pl.BlockSpec((1, length_y, half + 8, length_x), lambda t: (t + first_term, 0, 0, 0)),
            pl.BlockSpec((1, length_y, half, length_x), lambda t: (t + first_term, 0, 0, 0)),
            whole(high.shape, 1),
            whole(low.shape, 1),
        ],
        out_specs=pl.BlockSpec((blocks, 1, length_y, half, 2 * rows_x), lambda t: (0, t, 0, 0, 0)),
        out_shape=jax.ShapeDtypeStruct((blocks, terms, length_y, half, 2 * rows_x), F32),
        scratch_shapes=[
            pltpu.VMEM((length_y, 2, half, length_x), F32),
            pltpu.VMEM((length_y, first.shape[1], 2 * length_x), F32),
            pltpu.VMEM((length_y * first.shape[1], 2 * length_x), F32),
            pltpu.VMEM((rows, 2 * length_x), F32),
            pltpu.VMEM((rows, 2 * length_x), BF16),
            pltpu.VMEM((rows, 2 * length_x), BF16),
        ],
        compiler_params=params(1),
        cost_estimate=cost(terms * 6 * rows * 4 * length_x * length_x, terms * 16 * rows * length_x),
        name="spread",
    )(f, first, own, other, high, low)


def gather_kernel(data_ref, factor_ref, high_ref, low_ref, out_ref):
    blocks, terms, _, half, lanes = data_ref.shape
    rows = lanes // 2
    parts = []
    for t in range(terms):
        turned = data_ref[:, t, 0].reshape(blocks * half, lanes).T
        parts.append(jnp.concatenate([turned[:rows], turned[rows:]], axis=1))
    high, low = split(jnp.concatenate(parts, axis=0))
    fields = dot_three(high, low, high_ref[...], low_ref[...])
    total = factor_ref[0, 0] * fields[:rows]
    for t in range(1, terms):
        total = total + factor_ref[t, 0] * fields[t * rows : (t + 1) * rows]
    out_ref[0] = total


def gather(data, factor, scale):
    blocks, terms, length_y, half, lanes = data.shape
    rows, length_z = factor.shape[2], factor.shape[3]
    high, low = halves(inverse_z_table(blocks, length_z, scale))
    return pl.pallas_call(
        gather_kernel,
        grid=(length_y,),
        in_specs=[
            pl.BlockSpec((blocks, terms, 1, half, lanes), lambda y: (0, 0, y, 0, 0)),
            pl.BlockSpec((terms, 1, rows, length_z), lambda y: (0, y, 0, 0)),
            whole(high.shape, 1),
            whole(low.shape, 1),
        ],
        out_specs=pl.BlockSpec((1, rows, length_z), lambda y: (y, 0, 0)),
        out_shape=jax.ShapeDtypeStruct((length_y, rows, length_z), F32),
        compiler_params=params(1),
        cost_estimate=cost(6 * terms * length_y * rows * length_z * length_z, 4 * (data.size + factor.size)),
        name="gather_z",
    )(data, factor, jnp.asarray(high), jnp.asarray(low))


def mirror_kernel(in_ref, table_ref, out_ref, turned_ref):
    _, length_y, half, length_x = in_ref.shape
    high, low = split(in_ref[0].reshape(length_y * half, length_x))
    rest = in_ref[0].reshape(length_y * half, length_x) - high.astype(F32) - low.astype(F32)
    table = table_ref[...]
    turned = (dot(high, table) + dot(low, table)) + dot(rest.astype(BF16), table)
    turned_ref[...] = turned.reshape(length_y, half, length_x)
    for y in range(length_y):
        source = -y % length_y
        for s in range(half):
            row = -s % half
            out_ref[0, y, s : s + 1, :] = turned_ref[source, row : row + 1, :]


def mirror(multiplier):
    terms, length_y, width, length_x = multiplier.shape
    half = width // 2
    table = mirror_table(length_x)
    return pl.pallas_call(
        mirror_kernel,
        grid=(terms,),
        in_specs=[
            pl.BlockSpec((1, length_y, half, length_x), lambda t: (t, 0, 1, 0)),
            whole(table.shape, 1),
        ],
        out_specs=pl.BlockSpec((1, length_y, half, length_x), lambda t: (t, 0, 0, 0)),
        out_shape=jax.ShapeDtypeStruct((terms, length_y, half, length_x), F32),
        scratch_shapes=[pltpu.VMEM((length_y, half, length_x), F32)],
        compiler_params=params(1),
        cost_estimate=cost(6 * terms * length_y * half * length_x * length_x, 4 * multiplier.size),
        name="mirror",
    )(multiplier, jnp.asarray(table))


def flip(values, axis):
    return jnp.roll(jnp.flip(values, axis), 1, axis)


def padded_by_one(block, sides):
    for axis, dim in sides:
        count = lax.axis_size(axis)
        forward = [(i, i + 1) for i in range(count - 1)]
        backward = [(target, source) for source, target in forward]
        size = block.shape[dim]
        low = lax.ppermute(lax.slice_in_dim(block, size - 1, size, axis=dim), axis, forward)
        high = lax.ppermute(lax.slice_in_dim(block, 0, 1, axis=dim), axis, backward)
        yield dim, low, high


def heat_step(heat, perfuse):
    near = jnp.zeros_like(heat)
    for dim, low, high in padded_by_one(heat, (("term", 0), ("pencil", 1))):
        size = heat.shape[dim]
        near = near + jnp.concatenate([low, lax.slice_in_dim(heat, 0, size - 1, axis=dim)], axis=dim)
        near = near + jnp.concatenate([lax.slice_in_dim(heat, 1, size, axis=dim), high], axis=dim)
    deep = jnp.pad(heat, ((0, 0), (0, 0), (1, 1)))
    near = near + deep[:, :, 2:] + deep[:, :, :-2]
    return heat + DIFFUSION * (near - 6.0 * heat) - perfuse * heat


def on_device(
    present_acoustic,
    prior_acoustic,
    location_factor,
    spectral_multiplier,
    medium_kinds,
    organ_properties,
    thermal_increase,
):
    term_count = lax.axis_size("term")
    blocks = lax.axis_size("pencil")
    rows, length_y, length_z = present_acoustic.shape
    length_x = rows * blocks
    width = length_y // term_count
    half = length_z // blocks // 2
    terms = location_factor.shape[0]
    brick_start = lax.axis_index("term") * width
    scale = 2.0 / (length_x * length_y * length_z)

    def to_brick(values):
        return jnp.transpose(lax.dynamic_slice_in_dim(values, brick_start, width, 1), (1, 0, 2))

    other = lax.ppermute(mirror(spectral_multiplier), "pencil", [(p, blocks - 1 - p) for p in range(blocks)])
    lowest = spectral_multiplier[:, :, 0, :]
    lowest = lowest + lax.ppermute(
        flip(flip(lowest, 1), 2), "pencil", [(p, blocks - p) for p in range(1, blocks) if 2 * p != blocks]
    )
    lowest = jnp.transpose(lowest, (1, 0, 2))
    lowest = jnp.pad(lowest, ((0, 0), (0, -terms % 8), (0, 0)))
    factor = jnp.transpose(location_factor, (0, 2, 1, 3))

    def doubled(brick):
        sent = forward_z(brick, blocks)
        rows_spec = lax.all_to_all(sent, "pencil", 0, 0, tiled=True)
        part = forward_x(rows_spec.reshape(length_x, -1), width, half)
        spectrum = lax.all_gather(part, "term", axis=0, tiled=False)
        restored = spread(spectrum, lowest, spectral_multiplier, other, blocks, width, 0, terms)
        restored = lax.all_to_all(restored, "pencil", 0, 0, tiled=True)
        partial = gather(restored, factor, scale)
        return lax.psum_scatter(partial, "term", scatter_dimension=0, tiled=True)

    kinds = jnp.transpose(medium_kinds, (1, 0, 2))
    absorb, perfuse = [
        jnp.where(
            kinds == 0,
            organ_properties[0, at],
            jnp.where(kinds == 1, organ_properties[1, at], organ_properties[2, at]),
        )
        for at in range(2)
    ]
    heat = heat_step(jnp.transpose(thermal_increase, (1, 0, 2)), perfuse)

    previous = to_brick(prior_acoustic)
    current = to_brick(present_acoustic)
    dose = jnp.zeros(current.shape, F32)
    for _ in range(WAVE_STEPS):
        advanced = doubled(current) - previous
        dose = dose + advanced * advanced
        previous = current
        current = advanced
    source = absorb * dose
    heat = heat + source
    for _ in range(HEAT_STEPS - 1):
        heat = heat_step(heat, perfuse) + source
    return jnp.transpose(current, (1, 0, 2)), jnp.transpose(heat, (1, 0, 2))


def solution(mesh):
    return jax.shard_map(
        on_device,
        mesh=mesh,
        in_specs=(
            P("pencil", None, None),
            P("pencil", None, None),
            P("term", "pencil", None, None),
            P("term", None, "pencil", None),
            P("pencil", "term", None),
            P(),
            P("pencil", "term", None),
        ),
        out_specs=(P("pencil", "term", None), P("pencil", "term", None)),
        check_vma=False,
    )
```

time: 1830 us -> 646 us (0.35)
  matrix products: 547 us -> 0 us
  local copies, waits for them, and re-layouts: 415 us -> 21.3 us
  blocking collectives: 488 us -> 211 us
  other arithmetic: 209 us -> 13.2 us
  waiting for transfers between devices: 116 us -> 240 us
  Pallas kernels: 0 us -> 110 us
    dot_general x40 -> x0, matrix products: 547 us -> none  [the longest x24 276 us: contract(): jnp.einsum(form, left, right, precision=lax.Precision.HIGHEST, preferred_...]
    all_to_all x4 -> x3, blocking collectives: 488 us -> 211 us  [the longest x2 112 us: doubled(): rows_spec = lax.all_to_all(sent, 'pencil', 0, 0, tiled=True)]
    unnamed x54 -> x20, local copies, waits for them, and re-layouts: 156 us -> 16.7 us
    all_to_all x7 -> x0, local copies, waits for them, and re-layouts: 136 us -> none  [the longest x4 119 us: on_device(): lax.all_to_all(term_restored, 'pencil', split_axis=4, concat_axis=3, tile...]
    all_to_all x4 -> x0, other arithmetic: 128 us -> none  [the longest x2 101 us: on_device(): lax.all_to_all(term_restored, 'pencil', split_axis=4, concat_axis=3, tile...]
    pallas_call x0 -> x9, Pallas kernels: none -> 110 us  [the longest x2 51.4 us: spread(): pl.pallas_call(functools.partial(spread_kernel, width=width, first_term=f...]
    psum x1 -> x0, waiting for transfers between devices: 85.1 us -> none  [on_device(): summed = lax.psum(partial_value, 'term')]
    another operation x6 -> x0, local copies, waits for them, and re-layouts: 83.9 us -> none  [the longest x4 65.5 us: inverse_columns(): jnp.stack([real_part.reshape(inner_shape), imag_part.reshape(inner_shape)...]
  transfers between devices with their start and end apart: 10 -> 15, of which waited for: 6 -> 9; matrix products, arithmetic and copies ran while one was open for 0% -> 3% of each run, Pallas kernels for 0% -> 1%
where the time goes in v1:
time: 646 us; the launch traced here: 644 us
  waiting for transfers between devices  240 us (37%)
  blocking collectives  211 us (33%)
  Pallas kernels  110 us (17%)
  starting transfers between devices  34.3 us (5%)
  local copies, waits for them, and re-layouts  21.3 us (3%)
  between operations  14 us (2%)
  other arithmetic  13.2 us (2%)
    all_to_all x2, blocking collectives, doubled(): rows_spec = lax.all_to_all(sent, 'pencil', 0, 0, tiled=True)  112 us
    all_to_all x1, blocking collectives, doubled(): restored = lax.all_to_all(restored, 'pencil', 0, 0, tiled=True)  99.1 us
    all_gather x2, waiting for transfers between devices, doubled(): spectrum = lax.all_gather(part, 'term', axis=0, tiled=False)  82.1 us
    all_to_all x1, waiting for transfers between devices, doubled(): restored = lax.all_to_all(restored, 'pencil', 0, 0, tiled=True)  81.1 us
    reduce_scatter x2, waiting for transfers between devices, doubled(): return lax.psum_scatter(partial, 'term', scatter_dimension=0, tiled=True)  66.5 us
    pallas_call x2, Pallas kernels, spread(): pl.pallas_call(functools.partial(spread_kernel, width=width, first_term=f...  51.4 us
    pallas_call x2, Pallas kernels, gather(): pl.pallas_call(gather_kernel, grid=(length_y,), in_specs=[pl.BlockSpec((b...  35.8 us
    unnamed x20, local copies, waits for them, and re-layouts  16.7 us
  transfers between devices with their start and end apart: 15, of which 9 were waited for; matrix products, arithmetic and copies ran while one was open for 3% of the time, Pallas kernels for 1%

profile of v1, /device:TPU:11, one launch (start us, length us, event | category | flops | bytes accessed | tf_op | source)
XLA Modules:
  0.0 644.0 jit_solution(9041751056073657917)
XLA Ops:
  7.2 7.9 %mirror.1 = f32[4,16,32,512]{3,2,1,0:T(8,128)} custom-call(f32[4,16,64,512]{3,2,1,0:T(8,128)} %own_ref.3, bf16[512,512]{1,0:T(8,128)(2,1)} %constant.38.clone.table_ref), custom_call_target="tpu_custom_call" | custom-call | flops 3221225472 | bytes 8388608 | tf_op jit(solution)/shard_map/mirror/pallas_call | solution.py:402
  15.1 1.8 collective-permute-start.1
  17.0 1.0 copy.60
  18.0 3.7 forward_z.2
  21.7 96.2 %all_to_all.20 = f32[8,64,384]{2,1,0:T(8,128)} all-to-all(f32[8,64,384]{2,1,0:T(8,128)} %forward_z.2), channel_id=1, replica_groups=mesh['term'=4,'pencil'=8] {'pencil'}, dimensions={0} | all-to-all | bytes 1572864 | tf_op jit(solution)/shard_map/all_to_all | solution.py:477
  117.9 3.7 forward_x.2
  121.6 1.3 slice.105
  123.2 0.5 reverse.4
  123.8 0.1 fusion.20
  124.0 2.4 collective-permute-start
  126.4 4.3 collective-permute-done
  130.8 0.7 pad.11.first_ref
  131.5 36.3 %all-gather.5.cloned.1.call-done = f32[1056,512]{1,0:T(8,128)} async-done(((f32[264,512]{1,0:T(8,128)}), f32[1056,512]{1,0:T(8,128)}) %all-gather.5.cloned.1.call-update) | async-done | bytes 2162704 | tf_op jit(solution)/shard_map/all_gather | solution.py:479
  167.8 25.7 %spread.2 = f32[8,4,16,32,128]{4,3,2,1,0:T(8,128)} custom-call(f32[4,264,512]{2,1,0:T(8,128)} %bitcast.69, f32[16,8,512]{2,1,0:T(8,128)} %pad.11.first_ref, f32[4,16,64,512]{3,2,1,0:T(8,128)} %own_ref.3, f32[4,16,32,512]{3,2,1,0:T(8,128)} %collective-permute-done.1.other_ref, bf16[1024,1024]{1,0:T(8,128)(2,1)} %constant.43.clone.high_ref, ...), custom_call_target="tpu_custom_call" | custom-call | flops 12884901888 | bytes 16777216 | tf_op jit(solution)/shard_map/spread/pallas_call | solution.py:321
  193.5 6.0 all-to-all-start.1
  199.5 11.5 %copy.59 = f32[4,64,16,512]{3,1,2,0:T(8,128)} copy(f32[4,64,16,512]{3,2,1,0:T(8,128)} %param.26) | data formatting | bytes 16777216 | tf_op args[2]
  211.0 81.1 %all-to-all-done.1.data_ref = f32[8,4,16,32,128]{4,3,2,1,0:T(8,128)} async-done(((f32[8,4,16,32,128]{4,3,2,1,0:T(8,128)}), f32[8,4,16,32,128]{4,3,2,1,0:T(8,128)}, u32[]{:S(2)}, u32[]{:S(2)}) %all-to-all-start.1) | async-done | bytes 8388640 | tf_op jit(solution)/shard_map/all_to_all | solution.py:481
  292.1 17.9 %gather_z.2 = f32[16,64,512]{2,1,0:T(8,128)} custom-call(f32[8,4,16,32,128]{4,3,2,1,0:T(8,128)} %all-to-all-done.1.data_ref, f32[4,16,64,512]{3,2,1,0:T(8,128)} %bitcast.61, bf16[512,512]{1,0:T(8,128)(2,1)} %constant.45.clone.high_ref, bf16[512,512]{1,0:T(8,128)(2,1)} %constant.46.clone.low_ref), custom_call_target="tpu_custom_call" | custom-call | flops 6442450944 | bytes 16777216 | tf_op jit(solution)/shard_map/gather_z/pallas_call | solution.py:367
  310.1 1.3 constant_dynamic-slice_fusion
  311.4 39.5 %reduce-scatter.3.cloned.1.call-done = f32[4,64,512]{2,1,0:T(8,128)} async-done(((f32[16,64,512]{2,1,0:T(8,128)}), f32[4,64,512]{2,1,0:T(8,128)}) %reduce-scatter.3.cloned.1.call-update) | async-done | bytes 524304 | tf_op jit(solution)/shard_map/reduce_scatter | solution.py:483
  350.9 2.0 fusion.19.brick_ref
  353.0 3.7 forward_z.3
  356.6 16.1 %all_to_all.21 = f32[8,64,384]{2,1,0:T(8,128)} all-to-all(f32[8,64,384]{2,1,0:T(8,128)} %forward_z.3), channel_id=1, replica_groups=mesh['term'=4,'pencil'=8] {'pencil'}, dimensions={0} | all-to-all | bytes 1572864 | tf_op jit(solution)/shard_map/all_to_all | solution.py:477
  372.7 3.7 forward_x.3
  376.5 45.8 %all-gather.7.cloned.1.call-done = f32[1056,512]{1,0:T(8,128)} async-done(((f32[264,512]{1,0:T(8,128)}), f32[1056,512]{1,0:T(8,128)}) %all-gather.7.cloned.1.call-update) | async-done | bytes 2162704 | tf_op jit(solution)/shard_map/all_gather | solution.py:479
  422.3 25.7 %spread.3 = f32[8,4,16,32,128]{4,3,2,1,0:T(8,128)} custom-call(f32[4,264,512]{2,1,0:T(8,128)} %bitcast.70, f32[16,8,512]{2,1,0:T(8,128)} %pad.11.first_ref, f32[4,16,64,512]{3,2,1,0:T(8,128)} %own_ref.3, f32[4,16,32,512]{3,2,1,0:T(8,128)} %collective-permute-done.1.other_ref, bf16[1024,1024]{1,0:T(8,128)(2,1)} %constant.43.clone.high_ref, ...), custom_call_target="tpu_custom_call" | custom-call | flops 12884901888 | bytes 16777216 | tf_op jit(solution)/shard_map/spread/pallas_call | solution.py:321
  448.1 99.1 %all_to_all.22.data_ref = f32[8,4,16,32,128]{4,3,2,1,0:T(8,128)} all-to-all(f32[8,4,16,32,128]{4,3,2,1,0:T(8,128)} %spread.3), channel_id=1, replica_groups=mesh['term'=4,'pencil'=8] {'pencil'}, dimensions={0} | all-to-all | bytes 16777216 | tf_op jit(solution)/shard_map/all_to_all | solution.py:481
  547.2 17.9 %gather_z.3 = f32[16,64,512]{2,1,0:T(8,128)} custom-call(f32[8,4,16,32,128]{4,3,2,1,0:T(8,128)} %all_to_all.22.data_ref, f32[4,16,64,512]{3,2,1,0:T(8,128)} %bitcast.62, bf16[512,512]{1,0:T(8,128)(2,1)} %constant.45.clone.high_ref, bf16[512,512]{1,0:T(8,128)(2,1)} %constant.46.clone.low_ref), custom_call_target="tpu_custom_call" | custom-call | flops 6442450944 | bytes 16777216 | tf_op jit(solution)/shard_map/gather_z/pallas_call | solution.py:367
  565.1 1.0 copy-done.4
  566.1 0.2 copy.61
  566.4 3.5 collective-permute-start.2
  569.9 1.9 collective-permute-start.3
  571.9 4.1 collective-permute-start.4
  576.0 1.9 collective-permute-start.5
  578.1 0.7 fusion.29
  578.8 3.1 collective-permute-done.5
  581.9 0.2 collective-permute-done.3
  582.1 26.9 %reduce-scatter.5.cloned.1.call-done = f32[4,64,512]{2,1,0:T(8,128)} async-done(((f32[16,64,512]{2,1,0:T(8,128)}), f32[4,64,512]{2,1,0:T(8,128)}) %reduce-scatter.5.cloned.1.call-update) | async-done | bytes 524304 | tf_op jit(solution)/shard_map/reduce_scatter | solution.py:483
  609.0 5.8 fusion.6
  615.0 4.8 collective-permute-start.6
  619.8 1.9 collective-permute-start.7
  621.7 3.9 collective-permute-start.8
  625.7 1.9 collective-permute-start.9
  627.6 0.2 subtract_bitcast_fusion
  627.9 1.1 copy.33
  629.1 2.5 collective-permute-done.9
  631.6 4.8 fusion.14
  636.3 1.1 copy.34
  (41 shorter events, 1.3 us)
Async XLA Ops:
  7.2 9.7 %copy-start = (f32[64,16,512]{2,1,0:T(8,128)S(1)}, f32[64,16,512]{2,1,0:T(8,128)}, u32[]{:S(2)}) copy-start(f32[64,16,512]{2,1,0:T(8,128)} %param.24) | copy-start | bytes 6291460
  7.2 160.6 %all-gather.5.cloned.1.call-start = ((), (), s32[]{:S(2)}) async-start(), calls=%async_computation.8 | async-start | bytes 2703360 | tf_op jit(solution)/shard_map/all_gather | solution.py:479
  15.1 152.7 %collective-permute-start.1 = (f32[4,16,32,512]{3,2,1,0:T(8,128)}, f32[4,16,32,512]{3,2,1,0:T(8,128)}, u32[]{:S(2)}, u32[]{:S(2)}) collective-permute-start(f32[4,16,32,512]{3,2,1,0:T(8,128)} %mirror.1), channel_id=1, source_target_pairs={{0,7},{1,6},{2,5},{3,4},{4,3},{5,2},{6,1},{7,0},{8,15},{9,14},{10,... | collective-permute-start | bytes 12582920 | tf_op jit(solution)/shard_map/ppermute | solution.py:466
  124.0 6.7 %collective-permute-start = (f32[4,16,512]{2,0,1:T(4,128)S(1)}, f32[4,16,512]{2,0,1:T(4,128)S(1)}, u32[]{:S(2)}, u32[]{:S(2)}) collective-permute-start(f32[4,16,512]{2,0,1:T(4,128)S(1)} %fusion.20), channel_id=1, source_target_pairs={{1,7},{2,6},{3,5},{5,3},{6,2},{7,1},{9,15},{10,14},{11,13},{13,11}... | collective-permute-start | bytes 393224 | tf_op jit(solution)/shard_map/ppermute | solution.py:468
  193.5 98.6 %all-to-all-start.1 = ((f32[8,4,16,32,128]{4,3,2,1,0:T(8,128)}), f32[8,4,16,32,128]{4,3,2,1,0:T(8,128)}, u32[]{:S(2)}, u32[]{:S(2)}) async-start(f32[8,4,16,32,128]{4,3,2,1,0:T(8,128)} %spread.2), calls=%async_computation.1 | async-start | bytes 16777216 | tf_op jit(solution)/shard_map/all_to_all | solution.py:481
  199.5 151.4 %reduce-scatter.3.cloned.1.call-start = ((), (), s32[]{:S(2)}) async-start(), calls=%async_computation.6 | async-start | bytes 2621440 | tf_op jit(solution)/shard_map/reduce_scatter | solution.py:483
  310.0 112.3 %all-gather.7.cloned.1.call-start = ((), (), s32[]{:S(2)}) async-start(), calls=%async_computation.9 | async-start | bytes 2703360 | tf_op jit(solution)/shard_map/all_gather | solution.py:479
  376.5 232.6 %reduce-scatter.5.cloned.1.call-start = ((), (), s32[]{:S(2)}) async-start(), calls=%async_computation.7 | async-start | bytes 2621440 | tf_op jit(solution)/shard_map/reduce_scatter | solution.py:483
  565.1 1.0 copy-start.4
  566.3 11.8 %copy-start.5 = (f32[3,2]{0,1:T(2,128)S(1)}, f32[3,2]{0,1:T(2,128)}, u32[]{:S(2)}) copy-start(f32[3,2]{0,1:T(2,128)} %param.29) | copy-start | bytes 76
  566.3 42.7 %copy-start.2 = (f32[4,64,512]{2,1,0:T(8,128)S(1)}, f32[4,64,512]{2,1,0:T(8,128)}, u32[]{:S(2)}) copy-start(f32[4,64,512]{2,1,0:T(8,128)} %fusion.19.brick_ref) | copy-start | bytes 1572868
  566.4 15.5 %collective-permute-start.2 = (f32[1,64,512]{2,1,0:T(8,128)S(1)}, f32[1,64,512]{2,1,0:T(8,128)S(1)}, u32[]{:S(2)}, u32[]{:S(2)}) collective-permute-start(f32[1,64,512]{2,1,0:T(8,128)S(1)} %get-tuple-element.22), channel_id=1, source_target_pairs={{0,8},{8,16},{16,24},{1,9},{9,17},{17,25},{2,10},{10,18},{18,26},{... | collective-permute-start | bytes 393224 | tf_op jit(solution)/shard_map/ppermute | solution.py:428
  569.9 12.2 %collective-permute-start.3 = (f32[1,64,512]{2,1,0:T(8,128)S(1)}, f32[1,64,512]{2,1,0:T(8,128)}, u32[]{:S(2)}, u32[]{:S(2)}) collective-permute-start(f32[1,64,512]{2,1,0:T(8,128)S(1)} %get-tuple-element.21), channel_id=1, source_target_pairs={{8,0},{16,8},{24,16},{9,1},{17,9},{25,17},{10,2},{18,10},{26,18},{... | collective-permute-start | bytes 393224 | tf_op jit(solution)/shard_map/ppermute | solution.py:429
  571.9 6.9 %collective-permute-start.4 = (f32[4,1,512]{2,1,0:T(1,128)S(1)}, f32[4,1,512]{2,1,0:T(1,128)S(1)}, u32[]{:S(2)}, u32[]{:S(2)}) collective-permute-start(f32[4,1,512]{2,1,0:T(1,128)S(1)} %get-tuple-element.18), channel_id=1, source_target_pairs={{0,1},{1,2},{2,3},{3,4},{4,5},{5,6},{6,7},{8,9},{9,10},{10,11},{11... | collective-permute-start | bytes 24584 | tf_op jit(solution)/shard_map/ppermute | solution.py:428
  576.0 5.9 collective-permute-start.5
  614.9 12.7 %copy-start.3 = (f32[4,64,512]{2,1,0:T(8,128)S(1)}, f32[4,64,512]{2,1,0:T(8,128)}, u32[]{:S(2)}) copy-start(f32[4,64,512]{2,1,0:T(8,128)} %reduce-scatter.5.cloned.1.call-done) | copy-start | bytes 1572868
  615.0 16.5 %collective-permute-start.6 = (f32[1,64,512]{2,1,0:T(8,128)S(1)}, f32[1,64,512]{2,1,0:T(8,128)S(1)}, u32[]{:S(2)}, u32[]{:S(2)}) collective-permute-start(f32[1,64,512]{2,1,0:T(8,128)S(1)} %get-tuple-element.14), channel_id=1, source_target_pairs={{0,8},{8,16},{16,24},{1,9},{9,17},{17,25},{2,10},{10,18},{18,26},{... | collective-permute-start | bytes 393224 | tf_op jit(solution)/shard_map/ppermute | solution.py:428
  619.8 11.7 %collective-permute-start.7 = (f32[1,64,512]{2,1,0:T(8,128)S(1)}, f32[1,64,512]{2,1,0:T(8,128)S(1)}, u32[]{:S(2)}, u32[]{:S(2)}) collective-permute-start(f32[1,64,512]{2,1,0:T(8,128)S(1)} %get-tuple-element.13), channel_id=1, source_target_pairs={{8,0},{16,8},{24,16},{9,1},{17,9},{25,17},{10,2},{18,10},{26,18},{... | collective-permute-start | bytes 393224 | tf_op jit(solution)/shard_map/ppermute | solution.py:429
  621.7 7.3 %collective-permute-start.8 = (f32[4,1,512]{2,1,0:T(1,128)S(1)}, f32[4,1,512]{2,1,0:T(1,128)S(1)}, u32[]{:S(2)}, u32[]{:S(2)}) collective-permute-start(f32[4,1,512]{2,1,0:T(1,128)S(1)} %get-tuple-element.10), channel_id=1, source_target_pairs={{0,1},{1,2},{2,3},{3,4},{4,5},{5,6},{6,7},{8,9},{9,10},{10,11},{11... | collective-permute-start | bytes 24584 | tf_op jit(solution)/shard_map/ppermute | solution.py:428
  625.7 5.9 collective-permute-start.9
  631.5 5.9 copy-start.1
Sparse Core Ops, SparseCore 0:
  121.7 46.0 all-gather.4
  310.1 40.7 reduce-scatter.2
  376.6 45.7 all-gather.6
  565.2 43.7 reduce-scatter.4

commit v2 on v1

v2 whole, which is shorter than its diff:
```python
import functools
import math

import jax
import jax.numpy as jnp
import ml_dtypes
import numpy as np
from jax import lax
from jax.experimental import pallas as pl
from jax.experimental.pallas import tpu as pltpu
from jax.sharding import PartitionSpec as P

WAVE_STEPS = 2
HEAT_STEPS = 2
DIFFUSION = 0.125
VMEM_BYTES = 56 * 1024 * 1024
F32 = jnp.float32
BF16 = jnp.bfloat16


def halves(table):
    high = table.astype(ml_dtypes.bfloat16)
    low = (table - high.astype(np.float64)).astype(ml_dtypes.bfloat16)
    return high, low


def angles(left, right, length):
    return (np.outer(left, right) % length) * (2.0 * math.pi / length)


def slot_wavenumbers(blocks, length_z):
    width = length_z // blocks
    half = width // 2
    slots = np.concatenate([[half], np.arange(1, half)])
    starts = np.arange(blocks) * width
    return starts[:, None] + slots[None, :], starts


def forward_z_table(blocks, length_z):
    main, first = slot_wavenumbers(blocks, length_z)
    z = np.arange(length_z)
    theta = angles(z, main.reshape(-1), length_z).reshape(length_z, blocks, -1)
    real, imag = np.cos(theta), -np.sin(theta)
    for q in range(blocks // 2):
        real[:, q, 0], imag[:, q, 0] = -imag[:, q, 0].copy(), real[:, q, 0].copy()
    theta = angles(z, first, length_z)
    real0, imag0 = np.cos(theta), -np.sin(theta)
    for q in range(blocks // 2 + 1, blocks):
        real0[:, q], imag0[:, q] = imag0[:, q].copy(), -real0[:, q].copy()
    table = np.concatenate(
        [np.stack([real, imag], 2).reshape(length_z, -1), np.stack([real0, imag0], 2).reshape(length_z, -1)], axis=1
    )
    spare = -table.shape[1] % 128
    return np.pad(table, ((0, 0), (0, spare)))


def inverse_z_table(blocks, length_z, scale):
    main, first = slot_wavenumbers(blocks, length_z)
    z = np.arange(length_z)
    theta = angles(main.reshape(-1), z, length_z).reshape(blocks, -1, length_z)
    real, imag = np.cos(theta), -np.sin(theta)
    for p in range(blocks):
        middle = theta[p, 0]
        imag[p, 0] = np.cos(middle) if p < blocks // 2 else -np.sin(middle)
        lowest = angles(first[p : p + 1], z, length_z)[0]
        real[p, 0] = np.cos(lowest) if p <= blocks // 2 else -np.sin(lowest)
    return scale * np.concatenate([real.reshape(-1, length_z), imag.reshape(-1, length_z)], axis=0)


def forward_x_table(length_x):
    x = np.arange(length_x)
    theta = angles(x, x, length_x)
    return np.concatenate([np.cos(theta), np.sin(theta)], axis=1)


def inverse_x_table(blocks, length_x):
    x = np.arange(length_x)
    theta = angles(x, x, length_x).reshape(length_x, blocks, -1)
    cosine, sine = np.cos(theta), np.sin(theta)
    real_rows = np.stack([cosine, sine], axis=2).reshape(length_x, -1)
    imag_rows = np.stack([-sine, cosine], axis=2).reshape(length_x, -1)
    return np.concatenate([real_rows, imag_rows], axis=0)


def mirror_table(length):
    x = np.arange(length)
    table = np.zeros((length, length), ml_dtypes.bfloat16)
    table[x, (-x) % length] = 1
    return table


def turned_by(a, b, k, count, sign):
    if k == 0:
        return a, b
    if 4 * k == count:
        return (-b, a) if sign > 0 else (b, -a)
    angle = 2.0 * math.pi * k / count
    c, s = math.cos(angle), sign * math.sin(angle)
    if 8 * k == count or 8 * k == 3 * count:
        root = math.sqrt(0.5)
        sum_ab, less_ab = root * (a + b), root * (a - b)
        if c > 0:
            return (less_ab, sum_ab) if s > 0 else (sum_ab, -less_ab)
        return (-sum_ab, less_ab) if s > 0 else (-less_ab, -sum_ab)
    return c * a - s * b, c * b + s * a


def fourier(values, sign, wanted=None):
    count = len(values)
    wanted = range(count) if wanted is None else wanted
    if not wanted:
        return {}
    if count == 1:
        return {0: values[0]}
    if count % 2:
        out = {}
        for k in wanted:
            real, imag = values[0]
            for n in range(1, count):
                angle = 2.0 * math.pi * (k * n % count) / count
                c, s = math.cos(angle), sign * math.sin(angle)
                a, b = values[n]
                real, imag = real + (c * a - s * b), imag + (c * b + s * a)
            out[k] = (real, imag)
        return out
    half = count // 2
    out = {}
    even = [k // 2 for k in wanted if k % 2 == 0]
    odd = [k // 2 for k in wanted if k % 2]
    if even:
        added = [(values[n][0] + values[n + half][0], values[n][1] + values[n + half][1]) for n in range(half)]
        for k, value in fourier(added, sign, even).items():
            out[2 * k] = value
    if odd:
        less = [
            turned_by(values[n][0] - values[n + half][0], values[n][1] - values[n + half][1], n, count, sign)
            for n in range(half)
        ]
        for k, value in fourier(less, sign, odd).items():
            out[2 * k + 1] = value
    return out


def split(values):
    high = values.astype(BF16)
    return high, (values - high.astype(F32)).astype(BF16)


def dot(left, right):
    return jnp.dot(left, right, preferred_element_type=F32)


def dot_across(left, right):
    return lax.dot_general(left, right, (((1,), (1,)), ((), ())), preferred_element_type=F32)


def dot_three(high, low, table_high, table_low):
    return dot(high, table_high) + (dot(low, table_high) + dot(high, table_low))


def params(count=0):
    return pltpu.CompilerParams(vmem_limit_bytes=VMEM_BYTES, dimension_semantics=("arbitrary",) * count)


def cost(flops, moved):
    return pl.CostEstimate(flops=int(flops), bytes_accessed=int(moved), transcendentals=0)


def whole(shape, grid_rank):
    return pl.BlockSpec(shape, lambda *_: (0,) * len(shape), pipeline_mode=pl.Buffered(1)) if grid_rank else pl.BlockSpec(
        memory_space=pltpu.VMEM
    )


def forward_z_kernel(brick_ref, high_ref, low_ref, first_high_ref, first_low_ref, out_ref):
    width, rows, length_z = brick_ref.shape
    blocks = out_ref.shape[0]
    main = length_z // blocks
    high, low = split(brick_ref[...].reshape(width * rows, length_z))
    result = dot_three(high, low, high_ref[...], low_ref[...])
    first = (
        dot_across(first_high_ref[...], high)
        + (dot_across(first_low_ref[...], high) + dot_across(first_high_ref[...], low))
    )
    out_ref[:, rows:, :] = jnp.zeros_like(out_ref[:, rows:, :])
    for q in range(blocks):
        for w in range(width):
            out_ref[q, :rows, w * main : (w + 1) * main] = result[w * rows : (w + 1) * rows, q * main : (q + 1) * main]
            for c in range(2):
                row = rows + c * width + w
                out_ref[q, row : row + 1, :rows] = first[2 * q + c : 2 * q + c + 1, w * rows : (w + 1) * rows]


def forward_z(brick, blocks):
    width, rows, length_z = brick.shape
    lanes = max(width * length_z // blocks, rows)
    table = forward_z_table(blocks, length_z)
    high, low = halves(table[:, :length_z])
    first_high, first_low = halves(table[:, length_z : length_z + 2 * blocks].T)
    tables = [jnp.asarray(each) for each in (high, low, first_high, first_low)]
    return pl.pallas_call(
        forward_z_kernel,
        out_shape=jax.ShapeDtypeStruct((blocks, rows + 2 * width + (-2 * width) % 8, lanes), F32),
        compiler_params=params(),
        cost_estimate=cost(6 * width * rows * length_z * length_z, 16 * width * rows * length_z),
        name="forward_z",
    )(brick, *tables)


def forward_x_kernel(data_ref, high_ref, low_ref, out_ref, *, width, half, rows):
    blocks = data_ref.shape[0]
    length_x = blocks * rows
    main = width * 2 * half
    turned = data_ref[:, :rows, :main].reshape(length_x, main).T
    first = jnp.concatenate([data_ref[q, rows:, :rows] for q in range(blocks)], axis=1)
    high, low = split(jnp.concatenate([turned, first], axis=0))
    both = dot_three(high, low, high_ref[...], low_ref[...])
    by_cos, by_sin = both[:, :length_x], both[:, length_x:]
    for w in range(width):
        re, im = w * 2 * half, w * 2 * half + half
        out_ref[re : re + half] = by_cos[re : re + half] + by_sin[im : im + half]
        out_ref[im : im + half] = by_cos[im : im + half] - by_sin[re : re + half]
    re, im, end = main, main + width, main + 2 * width
    out_ref[re:im] = by_cos[re:im] + by_sin[im:end]
    out_ref[im:end] = by_cos[im:end] - by_sin[re:im]
    if end < out_ref.shape[0]:
        out_ref[end:] = jnp.zeros_like(out_ref[end:])


def forward_x(data, width, half, rows):
    blocks = data.shape[0]
    length_x = blocks * rows
    out_rows = width * 2 * half + data.shape[1] - rows
    high, low = halves(forward_x_table(length_x))
    return pl.pallas_call(
        functools.partial(forward_x_kernel, width=width, half=half, rows=rows),
        out_shape=jax.ShapeDtypeStruct((out_rows, length_x), F32),
        compiler_params=params(),
        cost_estimate=cost(12 * out_rows * length_x * length_x, 8 * out_rows * length_x),
        name="forward_x",
    )(data, jnp.asarray(high), jnp.asarray(low))


def spread_kernel(*refs, groups, group):
    f_refs = refs[:groups]
    (
        first_ref, own_ref, other_ref, high_ref, low_ref, out_ref,
        fk_ref, edge_ref, edge_out_ref, u_ref, u_high_ref, u_low_ref,
    ) = refs[groups:]
    length_y, _, half, length_x = fk_ref.shape
    lanes_out = out_ref.shape[-1]
    rows_x = lanes_out // 2
    count_y = out_ref.shape[2]
    wide = count_y // f_refs[0].shape[0]
    width = wide * groups
    main = wide * 2 * half
    step = pl.program_id(0)
    tiles = [slice(at, at + 128) for at in range(0, length_x, 128)]
    wanted = [y for y in range(length_y) if y % width // wide == group]

    def place(y):
        return f_refs[y % width // wide], y // width, y % wide

    @pl.when(step == 0)
    def _():
        @pl.loop(0, half // 8)
        def _(tile):
            for lanes in tiles:
                values = []
                for y in range(length_y):
                    ref, at, w = place(y)
                    row = w * 2 * half + tile * 8
                    values.append((
                        ref[at, pl.ds(pl.multiple_of(row, 8), 8), lanes],
                        ref[at, pl.ds(pl.multiple_of(row + half, 8), 8), lanes],
                    ))
                values = fourier(values, -1)
                at = pl.ds(pl.multiple_of(tile * 8, 8), 8)
                for y in range(length_y):
                    fk_ref[y, 0, at, lanes] = values[y][0]
                    fk_ref[y, 1, at, lanes] = values[y][1]

        for index, lanes in enumerate(tiles):
            values = []
            for y in range(length_y):
                ref, at, w = place(y)
                values.append((
                    ref[at, main + w : main + w + 1, lanes],
                    ref[at, main + wide + w : main + wide + w + 1, lanes],
                ))
            values = fourier(values, -1)
            factors = [first_ref[y, :, lanes] for y in range(length_y)]
            values = [(factors[y] * values[y][0], factors[y] * values[y][1]) for y in range(length_y)]
            values = fourier(values, 1, wanted)
            for n, y in enumerate(wanted):
                edge_ref[n, :, index * 128 : index * 128 + 128] = values[y][0]
                edge_ref[n, :, length_x + index * 128 : length_x + index * 128 + 128] = values[y][1]
        high, low = split(edge_ref[...].reshape(-1, 2 * length_x))
        edge_out_ref[...] = dot_three(high, low, high_ref[...], low_ref[...])

    row_index = lax.broadcasted_iota(jnp.int32, (8, 128), 0)

    @pl.loop(0, half // 8)
    def _(tile):
        at = pl.ds(pl.multiple_of(tile * 8, 8), 8)
        swapped = jnp.logical_and(row_index == 0, tile == 0)
        for index, lanes in enumerate(tiles):
            values = []
            for y in range(length_y):
                own = jnp.where(swapped, own_ref[0, y, half : half + 1, lanes], own_ref[0, y, at, lanes])
                factor = own + other_ref[0, y, at, lanes]
                values.append((factor * fk_ref[y, 0, at, lanes], factor * fk_ref[y, 1, at, lanes]))
            values = fourier(values, 1, wanted)
            for n, y in enumerate(wanted):
                rows = pl.ds(pl.multiple_of(n * half + tile * 8, 8), 8)
                u_ref[rows, index * 128 : index * 128 + 128] = values[y][0]
                u_ref[rows, length_x + index * 128 : length_x + index * 128 + 128] = values[y][1]

    @pl.loop(0, count_y * half // 64)
    def _(part):
        rows = pl.ds(pl.multiple_of(part * 64, 64), 64)
        high, low = split(u_ref[rows, :])
        u_high_ref[rows, :] = high
        u_low_ref[rows, :] = low

    lane_index = lax.broadcasted_iota(jnp.int32, (8, lanes_out), 1)
    row_index = lax.broadcasted_iota(jnp.int32, (8, lanes_out), 0)
    swapped = jnp.logical_and(row_index == 0, lane_index < rows_x)
    count = 256 // lanes_out
    for part in range(2 * length_x // 256):
        cols = slice(part * 256, part * 256 + 256)
        result = dot_three(u_high_ref[...], u_low_ref[...], high_ref[:, cols], low_ref[:, cols])
        edges = [edge_out_ref[pl.ds(n * first_ref.shape[1] + step, 1), cols] for n in range(count_y)]
        for k in range(count):
            q = part * count + k
            inside = slice(k * lanes_out, (k + 1) * lanes_out)
            piece = result[:, inside]
            for n in range(count_y):
                top = piece[n * half : n * half + 8]
                out_ref[q, 0, n, :8, :] = jnp.where(swapped, edges[n][:, inside], top)
                out_ref[q, 0, n, 8:, :] = piece[n * half + 8 : (n + 1) * half]


def spread(parts, first, own, other, blocks, group):
    terms, length_y, _, length_x = own.shape
    half = other.shape[2]
    groups = len(parts)
    count_y = length_y // groups
    rows_x = length_x // blocks
    high, low = halves(inverse_x_table(blocks, length_x))
    high, low = jnp.asarray(high), jnp.asarray(low)
    rows = count_y * half
    return pl.pallas_call(
        functools.partial(spread_kernel, groups=groups, group=group),
        grid=(terms,),
        in_specs=[whole(part.shape, 1) for part in parts] + [
            whole(first.shape, 1),
            pl.BlockSpec((1, length_y, half + 8, length_x), lambda t: (t, 0, 0, 0)),
            pl.BlockSpec((1, length_y, half, length_x), lambda t: (t, 0, 0, 0)),
            whole(high.shape, 1),
            whole(low.shape, 1),
        ],
        out_specs=pl.BlockSpec((blocks, 1, count_y, half, 2 * rows_x), lambda t: (0, t, 0, 0, 0)),
        out_shape=jax.ShapeDtypeStruct((blocks, terms, count_y, half, 2 * rows_x), F32),
        scratch_shapes=[
            pltpu.VMEM((length_y, 2, half, length_x), F32),
            pltpu.VMEM((count_y, first.shape[1], 2 * length_x), F32),
            pltpu.VMEM((count_y * first.shape[1], 2 * length_x), F32),
            pltpu.VMEM((rows, 2 * length_x), F32),
            pltpu.VMEM((rows, 2 * length_x), BF16),
            pltpu.VMEM((rows, 2 * length_x), BF16),
        ],
        compiler_params=params(1),
        cost_estimate=cost(terms * 24 * rows * length_x * length_x, terms * 16 * rows * length_x),
        name="spread",
    )(*parts, first, own, other, high, low)


def gather_kernel(data_ref, factor_ref, high_ref, low_ref, out_ref):
    blocks, terms, _, half, lanes = data_ref.shape
    rows = lanes // 2
    parts = []
    for t in range(terms):
        turned = data_ref[:, t, 0].reshape(blocks * half, lanes).T
        parts.append(jnp.concatenate([turned[:rows], turned[rows:]], axis=1))
    high, low = split(jnp.concatenate(parts, axis=0))
    fields = dot_three(high, low, high_ref[...], low_ref[...])
    total = factor_ref[0, 0] * fields[:rows]
    for t in range(1, terms):
        total = total + factor_ref[t, 0] * fields[t * rows : (t + 1) * rows]
    out_ref[0] = total


def gather(data, factor, scale, width, groups, group):
    blocks, terms, count_y, half, lanes = data.shape
    rows, length_z = factor.shape[2], factor.shape[3]
    wide = width // groups
    high, low = halves(inverse_z_table(blocks, length_z, scale))
    return pl.pallas_call(
        gather_kernel,
        grid=(count_y,),
        in_specs=[
            pl.BlockSpec((blocks, terms, 1, half, lanes), lambda n: (0, 0, n, 0, 0)),
            pl.BlockSpec((terms, 1, rows, length_z), lambda n: (0, n // wide * width + group * wide + n % wide, 0, 0)),
            whole(high.shape, 1),
            whole(low.shape, 1),
        ],
        out_specs=pl.BlockSpec((1, rows, length_z), lambda n: (n, 0, 0)),
        out_shape=jax.ShapeDtypeStruct((count_y, rows, length_z), F32),
        compiler_params=params(1),
        cost_estimate=cost(6 * terms * count_y * rows * length_z * length_z, 8 * data.size),
        name="gather_z",
    )(data, factor, jnp.asarray(high), jnp.asarray(low))


def mirror_kernel(in_ref, table_ref, out_ref, turned_ref):
    _, length_y, half, length_x = in_ref.shape
    high, low = split(in_ref[0].reshape(length_y * half, length_x))
    rest = in_ref[0].reshape(length_y * half, length_x) - high.astype(F32) - low.astype(F32)
    table = table_ref[...]
    turned = (dot(high, table) + dot(low, table)) + dot(rest.astype(BF16), table)
    turned_ref[...] = turned.reshape(length_y, half, length_x)
    for y in range(length_y):
        source = -y % length_y
        for s in range(half):
            row = -s % half
            out_ref[0, y, s : s + 1, :] = turned_ref[source, row : row + 1, :]


def mirror(multiplier):
    terms, length_y, width, length_x = multiplier.shape
    half = width // 2
    table = mirror_table(length_x)
    return pl.pallas_call(
        mirror_kernel,
        grid=(terms,),
        in_specs=[
            pl.BlockSpec((1, length_y, half, length_x), lambda t: (t, 0, 1, 0)),
            whole(table.shape, 1),
        ],
        out_specs=pl.BlockSpec((1, length_y, half, length_x), lambda t: (t, 0, 0, 0)),
        out_shape=jax.ShapeDtypeStruct((terms, length_y, half, length_x), F32),
        scratch_shapes=[pltpu.VMEM((length_y, half, length_x), F32)],
        compiler_params=params(1),
        cost_estimate=cost(6 * terms * length_y * half * length_x * length_x, 4 * multiplier.size),
        name="mirror",
    )(multiplier, jnp.asarray(table))


def flip(values, axis):
    return jnp.roll(jnp.flip(values, axis), 1, axis)


def padded_by_one(block, sides):
    for axis, dim in sides:
        count = lax.axis_size(axis)
        forward = [(i, i + 1) for i in range(count - 1)]
        backward = [(target, source) for source, target in forward]
        size = block.shape[dim]
        low = lax.ppermute(lax.slice_in_dim(block, size - 1, size, axis=dim), axis, forward)
        high = lax.ppermute(lax.slice_in_dim(block, 0, 1, axis=dim), axis, backward)
        yield dim, low, high


def heat_step(heat, perfuse):
    near = jnp.zeros_like(heat)
    for dim, low, high in padded_by_one(heat, (("term", 0), ("pencil", 1))):
        size = heat.shape[dim]
        near = near + jnp.concatenate([low, lax.slice_in_dim(heat, 0, size - 1, axis=dim)], axis=dim)
        near = near + jnp.concatenate([lax.slice_in_dim(heat, 1, size, axis=dim), high], axis=dim)
    deep = jnp.pad(heat, ((0, 0), (0, 0), (1, 1)))
    near = near + deep[:, :, 2:] + deep[:, :, :-2]
    return heat + DIFFUSION * (near - 6.0 * heat) - perfuse * heat


def on_device(
    present_acoustic,
    prior_acoustic,
    location_factor,
    spectral_multiplier,
    medium_kinds,
    organ_properties,
    thermal_increase,
):
    term_count = lax.axis_size("term")
    blocks = lax.axis_size("pencil")
    rows, length_y, length_z = present_acoustic.shape
    length_x = rows * blocks
    width = length_y // term_count
    half = length_z // blocks // 2
    terms = location_factor.shape[0]
    brick_start = lax.axis_index("term") * width
    scale = 2.0 / (length_x * length_y * length_z)

    groups = 2 if width % 4 == 0 else 1
    wide = width // groups

    def to_brick(values):
        brick = jnp.transpose(lax.dynamic_slice_in_dim(values, brick_start, width, 1), (1, 0, 2))
        return [brick[g * wide : (g + 1) * wide] for g in range(groups)]

    def rows_to_columns(brick):
        return lax.all_to_all(forward_z(brick, blocks), "pencil", 0, 0, tiled=True)

    current = to_brick(present_acoustic)
    sent = [rows_to_columns(part) for part in current]
    mirrored = mirror(spectral_multiplier)
    *sent, mirrored = lax.optimization_barrier((*sent, mirrored))
    other = lax.ppermute(mirrored, "pencil", [(p, blocks - 1 - p) for p in range(blocks)])
    lowest = spectral_multiplier[:, :, 0, :]
    lowest = lowest + lax.ppermute(
        flip(flip(lowest, 1), 2), "pencil", [(p, blocks - p) for p in range(1, blocks) if 2 * p != blocks]
    )
    lowest = jnp.transpose(lowest, (1, 0, 2))
    lowest = jnp.pad(lowest, ((0, 0), (0, -terms % 8), (0, 0)))
    factor = jnp.transpose(location_factor, (0, 2, 1, 3))

    def doubled(sent):
        parts = [lax.all_gather(forward_x(each, wide, half, rows), "term", axis=0, tiled=False) for each in sent]
        bricks = []
        for g in range(groups):
            restored = spread(parts, lowest, spectral_multiplier, other, blocks, g)
            restored = lax.all_to_all(restored, "pencil", 0, 0, tiled=True)
            partial = gather(restored, factor, scale, width, groups, g)
            bricks.append(lax.psum_scatter(partial, "term", scatter_dimension=0, tiled=True))
        return bricks

    kinds = jnp.transpose(medium_kinds, (1, 0, 2))
    absorb, perfuse = [
        jnp.where(
            kinds == 0,
            organ_properties[0, at],
            jnp.where(kinds == 1, organ_properties[1, at], organ_properties[2, at]),
        )
        for at in range(2)
    ]
    heat = heat_step(jnp.transpose(thermal_increase, (1, 0, 2)), perfuse)

    previous = to_brick(prior_acoustic)
    dose = [jnp.zeros(part.shape, F32) for part in current]
    for turn in range(WAVE_STEPS):
        if turn:
            sent = [rows_to_columns(part) for part in current]
        advanced = [fresh - old for fresh, old in zip(doubled(sent), previous)]
        dose = [total + fresh * fresh for total, fresh in zip(dose, advanced)]
        previous, current = current, advanced
    current = jnp.concatenate(current, axis=0)
    dose = jnp.concatenate(dose, axis=0)
    source = absorb * dose
    heat = heat + source
    for _ in range(HEAT_STEPS - 1):
        heat = heat_step(heat, perfuse) + source
    return jnp.transpose(current, (1, 0, 2)), jnp.transpose(heat, (1, 0, 2))


def solution(mesh):
    return jax.shard_map(
        on_device,
        mesh=mesh,
        in_specs=(
            P("pencil", None, None),
            P("pencil", None, None),
            P("term", "pencil", None, None),
            P("term", None, "pencil", None),
            P("pencil", "term", None),
            P(),
            P("pencil", "term", None),
        ),
        out_specs=(P("pencil", "term", None), P("pencil", "term", None)),
        check_vma=False,
    )
```

time: 646 us -> 567 us (0.88)
  blocking collectives: 211 us -> 21.9 us
  waiting for transfers between devices: 240 us -> 291 us
  Pallas kernels: 110 us -> 140 us
  starting transfers between devices: 34.3 us -> 60.4 us
    all_to_all x3 -> x2, blocking collectives: 211 us -> 21.9 us  [rows_to_columns(): return lax.all_to_all(forward_z(brick, blocks), 'pencil', 0, 0, tiled=True)]
    ppermute x1, waiting for transfers between devices: 4.26 us -> 82 us  [on_device(): lax.ppermute(flip(flip(lowest, 1), 2), 'pencil', [(p, blocks - p) for p i...]
    all_to_all x1 -> x4, waiting for transfers between devices: 81.1 us -> 124 us  [doubled(): restored = lax.all_to_all(restored, 'pencil', 0, 0, tiled=True)]
    all_gather x2 -> x4, waiting for transfers between devices: 82.1 us -> 42 us  [doubled(): lax.all_gather(forward_x(each, wide, half, rows), 'term', axis=0, tiled=F...]
    reduce_scatter x2 -> x4, waiting for transfers between devices: 66.5 us -> 36.8 us  [doubled(): lax.psum_scatter(partial, 'term', scatter_dimension=0, tiled=True)]
    pallas_call x4 -> x8, Pallas kernels: 87.2 us -> 109 us  [the longest x4 70.5 us: spread(): pl.pallas_call(functools.partial(spread_kernel, groups=groups, group=grou...]
    all_to_all x1 -> x4, starting transfers between devices: 5.97 us -> 23.4 us  [doubled(): restored = lax.all_to_all(restored, 'pencil', 0, 0, tiled=True)]
    all_to_all x0 -> x2, starting transfers between devices: none -> 9.55 us  [rows_to_columns(): return lax.all_to_all(forward_z(brick, blocks), 'pencil', 0, 0, tiled=True)]
  transfers between devices with their start and end apart: 15 -> 24, of which waited for: 9 -> 11; matrix products, arithmetic and copies ran while one was open for 3% -> 4% of each run, Pallas kernels for 1% -> 17%
where the time goes in v2:
time: 567 us; the launch traced here: 564 us
  waiting for transfers between devices  291 us (51%)
  Pallas kernels  140 us (25%)
  starting transfers between devices  60.4 us (11%)
  local copies, waits for them, and re-layouts  23.4 us (4%)
  blocking collectives  21.9 us (4%)
  between operations  14.5 us (3%)
  other arithmetic  13.5 us (2%)
    all_to_all x4, waiting for transfers between devices, doubled(): restored = lax.all_to_all(restored, 'pencil', 0, 0, tiled=True)  124 us
    ppermute x1, waiting for transfers between devices, on_device(): lax.ppermute(flip(flip(lowest, 1), 2), 'pencil', [(p, blocks - p) for p i...  82 us
    pallas_call x4, Pallas kernels, spread(): pl.pallas_call(functools.partial(spread_kernel, groups=groups, group=grou...  70.5 us
    all_gather x4, waiting for transfers between devices, doubled(): lax.all_gather(forward_x(each, wide, half, rows), 'term', axis=0, tiled=F...  42 us
    pallas_call x4, Pallas kernels, gather(): pl.pallas_call(gather_kernel, grid=(count_y,), in_specs=[pl.BlockSpec((bl...  39 us
    reduce_scatter x4, waiting for transfers between devices, doubled(): lax.psum_scatter(partial, 'term', scatter_dimension=0, tiled=True)  36.8 us
    all_to_all x4, starting transfers between devices, doubled(): restored = lax.all_to_all(restored, 'pencil', 0, 0, tiled=True)  23.4 us
    all_to_all x2, blocking collectives, rows_to_columns(): return lax.all_to_all(forward_z(brick, blocks), 'pencil', 0, 0, tiled=True)  21.9 us
  transfers between devices with their start and end apart: 24, of which 11 were waited for; matrix products, arithmetic and copies ran while one was open for 4% of the time, Pallas kernels for 17%

profile of v2, /device:TPU:11, one launch (start us, length us, event | category | flops | bytes accessed | tf_op | source)
XLA Modules:
  0.0 564.2 jit_solution(17466101271686969131)
XLA Ops:
  9.9 2.5 forward_z.4
  12.4 4.6 all-to-all-start
  17.0 2.5 forward_z.5
  19.5 3.1 all-to-all-done.data_ref
  22.6 5.0 all-to-all-start.1
  27.6 7.8 %mirror.1 = f32[4,16,32,512]{3,2,1,0:T(8,128)} custom-call(f32[4,16,64,512]{3,2,1,0:T(8,128)} %refs_3_.7, bf16[512,512]{1,0:T(8,128)(2,1)} %constant.46.clone.table_ref), custom_call_target="tpu_custom_call" | custom-call | flops 3221225472 | bytes 8388608 | tf_op jit(solution)/shard_map/mirror/pallas_call | solution.py:434
  36.9 3.1 forward_x.4
  40.0 3.1 forward_x.5
  45.5 3.1 collective-permute-start
  48.6 82.0 %collective-permute-done = f32[4,16,512]{2,0,1:T(4,128)S(1)} collective-permute-done((f32[4,16,512]{2,0,1:T(4,128)S(1)}, f32[4,16,512]{2,0,1:T(4,128)S(1)}, u32[]{:S(2)}, u32[]{:S(2)}) %collective-permute-start) | collective-permute-done | bytes 131104 | tf_op jit(solution)/shard_map/ppermute | solution.py:511
  131.5 17.7 %spread.5 = f32[8,4,8,32,128]{4,3,2,1,0:T(8,128)} custom-call(f32[4,136,512]{2,1,0:T(8,128)} %bitcast.62, f32[4,136,512]{2,1,0:T(8,128)} %bitcast.64, f32[16,8,512]{2,1,0:T(8,128)} %pad.11.refs_2_, f32[4,16,64,512]{3,2,1,0:T(8,128)} %refs_3_.7, f32[4,16,32,512]{3,2,1,0:T(8,128)} %collective-permute-done.1.refs_4_, ...), custom_call_target="tpu_custom_call" | custom-call | flops 6442450944 | bytes 8388608 | tf_op jit(solution)/shard_map/spread/pallas_call | solution.py:353
  149.1 5.8 %all-to-all-start.4 = ((f32[8,4,8,32,128]{4,3,2,1,0:T(8,128)}), f32[8,4,8,32,128]{4,3,2,1,0:T(8,128)}, u32[]{:S(2)}, u32[]{:S(2)}) async-start(f32[8,4,8,32,128]{4,3,2,1,0:T(8,128)} %spread.5), calls=%async_computation.5 | async-start | bytes 8388608 | tf_op jit(solution)/shard_map/all_to_all | solution.py:523
  155.0 17.6 %spread.4 = f32[8,4,8,32,128]{4,3,2,1,0:T(8,128)} custom-call(f32[4,136,512]{2,1,0:T(8,128)} %bitcast.63, f32[4,136,512]{2,1,0:T(8,128)} %bitcast.65, f32[16,8,512]{2,1,0:T(8,128)} %pad.11.refs_2_, f32[4,16,64,512]{3,2,1,0:T(8,128)} %refs_3_.7, f32[4,16,32,512]{3,2,1,0:T(8,128)} %collective-permute-done.1.refs_4_, ...), custom_call_target="tpu_custom_call" | custom-call | flops 6442450944 | bytes 8388608 | tf_op jit(solution)/shard_map/spread/pallas_call | solution.py:353
  172.6 30.0 %all-to-all-done.4.data_ref = f32[8,4,8,32,128]{4,3,2,1,0:T(8,128)} async-done(((f32[8,4,8,32,128]{4,3,2,1,0:T(8,128)}), f32[8,4,8,32,128]{4,3,2,1,0:T(8,128)}, u32[]{:S(2)}, u32[]{:S(2)}) %all-to-all-start.4) | async-done | bytes 4194336 | tf_op jit(solution)/shard_map/all_to_all | solution.py:523
  202.6 6.0 %all-to-all-start.2 = ((f32[8,4,8,32,128]{4,3,2,1,0:T(8,128)}), f32[8,4,8,32,128]{4,3,2,1,0:T(8,128)}, u32[]{:S(2)}, u32[]{:S(2)}) async-start(f32[8,4,8,32,128]{4,3,2,1,0:T(8,128)} %spread.4), calls=%async_computation.2 | async-start | bytes 8388608 | tf_op jit(solution)/shard_map/all_to_all | solution.py:523
  208.6 11.6 %copy.73 = f32[4,64,16,512]{3,1,2,0:T(8,128)} copy(f32[4,64,16,512]{3,2,1,0:T(8,128)} %param.50) | data formatting | bytes 16777216 | tf_op args[2]
  220.2 9.7 %gather_z.5 = f32[8,64,512]{2,1,0:T(8,128)} custom-call(f32[8,4,8,32,128]{4,3,2,1,0:T(8,128)} %all-to-all-done.4.data_ref, f32[4,16,64,512]{3,2,1,0:T(8,128)} %bitcast.47, bf16[512,512]{1,0:T(8,128)(2,1)} %constant.51.clone.high_ref, bf16[512,512]{1,0:T(8,128)(2,1)} %constant.52.clone.low_ref), custom_call_target="tpu_custom_call" | custom-call | flops 3221225472 | bytes 8388608 | tf_op jit(solution)/shard_map/gather_z/pallas_call | solution.py:399
  230.0 26.3 %all-to-all-done.2.data_ref = f32[8,4,8,32,128]{4,3,2,1,0:T(8,128)} async-done(((f32[8,4,8,32,128]{4,3,2,1,0:T(8,128)}), f32[8,4,8,32,128]{4,3,2,1,0:T(8,128)}, u32[]{:S(2)}, u32[]{:S(2)}) %all-to-all-start.2) | async-done | bytes 4194336 | tf_op jit(solution)/shard_map/all_to_all | solution.py:523
  256.3 9.7 %gather_z.4 = f32[8,64,512]{2,1,0:T(8,128)} custom-call(f32[8,4,8,32,128]{4,3,2,1,0:T(8,128)} %all-to-all-done.2.data_ref, f32[4,16,64,512]{3,2,1,0:T(8,128)} %bitcast.48, bf16[512,512]{1,0:T(8,128)(2,1)} %constant.51.clone.high_ref, bf16[512,512]{1,0:T(8,128)(2,1)} %constant.52.clone.low_ref), custom_call_target="tpu_custom_call" | custom-call | flops 3221225472 | bytes 8388608 | tf_op jit(solution)/shard_map/gather_z/pallas_call | solution.py:399
  267.7 23.8 %reduce-scatter.5.cloned.1.call-done = f32[2,64,512]{2,1,0:T(8,128)} async-done(((f32[8,64,512]{2,1,0:T(8,128)}), f32[2,64,512]{2,1,0:T(8,128)}) %reduce-scatter.5.cloned.1.call-update) | async-done | bytes 262160 | tf_op jit(solution)/shard_map/reduce_scatter | solution.py:525
  293.3 2.5 forward_z.6
  295.8 10.5 %all_to_all.40.data_ref = f32[8,72,128]{2,1,0:T(8,128)} all-to-all(f32[8,72,128]{2,1,0:T(8,128)} %forward_z.6), channel_id=1, replica_groups=mesh['term'=4,'pencil'=8] {'pencil'}, dimensions={0} | all-to-all | bytes 589824 | tf_op jit(solution)/shard_map/all_to_all | solution.py:503
  306.4 3.1 forward_x.6
  309.5 2.5 forward_z.7
  312.0 11.3 %all_to_all.41.data_ref = f32[8,72,128]{2,1,0:T(8,128)} all-to-all(f32[8,72,128]{2,1,0:T(8,128)} %forward_z.7), channel_id=1, replica_groups=mesh['term'=4,'pencil'=8] {'pencil'}, dimensions={0} | all-to-all | bytes 589824 | tf_op jit(solution)/shard_map/all_to_all | solution.py:503
  323.4 3.1 forward_x.7
  326.4 11.4 %all-gather.13.cloned.1.call-done = f32[544,512]{1,0:T(8,128)} async-done(((f32[136,512]{1,0:T(8,128)}), f32[544,512]{1,0:T(8,128)}) %all-gather.13.cloned.1.call-update) | async-done | bytes 1114128 | tf_op jit(solution)/shard_map/all_gather | solution.py:519
  337.9 30.5 %all-gather.15.cloned.1.call-done = f32[544,512]{1,0:T(8,128)} async-done(((f32[136,512]{1,0:T(8,128)}), f32[544,512]{1,0:T(8,128)}) %all-gather.15.cloned.1.call-update) | async-done | bytes 1114128 | tf_op jit(solution)/shard_map/all_gather | solution.py:519
  368.4 17.6 %spread.7 = f32[8,4,8,32,128]{4,3,2,1,0:T(8,128)} custom-call(f32[4,136,512]{2,1,0:T(8,128)} %bitcast.66, f32[4,136,512]{2,1,0:T(8,128)} %bitcast.68, f32[16,8,512]{2,1,0:T(8,128)} %pad.11.refs_2_, f32[4,16,64,512]{3,2,1,0:T(8,128)} %refs_3_.7, f32[4,16,32,512]{3,2,1,0:T(8,128)} %collective-permute-done.1.refs_4_, ...), custom_call_target="tpu_custom_call" | custom-call | flops 6442450944 | bytes 8388608 | tf_op jit(solution)/shard_map/spread/pallas_call | solution.py:353
  386.1 5.5 all-to-all-start.7
  391.6 17.6 %spread.6 = f32[8,4,8,32,128]{4,3,2,1,0:T(8,128)} custom-call(f32[4,136,512]{2,1,0:T(8,128)} %bitcast.67, f32[4,136,512]{2,1,0:T(8,128)} %bitcast.69, f32[16,8,512]{2,1,0:T(8,128)} %pad.11.refs_2_, f32[4,16,64,512]{3,2,1,0:T(8,128)} %refs_3_.7, f32[4,16,32,512]{3,2,1,0:T(8,128)} %collective-permute-done.1.refs_4_, ...), custom_call_target="tpu_custom_call" | custom-call | flops 6442450944 | bytes 8388608 | tf_op jit(solution)/shard_map/spread/pallas_call | solution.py:353
  409.2 30.1 %all-to-all-done.7.data_ref = f32[8,4,8,32,128]{4,3,2,1,0:T(8,128)} async-done(((f32[8,4,8,32,128]{4,3,2,1,0:T(8,128)}), f32[8,4,8,32,128]{4,3,2,1,0:T(8,128)}, u32[]{:S(2)}, u32[]{:S(2)}) %all-to-all-start.7) | async-done | bytes 4194336 | tf_op jit(solution)/shard_map/all_to_all | solution.py:523
  439.2 6.0 %all-to-all-start.6 = ((f32[8,4,8,32,128]{4,3,2,1,0:T(8,128)}), f32[8,4,8,32,128]{4,3,2,1,0:T(8,128)}, u32[]{:S(2)}, u32[]{:S(2)}) async-start(f32[8,4,8,32,128]{4,3,2,1,0:T(8,128)} %spread.6), calls=%async_computation.8 | async-start | bytes 8388608 | tf_op jit(solution)/shard_map/all_to_all | solution.py:523
  445.3 9.8 %gather_z.7 = f32[8,64,512]{2,1,0:T(8,128)} custom-call(f32[8,4,8,32,128]{4,3,2,1,0:T(8,128)} %all-to-all-done.7.data_ref, f32[4,16,64,512]{3,2,1,0:T(8,128)} %bitcast.49, bf16[512,512]{1,0:T(8,128)(2,1)} %constant.51.clone.high_ref, bf16[512,512]{1,0:T(8,128)(2,1)} %constant.52.clone.low_ref), custom_call_target="tpu_custom_call" | custom-call | flops 3221225472 | bytes 8388608 | tf_op jit(solution)/shard_map/gather_z/pallas_call | solution.py:399
  455.1 37.8 %all-to-all-done.6.data_ref = f32[8,4,8,32,128]{4,3,2,1,0:T(8,128)} async-done(((f32[8,4,8,32,128]{4,3,2,1,0:T(8,128)}), f32[8,4,8,32,128]{4,3,2,1,0:T(8,128)}, u32[]{:S(2)}, u32[]{:S(2)}) %all-to-all-start.6) | async-done | bytes 4194336 | tf_op jit(solution)/shard_map/all_to_all | solution.py:523
  492.9 9.7 %gather_z.6 = f32[8,64,512]{2,1,0:T(8,128)} custom-call(f32[8,4,8,32,128]{4,3,2,1,0:T(8,128)} %all-to-all-done.6.data_ref, f32[4,16,64,512]{3,2,1,0:T(8,128)} %bitcast.50, bf16[512,512]{1,0:T(8,128)(2,1)} %constant.51.clone.high_ref, bf16[512,512]{1,0:T(8,128)(2,1)} %constant.52.clone.low_ref), custom_call_target="tpu_custom_call" | custom-call | flops 3221225472 | bytes 8388608 | tf_op jit(solution)/shard_map/gather_z/pallas_call | solution.py:399
  503.6 2.7 collective-permute-start.2
  506.3 2.6 collective-permute-start.3
  509.5 4.0 collective-permute-start.4
  513.5 1.9 collective-permute-start.5
  516.3 13.0 %reduce-scatter.9.cloned.1.call-done = f32[2,64,512]{2,1,0:T(8,128)} async-done(((f32[8,64,512]{2,1,0:T(8,128)}), f32[2,64,512]{2,1,0:T(8,128)}) %reduce-scatter.9.cloned.1.call-update) | async-done | bytes 262160 | tf_op jit(solution)/shard_map/reduce_scatter | solution.py:525
  530.5 5.6 fusion.6
  536.4 4.0 collective-permute-start.6
  540.4 1.9 collective-permute-start.7
  542.3 3.6 collective-permute-start.8
  545.9 1.9 collective-permute-start.9
  549.0 2.8 collective-permute-done.9
  551.8 4.4 fusion.14
  (77 shorter events, 17.3 us)
Async XLA Ops:
  7.2 1.6 copy-start
  12.4 10.2 %all-to-all-start = ((f32[8,72,128]{2,1,0:T(8,128)}), f32[8,72,128]{2,1,0:T(8,128)S(1)}, u32[]{:S(2)}, u32[]{:S(2)}) async-start(f32[8,72,128]{2,1,0:T(8,128)} %forward_z.4), calls=%async_computation | async-start | bytes 589824 | tf_op jit(solution)/shard_map/all_to_all | solution.py:503
  22.6 12.7 %copy-start.4 = (f32[8,72,128]{2,1,0:T(8,128)}, f32[8,72,128]{2,1,0:T(8,128)S(1)}, u32[]{:S(2)}) copy-start(f32[8,72,128]{2,1,0:T(8,128)S(1)} %all-to-all-done.data_ref) | copy-start | bytes 884740
  22.6 12.7 %all-to-all-start.1 = ((f32[8,72,128]{2,1,0:T(8,128)}), f32[8,72,128]{2,1,0:T(8,128)S(1)}, u32[]{:S(2)}, u32[]{:S(2)}) async-start(f32[8,72,128]{2,1,0:T(8,128)} %forward_z.5), calls=%async_computation.1 | async-start | bytes 589824 | tf_op jit(solution)/shard_map/all_to_all | solution.py:503
  27.6 103.8 %all-gather.9.cloned.1.call-start = ((), (), s32[]{:S(2)}) async-start(), calls=%async_computation.16 | async-start | bytes 1392640 | tf_op jit(solution)/shard_map/all_gather | solution.py:519
  35.4 4.6 copy-start.5
  35.4 96.1 %collective-permute-start.1 = (f32[4,16,32,512]{3,2,1,0:T(8,128)}, f32[4,16,32,512]{3,2,1,0:T(8,128)}, u32[]{:S(2)}, u32[]{:S(2)}) collective-permute-start(f32[4,16,32,512]{3,2,1,0:T(8,128)} %mirror.1), channel_id=1, source_target_pairs={{0,7},{1,6},{2,5},{3,4},{4,3},{5,2},{6,1},{7,0},{8,15},{9,14},{10,... | collective-permute-start | bytes 12582920 | tf_op jit(solution)/shard_map/ppermute | solution.py:509
  40.0 91.5 %all-gather.11.cloned.1.call-start = ((), (), s32[]{:S(2)}) async-start(), calls=%async_computation.17 | async-start | bytes 1392640 | tf_op jit(solution)/shard_map/all_gather | solution.py:519
  45.5 85.1 %collective-permute-start = (f32[4,16,512]{2,0,1:T(4,128)S(1)}, f32[4,16,512]{2,0,1:T(4,128)S(1)}, u32[]{:S(2)}, u32[]{:S(2)}) collective-permute-start(f32[4,16,512]{2,0,1:T(4,128)S(1)} %fusion.19), channel_id=1, source_target_pairs={{1,7},{2,6},{3,5},{5,3},{6,2},{7,1},{9,15},{10,14},{11,13},{13,11}... | collective-permute-start | bytes 393224 | tf_op jit(solution)/shard_map/ppermute | solution.py:511
  149.1 53.5 %all-to-all-start.4 = ((f32[8,4,8,32,128]{4,3,2,1,0:T(8,128)}), f32[8,4,8,32,128]{4,3,2,1,0:T(8,128)}, u32[]{:S(2)}, u32[]{:S(2)}) async-start(f32[8,4,8,32,128]{4,3,2,1,0:T(8,128)} %spread.5), calls=%async_computation.5 | async-start | bytes 8388608 | tf_op jit(solution)/shard_map/all_to_all | solution.py:523
  202.6 53.7 %all-to-all-start.2 = ((f32[8,4,8,32,128]{4,3,2,1,0:T(8,128)}), f32[8,4,8,32,128]{4,3,2,1,0:T(8,128)}, u32[]{:S(2)}, u32[]{:S(2)}) async-start(f32[8,4,8,32,128]{4,3,2,1,0:T(8,128)} %spread.4), calls=%async_computation.2 | async-start | bytes 8388608 | tf_op jit(solution)/shard_map/all_to_all | solution.py:523
  208.6 59.0 %reduce-scatter.7.cloned.1.call-start = ((), (), s32[]{:S(2)}) async-start(), calls=%async_computation.13 | async-start | bytes 1310720 | tf_op jit(solution)/shard_map/reduce_scatter | solution.py:525
  230.0 61.4 %reduce-scatter.5.cloned.1.call-start = ((), (), s32[]{:S(2)}) async-start(), calls=%async_computation.12 | async-start | bytes 1310720 | tf_op jit(solution)/shard_map/reduce_scatter | solution.py:525
  266.0 71.8 %all-gather.13.cloned.1.call-start = ((), (), s32[]{:S(2)}) async-start(), calls=%async_computation.18 | async-start | bytes 1392640 | tf_op jit(solution)/shard_map/all_gather | solution.py:519
  309.4 59.0 %all-gather.15.cloned.1.call-start = ((), (), s32[]{:S(2)}) async-start(), calls=%async_computation.19 | async-start | bytes 1392640 | tf_op jit(solution)/shard_map/all_gather | solution.py:519
  386.1 53.2 %all-to-all-start.7 = ((f32[8,4,8,32,128]{4,3,2,1,0:T(8,128)}), f32[8,4,8,32,128]{4,3,2,1,0:T(8,128)}, u32[]{:S(2)}, u32[]{:S(2)}) async-start(f32[8,4,8,32,128]{4,3,2,1,0:T(8,128)} %spread.7), calls=%async_computation.10 | async-start | bytes 8388608 | tf_op jit(solution)/shard_map/all_to_all | solution.py:523
  439.2 53.7 %all-to-all-start.6 = ((f32[8,4,8,32,128]{4,3,2,1,0:T(8,128)}), f32[8,4,8,32,128]{4,3,2,1,0:T(8,128)}, u32[]{:S(2)}, u32[]{:S(2)}) async-start(f32[8,4,8,32,128]{4,3,2,1,0:T(8,128)} %spread.6), calls=%async_computation.8 | async-start | bytes 8388608 | tf_op jit(solution)/shard_map/all_to_all | solution.py:523
  445.3 71.1 %reduce-scatter.11.cloned.1.call-start = ((), (), s32[]{:S(2)}) async-start(), calls=%async_computation.15 | async-start | bytes 1310720 | tf_op jit(solution)/shard_map/reduce_scatter | solution.py:525
  455.1 47.6 %copy-start.6 = (f32[64,4,512]{2,1,0:T(4,128)S(1)}, f32[64,4,512]{2,1,0:T(4,128)}, u32[]{:S(2)}) copy-start(f32[64,4,512]{2,1,0:T(4,128)} %param.54) | copy-start | bytes 1572868
  455.1 60.3 %copy-start.7 = (f32[3,2]{0,1:T(2,128)S(1)}, f32[3,2]{0,1:T(2,128)}, u32[]{:S(2)}) copy-start(f32[3,2]{0,1:T(2,128)} %param.53) | copy-start | bytes 76
  455.1 74.2 %reduce-scatter.9.cloned.1.call-start = ((), (), s32[]{:S(2)}) async-start(), calls=%async_computation.14 | async-start | bytes 1310720 | tf_op jit(solution)/shard_map/reduce_scatter | solution.py:525
  502.6 26.7 %copy-start.2 = (f32[2,64,512]{2,1,0:T(8,128)S(1)}, f32[2,64,512]{2,1,0:T(8,128)}, u32[]{:S(2)}) copy-start(f32[2,64,512]{2,1,0:T(8,128)} %get-tuple-element.35.brick_ref) | copy-start | bytes 786436
  502.6 26.7 %copy-start.3 = (f32[2,64,512]{2,1,0:T(8,128)S(1)}, f32[2,64,512]{2,1,0:T(8,128)}, u32[]{:S(2)}) copy-start(f32[2,64,512]{2,1,0:T(8,128)} %get-tuple-element.36.brick_ref) | copy-start | bytes 786436
  503.6 26.9 %collective-permute-start.2 = (f32[1,64,512]{2,1,0:T(8,128)}, f32[1,64,512]{2,1,0:T(8,128)S(1)}, u32[]{:S(2)}, u32[]{:S(2)}) collective-permute-start(f32[1,64,512]{2,1,0:T(8,128)} %get-tuple-element.32), channel_id=1, source_target_pairs={{0,8},{8,16},{16,24},{1,9},{9,17},{17,25},{2,10},{10,18},{18,26},{... | collective-permute-start | bytes 393224 | tf_op jit(solution)/shard_map/ppermute | solution.py:460
  506.3 24.3 %collective-permute-start.3 = (f32[1,64,512]{2,1,0:T(8,128)}, f32[1,64,512]{2,1,0:T(8,128)}, u32[]{:S(2)}, u32[]{:S(2)}) collective-permute-start(f32[1,64,512]{2,1,0:T(8,128)} %get-tuple-element.31), channel_id=1, source_target_pairs={{8,0},{16,8},{24,16},{9,1},{17,9},{25,17},{10,2},{18,10},{26,18},{... | collective-permute-start | bytes 393224 | tf_op jit(solution)/shard_map/ppermute | solution.py:461
  509.5 21.0 %collective-permute-start.4 = (f32[4,1,512]{2,1,0:T(1,128)}, f32[4,1,512]{2,1,0:T(1,128)S(1)}, u32[]{:S(2)}, u32[]{:S(2)}) collective-permute-start(f32[4,1,512]{2,1,0:T(1,128)} %get-tuple-element.28), channel_id=1, source_target_pairs={{0,1},{1,2},{2,3},{3,4},{4,5},{5,6},{6,7},{8,9},{9,10},{10,11},{11... | collective-permute-start | bytes 24584 | tf_op jit(solution)/shard_map/ppermute | solution.py:460
  513.5 17.0 %collective-permute-start.5 = (f32[4,1,512]{2,1,0:T(1,128)}, f32[4,1,512]{2,1,0:T(1,128)S(1)}, u32[]{:S(2)}, u32[]{:S(2)}) collective-permute-start(f32[4,1,512]{2,1,0:T(1,128)} %get-tuple-element.27), channel_id=1, source_target_pairs={{1,0},{2,1},{3,2},{4,3},{5,4},{6,5},{7,6},{9,8},{10,9},{11,10},{12... | collective-permute-start | bytes 24584 | tf_op jit(solution)/shard_map/ppermute | solution.py:461
  536.3 21.1 %copy-start.1 = (f32[64,16,512]{2,1,0:T(8,128)S(1)}, f32[64,16,512]{2,1,0:T(8,128)}, u32[]{:S(2)}) copy-start(f32[64,16,512]{2,1,0:T(8,128)} %param.48) | copy-start | bytes 6291460
  536.4 15.4 %collective-permute-start.6 = (f32[1,64,512]{2,1,0:T(8,128)S(1)}, f32[1,64,512]{2,1,0:T(8,128)S(1)}, u32[]{:S(2)}, u32[]{:S(2)}) collective-permute-start(f32[1,64,512]{2,1,0:T(8,128)S(1)} %get-tuple-element.24), channel_id=1, source_target_pairs={{0,8},{8,16},{16,24},{1,9},{9,17},{17,25},{2,10},{10,18},{18,26},{... | collective-permute-start | bytes 393224 | tf_op jit(solution)/shard_map/ppermute | solution.py:460
  540.4 11.5 %collective-permute-start.7 = (f32[1,64,512]{2,1,0:T(8,128)S(1)}, f32[1,64,512]{2,1,0:T(8,128)S(1)}, u32[]{:S(2)}, u32[]{:S(2)}) collective-permute-start(f32[1,64,512]{2,1,0:T(8,128)S(1)} %get-tuple-element.23), channel_id=1, source_target_pairs={{8,0},{16,8},{24,16},{9,1},{17,9},{25,17},{10,2},{18,10},{26,18},{... | collective-permute-start | bytes 393224 | tf_op jit(solution)/shard_map/ppermute | solution.py:461
  542.3 6.7 %collective-permute-start.8 = (f32[4,1,512]{2,1,0:T(1,128)S(1)}, f32[4,1,512]{2,1,0:T(1,128)S(1)}, u32[]{:S(2)}, u32[]{:S(2)}) collective-permute-start(f32[4,1,512]{2,1,0:T(1,128)S(1)} %get-tuple-element.20), channel_id=1, source_target_pairs={{0,1},{1,2},{2,3},{3,4},{4,5},{5,6},{6,7},{8,9},{9,10},{10,11},{11... | collective-permute-start | bytes 24584 | tf_op jit(solution)/shard_map/ppermute | solution.py:460
  545.9 5.9 %collective-permute-start.9 = (f32[4,1,512]{2,1,0:T(1,128)S(1)}, f32[4,1,512]{2,1,0:T(1,128)S(1)}, u32[]{:S(2)}, u32[]{:S(2)}) collective-permute-start(f32[4,1,512]{2,1,0:T(1,128)S(1)} %get-tuple-element.19), channel_id=1, source_target_pairs={{1,0},{2,1},{3,2},{4,3},{5,4},{6,5},{7,6},{9,8},{10,9},{11,10},{12... | collective-permute-start | bytes 24584 | tf_op jit(solution)/shard_map/ppermute | solution.py:461
Sparse Core Ops, SparseCore 0:
  40.1 28.4 all-gather.8
  70.7 28.4 all-gather.10
  230.1 25.9 reduce-scatter.6
  266.2 25.1 reduce-scatter.4
  309.6 28.2 all-gather.12
  339.9 28.4 all-gather.14
  455.2 24.3 reduce-scatter.10
  502.8 26.4 reduce-scatter.8

commit v3 on v2

--- a/solution.py
+++ b/solution.py
@@ -172,11 +172,19 @@
     )
 
 
-def forward_z_kernel(brick_ref, high_ref, low_ref, first_high_ref, first_low_ref, out_ref):
-    width, rows, length_z = brick_ref.shape
+def forward_z_kernel(*refs, inputs):
+    fresh_ref, *older = refs[:inputs]
+    high_ref, low_ref, first_high_ref, first_low_ref, out_ref, *state = refs[inputs:]
+    width, rows, length_z = fresh_ref.shape
     blocks = out_ref.shape[0]
     main = length_z // blocks
-    high, low = split(brick_ref[...].reshape(width * rows, length_z))
+    brick = fresh_ref[...]
+    if older:
+        brick = brick - older[0][...]
+        state[0][...] = brick
+        dose = brick * brick
+        state[1][...] = dose + older[1][...] if len(older) > 1 else dose
+    high, low = split(brick.reshape(width * rows, length_z))
     result = dot_three(high, low, high_ref[...], low_ref[...])
     first = (
         dot_across(first_high_ref[...], high)
@@ -191,20 +199,23 @@
                 out_ref[q, row : row + 1, :rows] = first[2 * q + c : 2 * q + c + 1, w * rows : (w + 1) * rows]
 
 
-def forward_z(brick, blocks):
-    width, rows, length_z = brick.shape
+def forward_z(bricks, blocks):
+    width, rows, length_z = bricks[0].shape
     lanes = max(width * length_z // blocks, rows)
     table = forward_z_table(blocks, length_z)
     high, low = halves(table[:, :length_z])
     first_high, first_low = halves(table[:, length_z : length_z + 2 * blocks].T)
     tables = [jnp.asarray(each) for each in (high, low, first_high, first_low)]
+    out = [jax.ShapeDtypeStruct((blocks, rows + 2 * width + (-2 * width) % 8, lanes), F32)]
+    if len(bricks) > 1:
+        out += [jax.ShapeDtypeStruct(bricks[0].shape, F32)] * 2
     return pl.pallas_call(
-        forward_z_kernel,
-        out_shape=jax.ShapeDtypeStruct((blocks, rows + 2 * width + (-2 * width) % 8, lanes), F32),
+        functools.partial(forward_z_kernel, inputs=len(bricks)),
+        out_shape=out,
         compiler_params=params(),
         cost_estimate=cost(6 * width * rows * length_z * length_z, 16 * width * rows * length_z),
         name="forward_z",
-    )(brick, *tables)
+    )(*bricks, *tables)
 
 
 def forward_x_kernel(data_ref, high_ref, low_ref, out_ref, *, width, half, rows):
@@ -241,53 +252,56 @@
     )(data, jnp.asarray(high), jnp.asarray(low))
 
 
-def spread_kernel(*refs, groups, group):
-    f_refs = refs[:groups]
+def spread_kernel(*refs, spans, counts, group, pieces, first_term):
+    parts, at = [], 0
+    for count in counts:
+        parts.append(refs[at : at + count])
+        at += count
+    me_ref, first_ref, own_ref = refs[at : at + 3]
+    others = refs[at + 3 : at + 3 + len(pieces)]
     (
-        first_ref, own_ref, other_ref, high_ref, low_ref, out_ref,
-        fk_ref, edge_ref, edge_out_ref, u_ref, u_high_ref, u_low_ref,
-    ) = refs[groups:]
+        high_ref, low_ref, out_ref,
+        fk_ref, edge_in_ref, edge_ref, edge_out_ref, u_ref, u_high_ref, u_low_ref,
+    ) = refs[at + 3 + len(pieces) :]
     length_y, _, half, length_x = fk_ref.shape
     lanes_out = out_ref.shape[-1]
     rows_x = lanes_out // 2
     count_y = out_ref.shape[2]
-    wide = count_y // f_refs[0].shape[0]
-    width = wide * groups
-    main = wide * 2 * half
+    width = spans[-1][1]
+    holders = length_y // width
     step = pl.program_id(0)
     tiles = [slice(at, at + 128) for at in range(0, length_x, 128)]
-    wanted = [y for y in range(length_y) if y % width // wide == group]
-
-    def place(y):
-        return f_refs[y % width // wide], y // width, y % wide
+    wanted = [y for y in range(length_y) if group[0] <= y % width < group[1]]
 
     @pl.when(step == 0)
     def _():
+        for part, (start, end) in zip(parts, spans):
+            wide = end - start
+            for d in range(holders):
+                if len(part) == 1:
+                    source, holder = part[0].at[d], d
+                else:
+                    source, holder = part[d], lax.rem(me_ref[0] + d, holders)
+                for w in range(wide):
+                    y = holder * width + start + w
+                    fk_ref[y, 0] = source[w * 2 * half : w * 2 * half + half]
+                    fk_ref[y, 1] = source[w * 2 * half + half : (w + 1) * 2 * half]
+                    row = wide * 2 * half + w
+                    edge_in_ref[y, :1] = source[row : row + 1]
+                    edge_in_ref[y, 1:2] = source[row + wide : row + wide + 1]
+
         @pl.loop(0, half // 8)
         def _(tile):
+            at = pl.ds(pl.multiple_of(tile * 8, 8), 8)
             for lanes in tiles:
-                values = []
-                for y in range(length_y):
-                    ref, at, w = place(y)
-                    row = w * 2 * half + tile * 8
-                    values.append((
-                        ref[at, pl.ds(pl.multiple_of(row, 8), 8), lanes],
-                        ref[at, pl.ds(pl.multiple_of(row + half, 8), 8), lanes],
-                    ))
+                values = [(fk_ref[y, 0, at, lanes], fk_ref[y, 1, at, lanes]) for y in range(length_y)]
                 values = fourier(values, -1)
-                at = pl.ds(pl.multiple_of(tile * 8, 8), 8)
                 for y in range(length_y):
                     fk_ref[y, 0, at, lanes] = values[y][0]
                     fk_ref[y, 1, at, lanes] = values[y][1]
 
         for index, lanes in enumerate(tiles):
-            values = []
-            for y in range(length_y):
-                ref, at, w = place(y)
-                values.append((
-                    ref[at, main + w : main + w + 1, lanes],
-                    ref[at, main + wide + w : main + wide + w + 1, lanes],
-                ))
+            values = [(edge_in_ref[y, :1, lanes], edge_in_ref[y, 1:2, lanes]) for y in range(length_y)]
             values = fourier(values, -1)
             factors = [first_ref[y, :, lanes] for y in range(length_y)]
             values = [(factors[y] * values[y][0], factors[y] * values[y][1]) for y in range(length_y)]
@@ -300,21 +314,28 @@
 
     row_index = lax.broadcasted_iota(jnp.int32, (8, 128), 0)
 
-    @pl.loop(0, half // 8)
-    def _(tile):
-        at = pl.ds(pl.multiple_of(tile * 8, 8), 8)
-        swapped = jnp.logical_and(row_index == 0, tile == 0)
-        for index, lanes in enumerate(tiles):
-            values = []
-            for y in range(length_y):
-                own = jnp.where(swapped, own_ref[0, y, half : half + 1, lanes], own_ref[0, y, at, lanes])
-                factor = own + other_ref[0, y, at, lanes]
-                values.append((factor * fk_ref[y, 0, at, lanes], factor * fk_ref[y, 1, at, lanes]))
-            values = fourier(values, 1, wanted)
-            for n, y in enumerate(wanted):
-                rows = pl.ds(pl.multiple_of(n * half + tile * 8, 8), 8)
-                u_ref[rows, index * 128 : index * 128 + 128] = values[y][0]
-                u_ref[rows, length_x + index * 128 : length_x + index * 128 + 128] = values[y][1]
+    def weigh(other_ref):
+        @pl.loop(0, half // 8)
+        def _(tile):
+            at = pl.ds(pl.multiple_of(tile * 8, 8), 8)
+            swapped = jnp.logical_and(row_index == 0, tile == 0)
+            for index, lanes in enumerate(tiles):
+                values = []
+                for y in range(length_y):
+                    own = jnp.where(swapped, own_ref[0, y, half : half + 1, lanes], own_ref[0, y, at, lanes])
+                    factor = own + other_ref[0, y, at, lanes]
+                    values.append((factor * fk_ref[y, 0, at, lanes], factor * fk_ref[y, 1, at, lanes]))
+                values = fourier(values, 1, wanted)
+                for n, y in enumerate(wanted):
+                    rows = pl.ds(pl.multiple_of(n * half + tile * 8, 8), 8)
+                    u_ref[rows, index * 128 : index * 128 + 128] = values[y][0]
+                    u_ref[rows, length_x + index * 128 : length_x + index * 128 + 128] = values[y][1]
+
+    if len(others) == 1:
+        weigh(others[0])
+    else:
+        for other_ref, (start, end) in zip(others, pieces):
+            pl.when(jnp.logical_and(step >= start, step < end))(functools.partial(weigh, other_ref))
 
     @pl.loop(0, count_y * half // 64)
     def _(part):
@@ -330,7 +351,7 @@
     for part in range(2 * length_x // 256):
         cols = slice(part * 256, part * 256 + 256)
         result = dot_three(u_high_ref[...], u_low_ref[...], high_ref[:, cols], low_ref[:, cols])
-        edges = [edge_out_ref[pl.ds(n * first_ref.shape[1] + step, 1), cols] for n in range(count_y)]
+        edges = [edge_out_ref[pl.ds(n * first_ref.shape[1] + step + first_term, 1), cols] for n in range(count_y)]
         for k in range(count):
             q = part * count + k
             inside = slice(k * lanes_out, (k + 1) * lanes_out)
@@ -341,22 +362,34 @@
                 out_ref[q, 0, n, 8:, :] = piece[n * half + 8 : (n + 1) * half]
 
 
-def spread(parts, first, own, other, blocks, group):
-    terms, length_y, _, length_x = own.shape
-    half = other.shape[2]
-    groups = len(parts)
-    count_y = length_y // groups
+def spread(parts, spans, me, first, own, others, blocks, group, chosen):
+    _, length_y, _, length_x = own.shape
+    half = own.shape[2] // 2
+    first_term, end_term = chosen
+    terms = end_term - first_term
+    count_y = length_y // spans[-1][1] * (group[1] - group[0])
     rows_x = length_x // blocks
     high, low = halves(inverse_x_table(blocks, length_x))
     high, low = jnp.asarray(high), jnp.asarray(low)
     rows = count_y * half
+    others = [each for each in others if each[0] < end_term and each[1] > first_term]
+
+    def piece_spec(start, end):
+        return pl.BlockSpec(
+            (1, length_y, half, length_x), lambda t: (jnp.clip(t + first_term - start, 0, end - start - 1), 0, 0, 0)
+        )
+
     return pl.pallas_call(
-        functools.partial(spread_kernel, groups=groups, group=group),
+        functools.partial(
+            spread_kernel, spans=spans, counts=[len(part) for part in parts], group=group, first_term=first_term,
+            pieces=[(start - first_term, end - first_term) for start, end, _ in others],
+        ),
         grid=(terms,),
-        in_specs=[whole(part.shape, 1) for part in parts] + [
+        in_specs=[whole(array.shape, 1) for part in parts for array in part] + [
+            pl.BlockSpec(memory_space=pltpu.SMEM),
             whole(first.shape, 1),
-            pl.BlockSpec((1, length_y, half + 8, length_x), lambda t: (t, 0, 0, 0)),
-            pl.BlockSpec((1, length_y, half, length_x), lambda t: (t, 0, 0, 0)),
+            pl.BlockSpec((1, length_y, half + 8, length_x), lambda t: (t + first_term, 0, 0, 0)),
+        ] + [piece_spec(start, end) for start, end, _ in others] + [
             whole(high.shape, 1),
             whole(low.shape, 1),
         ],
@@ -364,6 +397,7 @@
         out_shape=jax.ShapeDtypeStruct((blocks, terms, count_y, half, 2 * rows_x), F32),
         scratch_shapes=[
             pltpu.VMEM((length_y, 2, half, length_x), F32),
+            pltpu.VMEM((length_y, 8, length_x), F32),
             pltpu.VMEM((count_y, first.shape[1], 2 * length_x), F32),
             pltpu.VMEM((count_y * first.shape[1], 2 * length_x), F32),
             pltpu.VMEM((rows, 2 * length_x), F32),
@@ -373,44 +407,55 @@
         compiler_params=params(1),
         cost_estimate=cost(terms * 24 * rows * length_x * length_x, terms * 16 * rows * length_x),
         name="spread",
-    )(*parts, first, own, other, high, low)
-
-
-def gather_kernel(data_ref, factor_ref, high_ref, low_ref, out_ref):
-    blocks, terms, _, half, lanes = data_ref.shape
+    )(*[array for part in parts for array in part], me, first, own, *[array for _, _, array in others], high, low)
+
+
+def gather_kernel(*refs):
+    *data_refs, factor_ref, high_ref, low_ref, out_ref = refs
+    blocks, _, _, half, lanes = data_refs[0].shape
     rows = lanes // 2
     parts = []
-    for t in range(terms):
-        turned = data_ref[:, t, 0].reshape(blocks * half, lanes).T
-        parts.append(jnp.concatenate([turned[:rows], turned[rows:]], axis=1))
+    for data_ref in data_refs:
+        for t in range(data_ref.shape[1]):
+            turned = data_ref[:, t, 0].reshape(blocks * half, lanes).T
+            parts.append(jnp.concatenate([turned[:rows], turned[rows:]], axis=1))
     high, low = split(jnp.concatenate(parts, axis=0))
     fields = dot_three(high, low, high_ref[...], low_ref[...])
     total = factor_ref[0, 0] * fields[:rows]
-    for t in range(1, terms):
+    for t in range(1, len(parts)):
         total = total + factor_ref[t, 0] * fields[t * rows : (t + 1) * rows]
     out_ref[0] = total
 
 
-def gather(data, factor, scale, width, groups, group):
-    blocks, terms, count_y, half, lanes = data.shape
-    rows, length_z = factor.shape[2], factor.shape[3]
-    wide = width // groups
+def gather(chunks, factor, scale, width, group):
+    blocks, _, _, half, lanes = chunks[0].shape
+    terms, length_y, rows, length_z = factor.shape
+    wide = group[1] - group[0]
+    count_y = length_y // width * wide
+
+    def row(n):
+        return n // wide * width + group[0] + n % wide
+
+    def chunk_spec(shape):
+        full = shape[2] == length_y
+        return pl.BlockSpec((blocks, shape[1], 1, half, lanes), lambda n: (0, 0, row(n) if full else n, 0, 0))
     high, low = halves(inverse_z_table(blocks, length_z, scale))
     return pl.pallas_call(
         gather_kernel,
         grid=(count_y,),
         in_specs=[
-            pl.BlockSpec((blocks, terms, 1, half, lanes), lambda n: (0, 0, n, 0, 0)),
-            pl.BlockSpec((terms, 1, rows, length_z), lambda n: (0, n // wide * width + group * wide + n % wide, 0, 0)),
+            chunk_spec(chunk.shape) for chunk in chunks
+        ] + [
+            pl.BlockSpec((terms, 1, rows, length_z), lambda n: (0, row(n), 0, 0)),
             whole(high.shape, 1),
             whole(low.shape, 1),
         ],
         out_specs=pl.BlockSpec((1, rows, length_z), lambda n: (n, 0, 0)),
         out_shape=jax.ShapeDtypeStruct((count_y, rows, length_z), F32),
         compiler_params=params(1),
-        cost_estimate=cost(6 * terms * count_y * rows * length_z * length_z, 8 * data.size),
+        cost_estimate=cost(6 * terms * count_y * rows * length_z * length_z, 8 * terms * count_y * rows * length_z),
         name="gather_z",
-    )(data, factor, jnp.asarray(high), jnp.asarray(low))
+    )(*chunks, factor, jnp.asarray(high), jnp.asarray(low))
 
 
 def mirror_kernel(in_ref, table_ref, out_ref, turned_ref):
@@ -427,22 +472,23 @@
             out_ref[0, y, s : s + 1, :] = turned_ref[source, row : row + 1, :]
 
 
-def mirror(multiplier):
-    terms, length_y, width, length_x = multiplier.shape
+def mirror(multiplier, start, end):
+    _, length_y, width, length_x = multiplier.shape
     half = width // 2
+    terms = end - start
     table = mirror_table(length_x)
     return pl.pallas_call(
         mirror_kernel,
         grid=(terms,),
         in_specs=[
-            pl.BlockSpec((1, length_y, half, length_x), lambda t: (t, 0, 1, 0)),
+            pl.BlockSpec((1, length_y, half, length_x), lambda t: (t + start, 0, 1, 0)),
             whole(table.shape, 1),
         ],
         out_specs=pl.BlockSpec((1, length_y, half, length_x), lambda t: (t, 0, 0, 0)),
         out_shape=jax.ShapeDtypeStruct((terms, length_y, half, length_x), F32),
         scratch_shapes=[pltpu.VMEM((length_y, half, length_x), F32)],
         compiler_params=params(1),
-        cost_estimate=cost(6 * terms * length_y * half * length_x * length_x, 4 * multiplier.size),
+        cost_estimate=cost(6 * terms * length_y * half * length_x * length_x, 8 * terms * length_y * half * length_x),
         name="mirror",
     )(multiplier, jnp.asarray(table))
 
@@ -471,6 +517,72 @@
     deep = jnp.pad(heat, ((0, 0), (0, 0), (1, 1)))
     near = near + deep[:, :, 2:] + deep[:, :, :-2]
     return heat + DIFFUSION * (near - 6.0 * heat) - perfuse * heat
+
+
+def update_kernel(fresh_ref, old_ref, dose_ref, heat_ref, absorb_ref, pressure_ref, source_ref, out_ref):
+    field = fresh_ref[...] - old_ref[...]
+    source = absorb_ref[...] * (dose_ref[...] + field * field)
+    pressure_ref[...] = field
+    source_ref[...] = source
+    out_ref[...] = heat_ref[...] + source
+
+
+def update(fresh, old, dose, heat, absorb):
+    return pl.pallas_call(
+        update_kernel,
+        out_shape=[jax.ShapeDtypeStruct(fresh.shape, F32)] * 3,
+        compiler_params=params(),
+        cost_estimate=cost(5 * fresh.size, 32 * fresh.size),
+        name="update",
+    )(fresh, old, dose, heat, absorb)
+
+
+def warm_kernel(*refs, groups, turned):
+    heat_refs, source_refs, low_refs, high_refs = [refs[k * groups : (k + 1) * groups] for k in range(4)]
+    below_ref, above_ref, perfuse_ref, out_ref = refs[4 * groups :]
+    rows, length_z = below_ref.shape[1:]
+    planes, sources, lows, highs = [], [], [], []
+    for heat_ref, source_ref, low_ref, high_ref in zip(heat_refs, source_refs, low_refs, high_refs):
+        for w in range(heat_ref.shape[0]):
+            planes.append(heat_ref[w])
+            sources.append(source_ref[w])
+            lows.append(low_ref[w])
+            highs.append(high_ref[w])
+    row = lax.broadcasted_iota(jnp.int32, (rows, length_z), 0)
+    lane = lax.broadcasted_iota(jnp.int32, (rows, length_z), 1)
+    for w, heat in enumerate(planes):
+        near = jnp.where(row == 0, lows[w], pltpu.roll(heat, 1, 0))
+        near = near + jnp.where(row == rows - 1, highs[w], pltpu.roll(heat, rows - 1, 0))
+        near = near + (planes[w - 1] if w else below_ref[0])
+        near = near + (planes[w + 1] if w + 1 < len(planes) else above_ref[0])
+        near = near + jnp.where(lane == 0, 0.0, pltpu.roll(heat, 1, 1))
+        near = near + jnp.where(lane == length_z - 1, 0.0, pltpu.roll(heat, length_z - 1, 1))
+        fresh = heat + DIFFUSION * (near - 6.0 * heat) - perfuse_ref[w] * heat + sources[w]
+        if turned:
+            out_ref[:, w, :] = fresh
+        else:
+            out_ref[w] = fresh
+
+
+def halo(heat, lowest):
+    (_, low, high), = padded_by_one(heat, (("pencil", 1),))
+    if not lowest:
+        return [low, high]
+    backward = [(i + 1, i) for i in range(lax.axis_size("term") - 1)]
+    return [low, high, lax.ppermute(heat[:1], "term", backward)]
+
+
+def warm(heats, sources, sides, perfuse, turned):
+    width, rows, length_z = perfuse.shape
+    above = sides[0][2]
+    below = lax.ppermute(heats[-1][-1:], "term", [(i, i + 1) for i in range(lax.axis_size("term") - 1)])
+    return pl.pallas_call(
+        functools.partial(warm_kernel, groups=len(heats), turned=turned),
+        out_shape=jax.ShapeDtypeStruct((rows, width, length_z) if turned else perfuse.shape, F32),
+        compiler_params=params(),
+        cost_estimate=cost(16 * perfuse.size, 16 * perfuse.size),
+        name="warm",
+    )(*heats, *sources, *[side[0] for side in sides], *[side[1] for side in sides], below, above, perfuse)
 
 
 def on_device(
@@ -492,38 +604,106 @@
     brick_start = lax.axis_index("term") * width
     scale = 2.0 / (length_x * length_y * length_z)
 
-    groups = 2 if width % 4 == 0 else 1
-    wide = width // groups
+    cut = width // 2 if width >= 4 else width
+    spans = [(0, cut), (cut, width)] if cut < width else [(0, width)]
 
     def to_brick(values):
-        brick = jnp.transpose(lax.dynamic_slice_in_dim(values, brick_start, width, 1), (1, 0, 2))
-        return [brick[g * wide : (g + 1) * wide] for g in range(groups)]
-
-    def rows_to_columns(brick):
-        return lax.all_to_all(forward_z(brick, blocks), "pencil", 0, 0, tiled=True)
-
-    current = to_brick(present_acoustic)
-    sent = [rows_to_columns(part) for part in current]
-    mirrored = mirror(spectral_multiplier)
-    *sent, mirrored = lax.optimization_barrier((*sent, mirrored))
-    other = lax.ppermute(mirrored, "pencil", [(p, blocks - 1 - p) for p in range(blocks)])
+        return jnp.transpose(lax.dynamic_slice_in_dim(values, brick_start, width, 1), (1, 0, 2))
+
+    def cut_up(brick):
+        return [brick[start:end] for start, end in spans]
+
+    def exchange(values):
+        return lax.all_to_all(values, "pencil", 0, 0, tiled=True)
+
     lowest = spectral_multiplier[:, :, 0, :]
     lowest = lowest + lax.ppermute(
         flip(flip(lowest, 1), 2), "pencil", [(p, blocks - p) for p in range(1, blocks) if 2 * p != blocks]
     )
     lowest = jnp.transpose(lowest, (1, 0, 2))
     lowest = jnp.pad(lowest, ((0, 0), (0, -terms % 8), (0, 0)))
+    opposite = [(p, blocks - 1 - p) for p in range(blocks)]
+    middle = terms // 2
+    sent = exchange(forward_z([to_brick(present_acoustic)], blocks)[0])
+    others = []
+    sent, lowest = lax.optimization_barrier((sent, lowest))
+    before = sent
+    for start, end in ((0, middle), (middle, terms)):
+        if end > start:
+            before, mirrored = lax.optimization_barrier((before, mirror(spectral_multiplier, start, end)))
+            if not others:
+                sent = before
+            before = lax.ppermute(mirrored, "pencil", opposite)
+            others.append((start, end, before))
+    me = lax.axis_index("term").reshape(1).astype(jnp.int32)
     factor = jnp.transpose(location_factor, (0, 2, 1, 3))
-
-    def doubled(sent):
-        parts = [lax.all_gather(forward_x(each, wide, half, rows), "term", axis=0, tiled=False) for each in sent]
-        bricks = []
-        for g in range(groups):
-            restored = spread(parts, lowest, spectral_multiplier, other, blocks, g)
-            restored = lax.all_to_all(restored, "pencil", 0, 0, tiled=True)
-            partial = gather(restored, factor, scale, width, groups, g)
-            bricks.append(lax.psum_scatter(partial, "term", scatter_dimension=0, tiled=True))
+    last, factor = lax.optimization_barrier((others[0][2], factor))
+    others[0] = (*others[0][:2], last)
+
+    def gathered(part):
+        return [part] + [
+            lax.ppermute(part, "term", [(i, (i - d) % term_count) for i in range(term_count)])
+            for d in range(1, term_count)
+        ]
+
+    def spread_from(parts, sent_spans, group, chosen):
+        out = spread(parts, sent_spans, me, lowest, spectral_multiplier, others, blocks, group, chosen)
+        flat, tree = jax.tree.flatten(parts)
+        out, *flat = lax.optimization_barrier((out, *flat))
+        return out, jax.tree.unflatten(tree, flat)
+
+    def summed(chunks, group):
+        partial = gather(chunks, factor, scale, width, group)
+        return lax.psum_scatter(partial, "term", scatter_dimension=0, tiled=True)
+
+    def doubled_first(part, tied):
+        parts = [[lax.all_gather(part, "term", axis=0, tiled=False)]]
+        shared, chunks, bricks = [], {}, []
+        if middle:
+            out, parts = spread_from(parts, [(0, width)], (0, width), (0, middle))
+            out, last = lax.optimization_barrier((out, others[-1][2]))
+            others[-1] = (*others[-1][:2], last)
+            shared = [exchange(out)]
+        before = shared
+        for index, group in enumerate(spans):
+            out, parts = spread_from(parts, [(0, width)], group, (middle, terms))
+            out, *before = lax.optimization_barrier((out, *before))
+            if index == 0:
+                shared = before
+            out = exchange(out)
+            before = [out]
+            if index == 0:
+                out, *tied = lax.optimization_barrier((out, *tied))
+            bricks.append(summed(shared + [out], group))
+        return bricks, tied
+
+    def doubled(parts):
+        bricks, before = [], []
+        for group in spans:
+            out, parts = spread_from(parts, spans, group, (0, terms))
+            out, *before = lax.optimization_barrier((out, *before))
+            if before:
+                chunks[0] = before[0]
+                bricks.append(summed(chunks, spans[0]))
+            chunks = [exchange(out)]
+            before = list(chunks)
+        bricks.append(summed(chunks, spans[-1]))
         return bricks
+
+    def forward(bricks):
+        parts, states, before = [], [], []
+        for (start, end), (fresh, *older) in zip(spans, bricks):
+            fresh, *before = lax.optimization_barrier((fresh, *before))
+            if before:
+                parts.append(gathered(before[0]))
+            sent, *state = forward_z([fresh, *older], blocks)
+            sent = exchange(sent)
+            if parts:
+                sent, *parts[-1] = lax.optimization_barrier((sent, *parts[-1]))
+            before = [forward_x(sent, end - start, half, rows)]
+            states.append(state)
+        parts.append(gathered(before[0]))
+        return parts, states
 
     kinds = jnp.transpose(medium_kinds, (1, 0, 2))
     absorb, perfuse = [
@@ -536,21 +716,31 @@
     ]
     heat = heat_step(jnp.transpose(thermal_increase, (1, 0, 2)), perfuse)
 
-    previous = to_brick(prior_acoustic)
-    dose = [jnp.zeros(part.shape, F32) for part in current]
-    for turn in range(WAVE_STEPS):
-        if turn:
-            sent = [rows_to_columns(part) for part in current]
-        advanced = [fresh - old for fresh, old in zip(doubled(sent), previous)]
-        dose = [total + fresh * fresh for total, fresh in zip(dose, advanced)]
-        previous, current = current, advanced
-    current = jnp.concatenate(current, axis=0)
-    dose = jnp.concatenate(dose, axis=0)
-    source = absorb * dose
-    heat = heat + source
-    for _ in range(HEAT_STEPS - 1):
-        heat = heat_step(heat, perfuse) + source
-    return jnp.transpose(current, (1, 0, 2)), jnp.transpose(heat, (1, 0, 2))
+    previous = cut_up(to_brick(prior_acoustic))
+    current = cut_up(to_brick(present_acoustic))
+    dose = []
+    doubles, (heat, absorb, perfuse) = doubled_first(forward_x(sent, width, half, rows), (heat, absorb, perfuse))
+    for _ in range(WAVE_STEPS - 1):
+        parts, states = forward(list(zip(doubles, previous, *dose)))
+        previous, current = current, [field for field, _ in states]
+        dose = [[total for _, total in states]]
+        doubles = doubled(parts)
+    dose = dose[0] if dose else [jnp.zeros(each.shape, F32) for each in current]
+    updated, sides, ahead = [], [], []
+    for fresh, *rest in zip(doubles, previous, dose, cut_up(heat), cut_up(absorb)):
+        fresh, *ahead = lax.optimization_barrier((fresh, *ahead))
+        if ahead:
+            sides.append(ahead)
+        updated.append(update(fresh, *rest))
+        ahead = halo(updated[-1][2], not sides)
+    sides.append(ahead)
+    pressure = jnp.concatenate([each[0] for each in updated], axis=0)
+    sources = [each[1] for each in updated]
+    heats = [each[2] for each in updated]
+    for _ in range(HEAT_STEPS - 2):
+        heats = cut_up(warm(heats, sources, sides, perfuse, False))
+        sides = [halo(each, index == 0) for index, each in enumerate(heats)]
+    return jnp.transpose(pressure, (1, 0, 2)), warm(heats, sources, sides, perfuse, True)
 
 
 def solution(mesh):

time: 567 us -> 530 us (0.935)
  waiting for transfers between devices: 291 us -> 225 us
  Pallas kernels: 140 us -> 151 us
  starting transfers between devices: 60.4 us -> 70.7 us
  local copies, waits for them, and re-layouts: 23.4 us -> 32.4 us
    ppermute x1 -> x10, waiting for transfers between devices: 0.01 us -> 95.6 us  [the longest x2 59.5 us: on_device(): before = lax.ppermute(mirrored, 'pencil', opposite)]
    ppermute x1, waiting for transfers between devices: 82 us -> 0.01 us  [on_device(): lax.ppermute(flip(flip(lowest, 1), 2), 'pencil', [(p, blocks - p) for p i...]
    all_gather x4 -> x1, waiting for transfers between devices: 42 us -> 0.01 us  [doubled_first(): parts = [[lax.all_gather(part, 'term', axis=0, tiled=False)]]]
    all_to_all x6, waiting for transfers between devices: 127 us -> 110 us  [exchange(): return lax.all_to_all(values, 'pencil', 0, 0, tiled=True)]
    reduce_scatter x4, waiting for transfers between devices: 36.8 us -> 19.4 us  [summed(): return lax.psum_scatter(partial, 'term', scatter_dimension=0, tiled=True)]
    pallas_call x12 -> x15, Pallas kernels: 120 us -> 132 us  [the longest x5 77.2 us: spread(): pl.pallas_call(functools.partial(spread_kernel, spans=spans, counts=[len(...]
    ppermute x1 -> x10, starting transfers between devices: 1.51 us -> 12.3 us  [the longest x6 6.6 us: gathered(): lax.ppermute(part, 'term', [(i, (i - d) % term_count) for i in range(term...]
    add x2 -> x0, other arithmetic: 6.82 us -> none  [the longest x1 5.62 us: on_device(): heat = heat + source]
  transfers between devices with their start and end apart: 24 -> 30, of which waited for: 11 -> 15; matrix products, arithmetic and copies ran while one was open for 4% -> 6% of each run, Pallas kernels for 17% -> 23%
where the time goes in v3:
time: 530 us; the launch traced here: 527 us
  waiting for transfers between devices  225 us (42%)
  Pallas kernels  151 us (28%)
  starting transfers between devices  70.7 us (13%)
  local copies, waits for them, and re-layouts  32.4 us (6%)
  blocking collectives  22.7 us (4%)
  between operations  14.2 us (3%)
  other arithmetic  10.3 us (2%)
    all_to_all x6, waiting for transfers between devices, exchange(): return lax.all_to_all(values, 'pencil', 0, 0, tiled=True)  110 us
    pallas_call x5, Pallas kernels, spread(): pl.pallas_call(functools.partial(spread_kernel, spans=spans, counts=[len(...  77.2 us
    ppermute x2, waiting for transfers between devices, on_device(): before = lax.ppermute(mirrored, 'pencil', opposite)  59.5 us
    pallas_call x4, Pallas kernels, gather(): pl.pallas_call(gather_kernel, grid=(count_y,), in_specs=[chunk_spec(chunk...  39.1 us
    ppermute x6, waiting for transfers between devices, gathered(): lax.ppermute(part, 'term', [(i, (i - d) % term_count) for i in range(term...  33.3 us
    all_to_all x6, starting transfers between devices, exchange(): return lax.all_to_all(values, 'pencil', 0, 0, tiled=True)  30.5 us
    all_to_all x2, blocking collectives, exchange(): return lax.all_to_all(values, 'pencil', 0, 0, tiled=True)  22.7 us
    unnamed x48, local copies, waits for them, and re-layouts  21 us
  transfers between devices with their start and end apart: 30, of which 15 were waited for; matrix products, arithmetic and copies ran while one was open for 6% of the time, Pallas kernels for 23%

profile of v3, /device:TPU:11, one launch (start us, length us, event | category | flops | bytes accessed | tf_op | source)
XLA Modules:
  0.0 527.0 jit_solution(13847167874411458549)
XLA Ops:
  9.9 3.0 forward_z.3
  13.0 4.6 all-to-all-start
  19.9 3.1 collective-permute-start
  23.0 4.8 mirror.2
  29.5 3.6 forward_x.3
  33.2 4.8 mirror.3
  38.0 38.9 %collective-permute-done.1.refs_4_.refs_11_ = f32[2,16,32,512]{3,2,1,0:T(8,128)} collective-permute-done((f32[2,16,32,512]{3,2,1,0:T(8,128)}, f32[2,16,32,512]{3,2,1,0:T(8,128)}, u32[]{:S(2)}, u32[]{:S(2)}) %collective-permute-start.1) | collective-permute-done | bytes 2097184 | tf_op jit(solution)/shard_map/ppermute | solution.py:636
  76.9 11.6 %copy.69 = f32[4,64,16,512]{3,1,2,0:T(8,128)} copy(f32[4,64,16,512]{3,2,1,0:T(8,128)} %param.47) | data formatting | bytes 16777216 | tf_op args[2]
  88.5 16.3 %spread.5 = f32[8,2,16,32,128]{4,3,2,1,0:T(8,128)} custom-call(f32[4,264,512]{2,1,0:T(8,128)} %bitcast.45, s32[1]{0:T(128)} %bitcast.4.refs_1_.refs_8_, f32[16,8,512]{2,1,0:T(8,128)} %pad.8.refs_2_.refs_9_, f32[4,16,64,512]{3,2,1,0:T(8,128)} %refs_10_.3, f32[2,16,32,512]{3,2,1,0:T(8,128)} %collective-permute-done.1.refs_4_.refs_11_, ...), custom_call_target="tpu_custom_call" | custom-call | flops 6442450944 | bytes 8388608 | tf_op jit(solution)/shard_map/spread/pallas_call | solution.py:382
  104.8 20.6 %collective-permute-done.2.refs_4_.refs_12_ = f32[2,16,32,512]{3,2,1,0:T(8,128)S(1)} collective-permute-done((f32[2,16,32,512]{3,2,1,0:T(8,128)}, f32[2,16,32,512]{3,2,1,0:T(8,128)S(1)}, u32[]{:S(2)}, u32[]{:S(2)}) %collective-permute-start.2) | collective-permute-done | bytes 2097184 | tf_op jit(solution)/shard_map/ppermute | solution.py:636
  126.7 4.7 all-to-all-start.1
  132.6 3.2 collective-permute-start.6
  135.8 3.3 collective-permute-start.5
  139.1 12.3 %spread.6 = f32[8,2,8,32,128]{4,3,2,1,0:T(8,128)} custom-call(f32[4,264,512]{2,1,0:T(8,128)} %bitcast.46, s32[1]{0:T(128)} %bitcast.4.refs_1_.refs_8_, f32[16,8,512]{2,1,0:T(8,128)} %pad.8.refs_2_.refs_9_, f32[4,16,64,512]{3,2,1,0:T(8,128)} %refs_10_.3, f32[2,16,32,512]{3,2,1,0:T(8,128)} %copy-done.1, bf16[1024,1024]{1,0:T(8,128)(2,1)} %constant.49.clone.refs_5_.refs_13_, ...), custom_call_target="tpu_custom_call" | custom-call | flops 3221225472 | bytes 4194304 | tf_op jit(solution)/shard_map/spread/pallas_call | solution.py:382
  151.4 27.2 %all-to-all-done.1.refs_0_ = f32[8,2,16,32,128]{4,3,2,1,0:T(8,128)} async-done(((f32[8,2,16,32,128]{4,3,2,1,0:T(8,128)}), f32[8,2,16,32,128]{4,3,2,1,0:T(8,128)}, u32[]{:S(2)}, u32[]{:S(2)}) %all-to-all-start.1) | async-done | bytes 4194336 | tf_op jit(solution)/shard_map/all_to_all | solution.py:617
  178.5 5.1 all-to-all-start.2
  185.9 3.2 collective-permute-start.3
  189.9 2.9 select_bitcast_fusion.1
  192.9 2.8 select_bitcast_fusion
  195.7 3.2 fusion.5
  198.8 12.3 %spread.7 = f32[8,2,8,32,128]{4,3,2,1,0:T(8,128)} custom-call(f32[4,264,512]{2,1,0:T(8,128)} %bitcast.47, s32[1]{0:T(128)} %bitcast.4.refs_1_.refs_8_, f32[16,8,512]{2,1,0:T(8,128)} %pad.8.refs_2_.refs_9_, f32[4,16,64,512]{3,2,1,0:T(8,128)} %refs_10_.3, f32[2,16,32,512]{3,2,1,0:T(8,128)} %copy-done.1, bf16[1024,1024]{1,0:T(8,128)(2,1)} %constant.49.clone.refs_5_.refs_13_, ...), custom_call_target="tpu_custom_call" | custom-call | flops 3221225472 | bytes 4194304 | tf_op jit(solution)/shard_map/spread/pallas_call | solution.py:382
  212.5 5.0 all-to-all-start.3
  217.5 9.8 %gather_z.5 = f32[8,64,512]{2,1,0:T(8,128)} custom-call(f32[8,2,16,32,128]{4,3,2,1,0:T(8,128)} %all-to-all-done.1.refs_0_, f32[8,2,8,32,128]{4,3,2,1,0:T(8,128)} %copy-done, f32[4,16,64,512]{3,2,1,0:T(8,128)} %bitcast.36, bf16[512,512]{1,0:T(8,128)(2,1)} %constant.51.clone.refs_3_.refs_2_, bf16[512,512]{1,0:T(8,128)(2,1)} %constant.52.clone.refs_4_.refs_3_), custom_call_target="tpu_custom_call" | custom-call | flops 3221225472 | bytes 8388608 | tf_op jit(solution)/shard_map/gather_z/pallas_call | solution.py:443
  227.4 15.3 %all-to-all-done.3.refs_1_ = f32[8,2,8,32,128]{4,3,2,1,0:T(8,128)} async-done(((f32[8,2,8,32,128]{4,3,2,1,0:T(8,128)}), f32[8,2,8,32,128]{4,3,2,1,0:T(8,128)}, u32[]{:S(2)}, u32[]{:S(2)}) %all-to-all-start.3) | async-done | bytes 2097184 | tf_op jit(solution)/shard_map/all_to_all | solution.py:617
  242.6 9.8 %gather_z.4 = f32[8,64,512]{2,1,0:T(8,128)} custom-call(f32[8,2,16,32,128]{4,3,2,1,0:T(8,128)} %all-to-all-done.1.refs_0_, f32[8,2,8,32,128]{4,3,2,1,0:T(8,128)} %all-to-all-done.3.refs_1_, f32[4,16,64,512]{3,2,1,0:T(8,128)} %bitcast.37, bf16[512,512]{1,0:T(8,128)(2,1)} %constant.51.clone.refs_3_.refs_2_, bf16[512,512]{1,0:T(8,128)(2,1)} %constant.52.clone.refs_4_.refs_3_), custom_call_target="tpu_custom_call" | custom-call | flops 3221225472 | bytes 8388608 | tf_op jit(solution)/shard_map/gather_z/pallas_call | solution.py:443
  256.1 11.3 %all_to_all.40.data_ref = f32[8,72,128]{2,1,0:T(8,128)} all-to-all(f32[8,72,128]{2,1,0:T(8,128)} %get-tuple-element.74), channel_id=1, replica_groups=mesh['term'=4,'pencil'=8] {'pencil'}, dimensions={0} | all-to-all | bytes 589824 | tf_op jit(solution)/shard_map/all_to_all | solution.py:617
  267.4 3.1 forward_x.4.refs_0_
  270.5 10.1 %reduce-scatter.5.cloned.1.call-done.refs_0_ = f32[2,64,512]{2,1,0:T(8,128)} async-done(((f32[8,64,512]{2,1,0:T(8,128)}), f32[2,64,512]{2,1,0:T(8,128)}) %reduce-scatter.5.cloned.1.call-update) | async-done | bytes 262160 | tf_op jit(solution)/shard_map/reduce_scatter | solution.py:657
  287.4 11.4 %all_to_all.41.data_ref = f32[8,72,128]{2,1,0:T(8,128)} all-to-all(f32[8,72,128]{2,1,0:T(8,128)} %get-tuple-element.76), channel_id=1, replica_groups=mesh['term'=4,'pencil'=8] {'pencil'}, dimensions={0} | all-to-all | bytes 589824 | tf_op jit(solution)/shard_map/all_to_all | solution.py:617
  298.8 7.3 %collective-permute-done.8.refs_2_ = f32[136,512]{1,0:T(8,128)S(1)} collective-permute-done((f32[136,512]{1,0:T(8,128)}, f32[136,512]{1,0:T(8,128)S(1)}, u32[]{:S(2)}, u32[]{:S(2)}) %collective-permute-start.8) | collective-permute-done | bytes 278560 | tf_op jit(solution)/shard_map/ppermute | solution.py:645
  308.2 3.2 forward_x.5.refs_4_
  313.9 4.5 collective-permute-done.12.refs_7_
  318.4 16.1 %collective-permute-done.11.refs_6_ = f32[136,512]{1,0:T(8,128)S(1)} collective-permute-done((f32[136,512]{1,0:T(8,128)}, f32[136,512]{1,0:T(8,128)S(1)}, u32[]{:S(2)}, u32[]{:S(2)}) %collective-permute-start.11) | collective-permute-done | bytes 278560 | tf_op jit(solution)/shard_map/ppermute | solution.py:645
  334.5 3.2 collective-permute-done.10.refs_5_
  338.4 18.1 %spread.8 = f32[8,4,8,32,128]{4,3,2,1,0:T(8,128)} custom-call(f32[136,512]{1,0:T(8,128)} %forward_x.4.refs_0_, f32[136,512]{1,0:T(8,128)} %copy-done.16, f32[136,512]{1,0:T(8,128)} %copy-done.15, f32[136,512]{1,0:T(8,128)} %copy-done.14, f32[136,512]{1,0:T(8,128)} %forward_x.5.refs_4_, f32[136,512]{1,0:T(8,128)} %copy-done.19, f32[136,512]{1,0:T(8,128)} %copy-done.18, ...), custom_call_target="tpu_custom_call" | custom-call | flops 6442450944 | bytes 8388608 | tf_op jit(solution)/shard_map/spread/pallas_call | solution.py:382
  356.5 5.2 all-to-all-start.6
  361.7 18.2 %spread.9 = f32[8,4,8,32,128]{4,3,2,1,0:T(8,128)} custom-call(f32[136,512]{1,0:T(8,128)} %forward_x.4.refs_0_, f32[136,512]{1,0:T(8,128)} %copy-done.16, f32[136,512]{1,0:T(8,128)} %copy-done.15, f32[136,512]{1,0:T(8,128)} %copy-done.14, f32[136,512]{1,0:T(8,128)} %forward_x.5.refs_4_, f32[136,512]{1,0:T(8,128)} %copy-done.19, f32[136,512]{1,0:T(8,128)} %copy-done.18, ...), custom_call_target="tpu_custom_call" | custom-call | flops 6442450944 | bytes 8388608 | tf_op jit(solution)/shard_map/spread/pallas_call | solution.py:382
  379.9 29.4 %all-to-all-done.6.refs_0_ = f32[8,4,8,32,128]{4,3,2,1,0:T(8,128)} async-done(((f32[8,4,8,32,128]{4,3,2,1,0:T(8,128)}), f32[8,4,8,32,128]{4,3,2,1,0:T(8,128)}, u32[]{:S(2)}, u32[]{:S(2)}) %all-to-all-start.6) | async-done | bytes 4194336 | tf_op jit(solution)/shard_map/all_to_all | solution.py:617
  409.4 6.0 %all-to-all-start.7 = ((f32[8,4,8,32,128]{4,3,2,1,0:T(8,128)}), f32[8,4,8,32,128]{4,3,2,1,0:T(8,128)}, u32[]{:S(2)}, u32[]{:S(2)}) async-start(f32[8,4,8,32,128]{4,3,2,1,0:T(8,128)} %spread.9), calls=%async_computation.10 | async-start | bytes 8388608 | tf_op jit(solution)/shard_map/all_to_all | solution.py:617
  415.4 9.8 %gather_z.6 = f32[8,64,512]{2,1,0:T(8,128)} custom-call(f32[8,4,8,32,128]{4,3,2,1,0:T(8,128)} %all-to-all-done.6.refs_0_, f32[4,16,64,512]{3,2,1,0:T(8,128)} %bitcast.38, bf16[512,512]{1,0:T(8,128)(2,1)} %constant.51.clone.refs_3_.refs_2_, bf16[512,512]{1,0:T(8,128)(2,1)} %constant.52.clone.refs_4_.refs_3_), custom_call_target="tpu_custom_call" | custom-call | flops 3221225472 | bytes 8388608 | tf_op jit(solution)/shard_map/gather_z/pallas_call | solution.py:443
  425.3 37.8 %all-to-all-done.7.refs_0_ = f32[8,4,8,32,128]{4,3,2,1,0:T(8,128)} async-done(((f32[8,4,8,32,128]{4,3,2,1,0:T(8,128)}), f32[8,4,8,32,128]{4,3,2,1,0:T(8,128)}, u32[]{:S(2)}, u32[]{:S(2)}) %all-to-all-start.7) | async-done | bytes 4194336 | tf_op jit(solution)/shard_map/all_to_all | solution.py:617
  463.0 9.7 %gather_z.7 = f32[8,64,512]{2,1,0:T(8,128)} custom-call(f32[8,4,8,32,128]{4,3,2,1,0:T(8,128)} %all-to-all-done.7.refs_0_, f32[4,16,64,512]{3,2,1,0:T(8,128)} %bitcast.39, bf16[512,512]{1,0:T(8,128)(2,1)} %constant.51.clone.refs_3_.refs_2_, bf16[512,512]{1,0:T(8,128)(2,1)} %constant.52.clone.refs_4_.refs_3_), custom_call_target="tpu_custom_call" | custom-call | flops 3221225472 | bytes 8388608 | tf_op jit(solution)/shard_map/gather_z/pallas_call | solution.py:443
  483.8 4.1 collective-permute-start.13
  488.7 2.8 collective-permute-done.15.refs_9_
  491.5 9.2 %reduce-scatter.11.cloned.1.call-done.fresh_ref = f32[2,64,512]{2,1,0:T(8,128)} async-done(((f32[8,64,512]{2,1,0:T(8,128)}), f32[2,64,512]{2,1,0:T(8,128)}) %reduce-scatter.11.cloned.1.call-update) | async-done | bytes 262160 | tf_op jit(solution)/shard_map/reduce_scatter | solution.py:657
  503.9 3.7 collective-permute-start.18
  508.4 2.8 collective-permute-start.17
  511.2 3.6 collective-permute-start.16
  (113 shorter events, 50.8 us)
Async XLA Ops:
  13.0 15.7 %all-to-all-start = ((f32[8,72,256]{2,1,0:T(8,128)}), f32[8,72,256]{2,1,0:T(8,128)S(1)}, u32[]{:S(2)}, u32[]{:S(2)}) async-start(f32[8,72,256]{2,1,0:T(8,128)} %forward_z.3), calls=%async_computation | async-start | bytes 1179648 | tf_op jit(solution)/shard_map/all_to_all | solution.py:617
  17.5 71.0 %all-gather.3.cloned.1.call-start = ((), (), s32[]{:S(2)}) async-start(), calls=%async_computation.16 | async-start | bytes 2703360 | tf_op jit(solution)/shard_map/all_gather | solution.py:660
  19.9 7.9 %collective-permute-start = (f32[4,16,512]{2,0,1:T(4,128)S(1)}, f32[4,16,512]{2,0,1:T(4,128)S(1)}, u32[]{:S(2)}, u32[]{:S(2)}) collective-permute-start(f32[4,16,512]{2,0,1:T(4,128)S(1)} %fusion.8), channel_id=1, source_target_pairs={{1,7},{2,6},{3,5},{5,3},{6,2},{7,1},{9,15},{10,14},{11,13},{13,11}... | collective-permute-start | bytes 393224 | tf_op jit(solution)/shard_map/ppermute | solution.py:620
  28.7 0.8 copy-start.3
  28.7 48.2 %collective-permute-start.1 = (f32[2,16,32,512]{3,2,1,0:T(8,128)}, f32[2,16,32,512]{3,2,1,0:T(8,128)}, u32[]{:S(2)}, u32[]{:S(2)}) collective-permute-start(f32[2,16,32,512]{3,2,1,0:T(8,128)} %mirror.2), channel_id=1, source_target_pairs={{0,7},{1,6},{2,5},{3,4},{4,3},{5,2},{6,1},{7,0},{8,15},{9,14},{10,... | collective-permute-start | bytes 6291464 | tf_op jit(solution)/shard_map/ppermute | solution.py:636
  76.9 48.5 %collective-permute-start.2 = (f32[2,16,32,512]{3,2,1,0:T(8,128)}, f32[2,16,32,512]{3,2,1,0:T(8,128)S(1)}, u32[]{:S(2)}, u32[]{:S(2)}) collective-permute-start(f32[2,16,32,512]{3,2,1,0:T(8,128)} %mirror.3), channel_id=1, source_target_pairs={{0,7},{1,6},{2,5},{3,4},{4,3},{5,2},{6,1},{7,0},{8,15},{9,14},{10,... | collective-permute-start | bytes 6291464 | tf_op jit(solution)/shard_map/ppermute | solution.py:636
  125.4 1.3 copy-start.1
  126.7 51.8 %all-to-all-start.1 = ((f32[8,2,16,32,128]{4,3,2,1,0:T(8,128)}), f32[8,2,16,32,128]{4,3,2,1,0:T(8,128)}, u32[]{:S(2)}, u32[]{:S(2)}) async-start(f32[8,2,16,32,128]{4,3,2,1,0:T(8,128)} %spread.5), calls=%async_computation.1 | async-start | bytes 8388608 | tf_op jit(solution)/shard_map/all_to_all | solution.py:617
  132.6 63.0 %collective-permute-start.6 = (f32[4,1,512]{2,1,0:T(1,128)S(1)}, f32[4,1,512]{2,1,0:T(1,128)S(1)}, u32[]{:S(2)}, u32[]{:S(2)}) collective-permute-start(f32[4,1,512]{2,1,0:T(1,128)S(1)} %get-tuple-element.125), channel_id=1, source_target_pairs={{1,0},{2,1},{3,2},{4,3},{5,4},{6,5},{7,6},{9,8},{10,9},{11,10},{12... | collective-permute-start | bytes 24584 | tf_op jit(solution)/shard_map/ppermute | solution.py:507
  135.8 59.8 %collective-permute-start.5 = (f32[4,1,512]{2,1,0:T(1,128)S(1)}, f32[4,1,512]{2,1,0:T(1,128)S(1)}, u32[]{:S(2)}, u32[]{:S(2)}) collective-permute-start(f32[4,1,512]{2,1,0:T(1,128)S(1)} %get-tuple-element.126), channel_id=1, source_target_pairs={{0,1},{1,2},{2,3},{3,4},{4,5},{5,6},{6,7},{8,9},{9,10},{10,11},{11... | collective-permute-start | bytes 24584 | tf_op jit(solution)/shard_map/ppermute | solution.py:506
  151.4 37.7 %copy-start.9 = (f32[3,2]{0,1:T(2,128)S(1)}, f32[3,2]{0,1:T(2,128)}, u32[]{:S(2)}) copy-start(f32[3,2]{0,1:T(2,128)} %param.50) | copy-start | bytes 76
  178.5 32.6 %all-to-all-start.2 = ((f32[8,2,8,32,128]{4,3,2,1,0:T(8,128)}), f32[8,2,8,32,128]{4,3,2,1,0:T(8,128)S(1)}, u32[]{:S(2)}, u32[]{:S(2)}) async-start(f32[8,2,8,32,128]{4,3,2,1,0:T(8,128)} %spread.6), calls=%async_computation.2 | async-start | bytes 4194304 | tf_op jit(solution)/shard_map/all_to_all | solution.py:617
  183.6 6.2 %copy-start.6 = (s32[64,4,512]{2,1,0:T(4,128)S(1)}, s32[64,4,512]{2,1,0:T(4,128)}, u32[]{:S(2)}) copy-start(s32[64,4,512]{2,1,0:T(4,128)} %param.49) | copy-start | bytes 1572868
  183.7 12.0 %collective-permute-start.4 = (f32[1,64,512]{2,1,0:T(8,128)S(1)}, f32[1,64,512]{2,1,0:T(8,128)S(1)}, u32[]{:S(2)}, u32[]{:S(2)}) collective-permute-start(f32[1,64,512]{2,1,0:T(8,128)S(1)} %get-tuple-element.129), channel_id=1, source_target_pairs={{8,0},{16,8},{24,16},{9,1},{17,9},{25,17},{10,2},{18,10},{26,18},{... | collective-permute-start | bytes 393224 | tf_op jit(solution)/shard_map/ppermute | solution.py:507
  185.9 9.8 %collective-permute-start.3 = (f32[1,64,512]{2,1,0:T(8,128)S(1)}, f32[1,64,512]{2,1,0:T(8,128)S(1)}, u32[]{:S(2)}, u32[]{:S(2)}) collective-permute-start(f32[1,64,512]{2,1,0:T(8,128)S(1)} %get-tuple-element.130), channel_id=1, source_target_pairs={{0,8},{8,16},{16,24},{1,9},{9,17},{17,25},{2,10},{10,18},{18,26},{... | collective-permute-start | bytes 393224 | tf_op jit(solution)/shard_map/ppermute | solution.py:506
  211.2 1.4 copy-start
  212.5 30.1 %all-to-all-start.3 = ((f32[8,2,8,32,128]{4,3,2,1,0:T(8,128)}), f32[8,2,8,32,128]{4,3,2,1,0:T(8,128)}, u32[]{:S(2)}, u32[]{:S(2)}) async-start(f32[8,2,8,32,128]{4,3,2,1,0:T(8,128)} %spread.7), calls=%async_computation.3 | async-start | bytes 4194304 | tf_op jit(solution)/shard_map/all_to_all | solution.py:617
  217.5 36.0 %reduce-scatter.7.cloned.1.call-start = ((), (), s32[]{:S(2)}) async-start(), calls=%async_computation.13 | async-start | bytes 1310720 | tf_op jit(solution)/shard_map/reduce_scatter | solution.py:657
  227.3 53.3 %reduce-scatter.5.cloned.1.call-start = ((), (), s32[]{:S(2)}) async-start(), calls=%async_computation.12 | async-start | bytes 1310720 | tf_op jit(solution)/shard_map/reduce_scatter | solution.py:657
  280.6 18.1 %collective-permute-start.9 = (f32[136,512]{1,0:T(8,128)}, f32[136,512]{1,0:T(8,128)S(1)}, u32[]{:S(2)}, u32[]{:S(2)}) collective-permute-start(f32[136,512]{1,0:T(8,128)} %forward_x.4.refs_0_), channel_id=1, source_target_pairs={{0,8},{8,16},{16,24},{24,0},{1,9},{9,17},{17,25},{25,1},{2,10},{10... | collective-permute-start | bytes 835592 | tf_op jit(solution)/shard_map/ppermute | solution.py:645
  282.5 23.6 %collective-permute-start.8 = (f32[136,512]{1,0:T(8,128)}, f32[136,512]{1,0:T(8,128)S(1)}, u32[]{:S(2)}, u32[]{:S(2)}) collective-permute-start(f32[136,512]{1,0:T(8,128)} %forward_x.4.refs_0_), channel_id=1, source_target_pairs={{0,16},{8,24},{16,0},{24,8},{1,17},{9,25},{17,1},{25,9},{2,18},{10... | collective-permute-start | bytes 835592 | tf_op jit(solution)/shard_map/ppermute | solution.py:645
  284.8 23.4 %collective-permute-start.7 = (f32[136,512]{1,0:T(8,128)}, f32[136,512]{1,0:T(8,128)S(1)}, u32[]{:S(2)}, u32[]{:S(2)}) collective-permute-start(f32[136,512]{1,0:T(8,128)} %forward_x.4.refs_0_), channel_id=1, source_target_pairs={{0,24},{8,0},{16,8},{24,16},{1,25},{9,1},{17,9},{25,17},{2,26},{10... | collective-permute-start | bytes 835592 | tf_op jit(solution)/shard_map/ppermute | solution.py:645
  298.8 38.9 %copy-start.14 = (f32[136,512]{1,0:T(8,128)}, f32[136,512]{1,0:T(8,128)S(1)}, u32[]{:S(2)}) copy-start(f32[136,512]{1,0:T(8,128)S(1)} %collective-permute-done.9.refs_3_) | copy-start | bytes 835588
  306.1 31.6 %copy-start.15 = (f32[136,512]{1,0:T(8,128)}, f32[136,512]{1,0:T(8,128)S(1)}, u32[]{:S(2)}) copy-start(f32[136,512]{1,0:T(8,128)S(1)} %collective-permute-done.8.refs_2_) | copy-start | bytes 835588
  308.2 29.4 %copy-start.16 = (f32[136,512]{1,0:T(8,128)}, f32[136,512]{1,0:T(8,128)S(1)}, u32[]{:S(2)}) copy-start(f32[136,512]{1,0:T(8,128)S(1)} %collective-permute-done.7.refs_1_) | copy-start | bytes 835588
  311.4 6.9 %collective-permute-start.12 = (f32[136,512]{1,0:T(8,128)}, f32[136,512]{1,0:T(8,128)S(1)}, u32[]{:S(2)}, u32[]{:S(2)}) collective-permute-start(f32[136,512]{1,0:T(8,128)} %forward_x.5.refs_4_), channel_id=1, source_target_pairs={{0,8},{8,16},{16,24},{24,0},{1,9},{9,17},{17,25},{25,1},{2,10},{10... | collective-permute-start | bytes 835592 | tf_op jit(solution)/shard_map/ppermute | solution.py:645
  311.4 23.0 %collective-permute-start.11 = (f32[136,512]{1,0:T(8,128)}, f32[136,512]{1,0:T(8,128)S(1)}, u32[]{:S(2)}, u32[]{:S(2)}) collective-permute-start(f32[136,512]{1,0:T(8,128)} %forward_x.5.refs_4_), channel_id=1, source_target_pairs={{0,16},{8,24},{16,0},{24,8},{1,17},{9,25},{17,1},{25,9},{2,18},{10... | collective-permute-start | bytes 835592 | tf_op jit(solution)/shard_map/ppermute | solution.py:645
  312.4 25.3 %collective-permute-start.10 = (f32[136,512]{1,0:T(8,128)}, f32[136,512]{1,0:T(8,128)S(1)}, u32[]{:S(2)}, u32[]{:S(2)}) collective-permute-start(f32[136,512]{1,0:T(8,128)} %forward_x.5.refs_4_), channel_id=1, source_target_pairs={{0,24},{8,0},{16,8},{24,16},{1,25},{9,1},{17,9},{25,17},{2,26},{10... | collective-permute-start | bytes 835592 | tf_op jit(solution)/shard_map/ppermute | solution.py:645
  318.4 19.3 %copy-start.17 = (f32[136,512]{1,0:T(8,128)}, f32[136,512]{1,0:T(8,128)S(1)}, u32[]{:S(2)}) copy-start(f32[136,512]{1,0:T(8,128)S(1)} %collective-permute-done.12.refs_7_) | copy-start | bytes 835588
  334.5 3.2 copy-start.18
  337.7 0.7 copy-start.19
  356.5 52.8 %all-to-all-start.6 = ((f32[8,4,8,32,128]{4,3,2,1,0:T(8,128)}), f32[8,4,8,32,128]{4,3,2,1,0:T(8,128)}, u32[]{:S(2)}, u32[]{:S(2)}) async-start(f32[8,4,8,32,128]{4,3,2,1,0:T(8,128)} %spread.8), calls=%async_computation.8 | async-start | bytes 8388608 | tf_op jit(solution)/shard_map/all_to_all | solution.py:617
  409.4 53.7 %all-to-all-start.7 = ((f32[8,4,8,32,128]{4,3,2,1,0:T(8,128)}), f32[8,4,8,32,128]{4,3,2,1,0:T(8,128)}, u32[]{:S(2)}, u32[]{:S(2)}) async-start(f32[8,4,8,32,128]{4,3,2,1,0:T(8,128)} %spread.9), calls=%async_computation.10 | async-start | bytes 8388608 | tf_op jit(solution)/shard_map/all_to_all | solution.py:617
  415.4 60.2 %reduce-scatter.9.cloned.1.call-start = ((), (), s32[]{:S(2)}) async-start(), calls=%async_computation.14 | async-start | bytes 1310720 | tf_op jit(solution)/shard_map/reduce_scatter | solution.py:657
  425.2 47.6 %copy-start.2 = (f32[64,4,512]{2,0,1:T(8,128)S(1)}, f32[64,4,512]{2,0,1:T(8,128)}, u32[]{:S(2)}) copy-start(f32[64,4,512]{2,0,1:T(8,128)} %copy.71) | copy-start | bytes 1572868
  425.2 75.5 %reduce-scatter.11.cloned.1.call-start = ((), (), s32[]{:S(2)}) async-start(), calls=%async_computation.15 | async-start | bytes 1310720 | tf_op jit(solution)/shard_map/reduce_scatter | solution.py:657
  472.8 1.2 copy-start.5
  472.8 2.0 copy-start.4
  478.8 12.7 %collective-permute-start.15 = (f32[1,64,512]{2,1,0:T(8,128)S(1)}, f32[1,64,512]{2,1,0:T(8,128)S(1)}, u32[]{:S(2)}, u32[]{:S(2)}) collective-permute-start(f32[1,64,512]{2,1,0:T(8,128)S(1)} %slice.147), channel_id=1, source_target_pairs={{8,0},{16,8},{24,16},{9,1},{17,9},{25,17},{10,2},{18,10},{26,18},{... | collective-permute-start | bytes 393224 | tf_op jit(solution)/shard_map/ppermute | solution.py:572
  481.5 6.5 %collective-permute-start.14 = (f32[2,1,512]{2,1,0:T(1,128)S(1)}, f32[2,1,512]{2,1,0:T(1,128)S(1)}, u32[]{:S(2)}, u32[]{:S(2)}) collective-permute-start(f32[2,1,512]{2,1,0:T(1,128)S(1)} %get-tuple-element.133), channel_id=1, source_target_pairs={{1,0},{2,1},{3,2},{4,3},{5,4},{6,5},{7,6},{9,8},{10,9},{11,10},{12... | collective-permute-start | bytes 12296 | tf_op jit(solution)/shard_map/ppermute | solution.py:507
  483.8 4.9 collective-permute-start.13
  487.9 29.1 %copy-start.10 = (f32[2,1,512]{2,1,0:T(1,128)}, f32[2,1,512]{2,1,0:T(1,128)S(1)}, u32[]{:S(2)}) copy-start(f32[2,1,512]{2,1,0:T(1,128)S(1)} %collective-permute-done.14.refs_6_) | copy-start | bytes 12292
  488.7 28.4 %copy-start.11 = (f32[2,1,512]{2,1,0:T(1,128)}, f32[2,1,512]{2,1,0:T(1,128)S(1)}, u32[]{:S(2)}) copy-start(f32[2,1,512]{2,1,0:T(1,128)S(1)} %collective-permute-done.13.refs_4_) | copy-start | bytes 12292
  491.5 25.6 %copy-start.7 = (f32[1,64,512]{2,1,0:T(8,128)}, f32[1,64,512]{2,1,0:T(8,128)S(1)}, u32[]{:S(2)}) copy-start(f32[1,64,512]{2,1,0:T(8,128)S(1)} %collective-permute-done.15.refs_9_) | copy-start | bytes 393220
  503.9 13.2 %collective-permute-start.18 = (f32[1,64,512]{2,1,0:T(8,128)S(1)}, f32[1,64,512]{2,1,0:T(8,128)S(1)}, u32[]{:S(2)}, u32[]{:S(2)}) collective-permute-start(f32[1,64,512]{2,1,0:T(8,128)S(1)} %slice.153), channel_id=1, source_target_pairs={{0,8},{8,16},{16,24},{1,9},{9,17},{17,25},{2,10},{10,18},{18,26},{... | collective-permute-start | bytes 393224 | tf_op jit(solution)/shard_map/ppermute | solution.py:578
  508.4 8.7 %collective-permute-start.17 = (f32[2,1,512]{2,1,0:T(1,128)S(1)}, f32[2,1,512]{2,1,0:T(1,128)S(1)}, u32[]{:S(2)}, u32[]{:S(2)}) collective-permute-start(f32[2,1,512]{2,1,0:T(1,128)S(1)} %get-tuple-element.131), channel_id=1, source_target_pairs={{1,0},{2,1},{3,2},{4,3},{5,4},{6,5},{7,6},{9,8},{10,9},{11,10},{12... | collective-permute-start | bytes 12296 | tf_op jit(solution)/shard_map/ppermute | solution.py:507
  511.2 5.9 %collective-permute-start.16 = (f32[2,1,512]{2,1,0:T(1,128)S(1)}, f32[2,1,512]{2,1,0:T(1,128)S(1)}, u32[]{:S(2)}, u32[]{:S(2)}) collective-permute-start(f32[2,1,512]{2,1,0:T(1,128)S(1)} %get-tuple-element.132), channel_id=1, source_target_pairs={{0,1},{1,2},{2,3},{3,4},{4,5},{5,6},{6,7},{8,9},{9,10},{10,11},{11... | collective-permute-start | bytes 12296 | tf_op jit(solution)/shard_map/ppermute | solution.py:506
  517.1 0.7 copy-start.8
  (2 other events, 1.2 us)
Sparse Core Ops, SparseCore 0:
  33.3 46.8 all-gather.2
  227.4 24.8 reduce-scatter.6
  254.8 25.8 reduce-scatter.4
  425.3 25.6 reduce-scatter.8
  472.9 27.7 reduce-scatter.10

commit v4 on v3

--- a/solution.py
+++ b/solution.py
@@ -158,6 +158,12 @@
     return dot(high, table_high) + (dot(low, table_high) + dot(high, table_low))
 
 
+def dot_stacked(both, table_high, table_low):
+    count = both.shape[0] // 2
+    by_high = dot(both, table_high)
+    return by_high[:count] + (by_high[count:] + dot(both[:count], table_low))
+
+
 def params(count=0):
     return pltpu.CompilerParams(vmem_limit_bytes=VMEM_BYTES, dimension_semantics=("arbitrary",) * count)
 
@@ -261,7 +267,7 @@
     others = refs[at + 3 : at + 3 + len(pieces)]
     (
         high_ref, low_ref, out_ref,
-        fk_ref, edge_in_ref, edge_ref, edge_out_ref, u_ref, u_high_ref, u_low_ref,
+        fk_ref, edge_in_ref, edge_ref, edge_out_ref, u_ref, u_both_ref,
     ) = refs[at + 3 + len(pieces) :]
     length_y, _, half, length_x = fk_ref.shape
     lanes_out = out_ref.shape[-1]
@@ -341,8 +347,8 @@
     def _(part):
         rows = pl.ds(pl.multiple_of(part * 64, 64), 64)
         high, low = split(u_ref[rows, :])
-        u_high_ref[rows, :] = high
-        u_low_ref[rows, :] = low
+        u_both_ref[rows, :] = high
+        u_both_ref[pl.ds(pl.multiple_of(count_y * half + part * 64, 64), 64), :] = low
 
     lane_index = lax.broadcasted_iota(jnp.int32, (8, lanes_out), 1)
     row_index = lax.broadcasted_iota(jnp.int32, (8, lanes_out), 0)
@@ -350,7 +356,7 @@
     count = 256 // lanes_out
     for part in range(2 * length_x // 256):
         cols = slice(part * 256, part * 256 + 256)
-        result = dot_three(u_high_ref[...], u_low_ref[...], high_ref[:, cols], low_ref[:, cols])
+        result = dot_stacked(u_both_ref[...], high_ref[:, cols], low_ref[:, cols])
         edges = [edge_out_ref[pl.ds(n * first_ref.shape[1] + step + first_term, 1), cols] for n in range(count_y)]
         for k in range(count):
             q = part * count + k
@@ -401,8 +407,7 @@
             pltpu.VMEM((count_y, first.shape[1], 2 * length_x), F32),
             pltpu.VMEM((count_y * first.shape[1], 2 * length_x), F32),
             pltpu.VMEM((rows, 2 * length_x), F32),
-            pltpu.VMEM((rows, 2 * length_x), BF16),
-            pltpu.VMEM((rows, 2 * length_x), BF16),
+            pltpu.VMEM((2 * rows, 2 * length_x), BF16),
         ],
         compiler_params=params(1),
         cost_estimate=cost(terms * 24 * rows * length_x * length_x, terms * 16 * rows * length_x),
@@ -412,48 +417,53 @@
 
 def gather_kernel(*refs):
     *data_refs, factor_ref, high_ref, low_ref, out_ref = refs
-    blocks, _, _, half, lanes = data_refs[0].shape
+    blocks, _, wide, half, lanes = data_refs[0].shape
     rows = lanes // 2
     parts = []
-    for data_ref in data_refs:
-        for t in range(data_ref.shape[1]):
-            turned = data_ref[:, t, 0].reshape(blocks * half, lanes).T
-            parts.append(jnp.concatenate([turned[:rows], turned[rows:]], axis=1))
+    for y in range(wide):
+        for data_ref in data_refs:
+            for t in range(data_ref.shape[1]):
+                turned = data_ref[:, t, y].reshape(blocks * half, lanes).T
+                parts.append(jnp.concatenate([turned[:rows], turned[rows:]], axis=1))
     high, low = split(jnp.concatenate(parts, axis=0))
-    fields = dot_three(high, low, high_ref[...], low_ref[...])
-    total = factor_ref[0, 0] * fields[:rows]
-    for t in range(1, len(parts)):
-        total = total + factor_ref[t, 0] * fields[t * rows : (t + 1) * rows]
-    out_ref[0] = total
+    fields = dot_stacked(jnp.concatenate([high, low], axis=0), high_ref[...], low_ref[...])
+    terms = len(parts) // wide
+    for y in range(wide):
+        total = factor_ref[0, y] * fields[y * terms * rows : (y * terms + 1) * rows]
+        for t in range(1, terms):
+            at = (y * terms + t) * rows
+            total = total + factor_ref[t, y] * fields[at : at + rows]
+        out_ref[y] = total
 
 
 def gather(chunks, factor, scale, width, group):
     blocks, _, _, half, lanes = chunks[0].shape
     terms, length_y, rows, length_z = factor.shape
     wide = group[1] - group[0]
-    count_y = length_y // width * wide
+    holders = length_y // width
+    high, low = halves(inverse_z_table(blocks, length_z, scale))
 
     def row(n):
-        return n // wide * width + group[0] + n % wide
+        return (n * width + group[0]) // wide
 
     def chunk_spec(shape):
         full = shape[2] == length_y
-        return pl.BlockSpec((blocks, shape[1], 1, half, lanes), lambda n: (0, 0, row(n) if full else n, 0, 0))
-    high, low = halves(inverse_z_table(blocks, length_z, scale))
+        return pl.BlockSpec((blocks, shape[1], wide, half, lanes), lambda n: (0, 0, row(n) if full else n, 0, 0))
+
     return pl.pallas_call(
         gather_kernel,
-        grid=(count_y,),
-        in_specs=[
-            chunk_spec(chunk.shape) for chunk in chunks
-        ] + [
-            pl.BlockSpec((terms, 1, rows, length_z), lambda n: (0, row(n), 0, 0)),
+        grid=(holders,),
+        in_specs=[chunk_spec(chunk.shape) for chunk in chunks] + [
+            pl.BlockSpec((terms, wide, rows, length_z), lambda n: (0, row(n), 0, 0)),
             whole(high.shape, 1),
             whole(low.shape, 1),
         ],
-        out_specs=pl.BlockSpec((1, rows, length_z), lambda n: (n, 0, 0)),
-        out_shape=jax.ShapeDtypeStruct((count_y, rows, length_z), F32),
+        out_specs=pl.BlockSpec((wide, rows, length_z), lambda n: (n, 0, 0)),
+        out_shape=jax.ShapeDtypeStruct((holders * wide, rows, length_z), F32),
         compiler_params=params(1),
-        cost_estimate=cost(6 * terms * count_y * rows * length_z * length_z, 8 * terms * count_y * rows * length_z),
+        cost_estimate=cost(
+            6 * terms * holders * wide * rows * length_z * length_z, 8 * terms * holders * wide * rows * length_z
+        ),
         name="gather_z",
     )(*chunks, factor, jnp.asarray(high), jnp.asarray(low))
 
@@ -616,31 +626,39 @@
     def exchange(values):
         return lax.all_to_all(values, "pencil", 0, 0, tiled=True)
 
+    opposite = [(p, blocks - 1 - p) for p in range(blocks)]
+    middle = terms // 2
+    sent = forward_z([to_brick(present_acoustic)], blocks)[0]
+    sent, multiplier = lax.optimization_barrier((sent, spectral_multiplier))
+    sent = exchange(sent)
     lowest = spectral_multiplier[:, :, 0, :]
-    lowest = lowest + lax.ppermute(
-        flip(flip(lowest, 1), 2), "pencil", [(p, blocks - p) for p in range(1, blocks) if 2 * p != blocks]
-    )
+    others, before = [], None
+    for start, end in ((0, middle), (middle, terms)):
+        if end > start:
+            mirrored = mirror(multiplier, start, end)
+            if others:
+                mirrored, before, lowest = lax.optimization_barrier((mirrored, before, lowest))
+                others = [(*others[0][:2], before)]
+            else:
+                mirrored, lowest = lax.optimization_barrier((mirrored, lowest))
+            before = lax.ppermute(mirrored, "pencil", opposite)
+            if not others:
+                lowest = lowest + lax.ppermute(
+                    flip(flip(lowest, 1), 2),
+                    "pencil",
+                    [(p, blocks - p) for p in range(1, blocks) if 2 * p != blocks],
+                )
+            others.append((start, end, before))
     lowest = jnp.transpose(lowest, (1, 0, 2))
     lowest = jnp.pad(lowest, ((0, 0), (0, -terms % 8), (0, 0)))
-    opposite = [(p, blocks - 1 - p) for p in range(blocks)]
-    middle = terms // 2
-    sent = exchange(forward_z([to_brick(present_acoustic)], blocks)[0])
-    others = []
-    sent, lowest = lax.optimization_barrier((sent, lowest))
-    before = sent
-    for start, end in ((0, middle), (middle, terms)):
-        if end > start:
-            before, mirrored = lax.optimization_barrier((before, mirror(spectral_multiplier, start, end)))
-            if not others:
-                sent = before
-            before = lax.ppermute(mirrored, "pencil", opposite)
-            others.append((start, end, before))
     me = lax.axis_index("term").reshape(1).astype(jnp.int32)
     factor = jnp.transpose(location_factor, (0, 2, 1, 3))
     last, factor = lax.optimization_barrier((others[0][2], factor))
     others[0] = (*others[0][:2], last)
 
-    def gathered(part):
+    def gathered(part, offload):
+        if offload or term_count == 1:
+            return [lax.all_gather(part, "term", axis=0, tiled=False)]
         return [part] + [
             lax.ppermute(part, "term", [(i, (i - d) % term_count) for i in range(term_count)])
             for d in range(1, term_count)
@@ -695,14 +713,12 @@
         for (start, end), (fresh, *older) in zip(spans, bricks):
             fresh, *before = lax.optimization_barrier((fresh, *before))
             if before:
-                parts.append(gathered(before[0]))
+                parts.append(gathered(before[0], True))
             sent, *state = forward_z([fresh, *older], blocks)
             sent = exchange(sent)
-            if parts:
-                sent, *parts[-1] = lax.optimization_barrier((sent, *parts[-1]))
             before = [forward_x(sent, end - start, half, rows)]
             states.append(state)
-        parts.append(gathered(before[0]))
+        parts.append(gathered(before[0], False))
         return parts, states
 
     kinds = jnp.transpose(medium_kinds, (1, 0, 2))

time: 530 us -> 521 us (0.983)
  Pallas kernels: 151 us -> 144 us
    ppermute x2, waiting for transfers between devices: 59.5 us -> 19.4 us  [on_device(): before = lax.ppermute(mirrored, 'pencil', opposite)]
    ppermute x1, waiting for transfers between devices: 0.01 us -> 35.1 us  [on_device(): lax.ppermute(flip(flip(lowest, 1), 2), 'pencil', [(p, blocks - p) for p i...]
    pallas_call x4, Pallas kernels: 39.1 us -> 31.9 us  [gather(): pl.pallas_call(gather_kernel, grid=(holders,), in_specs=[chunk_spec(chunk...]
    ppermute x6 -> x3, waiting for transfers between devices: 33.3 us -> 33.7 us  [gathered(): lax.ppermute(part, 'term', [(i, (i - d) % term_count) for i in range(term...]
    unnamed x48 -> x42, local copies, waits for them, and re-layouts: 21 us -> 21 us
  transfers between devices with their start and end apart: 30 -> 28, of which waited for: 15 -> 14; matrix products, arithmetic and copies ran while one was open for 6% -> 7% of each run, Pallas kernels for 23% -> 23%
where the time goes in v4:
time: 521 us; the launch traced here: 519 us
  waiting for transfers between devices  225 us (43%)
  Pallas kernels  144 us (28%)
  starting transfers between devices  70.3 us (13%)
  local copies, waits for them, and re-layouts  32.4 us (6%)
  blocking collectives  21.9 us (4%)
  between operations  14.5 us (3%)
  other arithmetic  10.5 us (2%)
    all_to_all x6, waiting for transfers between devices, exchange(): return lax.all_to_all(values, 'pencil', 0, 0, tiled=True)  115 us
    pallas_call x5, Pallas kernels, spread(): pl.pallas_call(functools.partial(spread_kernel, spans=spans, counts=[len(...  77.1 us
    ppermute x1, waiting for transfers between devices, on_device(): lax.ppermute(flip(flip(lowest, 1), 2), 'pencil', [(p, blocks - p) for p i...  35.1 us
    ppermute x3, waiting for transfers between devices, gathered(): lax.ppermute(part, 'term', [(i, (i - d) % term_count) for i in range(term...  33.7 us
    pallas_call x4, Pallas kernels, gather(): pl.pallas_call(gather_kernel, grid=(holders,), in_specs=[chunk_spec(chunk...  31.9 us
    all_to_all x6, starting transfers between devices, exchange(): return lax.all_to_all(values, 'pencil', 0, 0, tiled=True)  31.3 us
    all_to_all x2, blocking collectives, exchange(): return lax.all_to_all(values, 'pencil', 0, 0, tiled=True)  21.9 us
    unnamed x42, local copies, waits for them, and re-layouts  21 us
  transfers between devices with their start and end apart: 28, of which 14 were waited for; matrix products, arithmetic and copies ran while one was open for 7% of the time, Pallas kernels for 23%

profile of v4, /device:TPU:11, one launch (start us, length us, event | category | flops | bytes accessed | tf_op | source)
XLA Modules:
  0.0 518.6 jit_solution(18229033260581471978)
XLA Ops:
  9.9 3.0 forward_z.3
  12.9 4.6 all-to-all-start
  18.9 4.8 mirror.3
  27.2 3.6 forward_x.3
  34.0 4.9 mirror.2
  38.9 35.1 %collective-permute-done.1 = f32[4,16,512]{2,0,1:T(4,128)S(1)} collective-permute-done((f32[4,16,512]{2,0,1:T(4,128)S(1)}, f32[4,16,512]{2,0,1:T(4,128)S(1)}, u32[]{:S(2)}, u32[]{:S(2)}) %collective-permute-start.1) | collective-permute-done | bytes 131104 | tf_op jit(solution)/shard_map/ppermute | solution.py:646
  74.1 11.6 %copy.67 = f32[4,64,16,512]{3,1,2,0:T(8,128)} copy(f32[4,64,16,512]{3,2,1,0:T(8,128)} %param.47) | data formatting | bytes 16777216 | tf_op args[2]
  86.4 16.3 %spread.5 = f32[8,2,16,32,128]{4,3,2,1,0:T(8,128)} custom-call(f32[4,264,512]{2,1,0:T(8,128)} %bitcast.43, s32[1]{0:T(128)} %bitcast.2.refs_1_.refs_5_, f32[16,8,512]{2,1,0:T(8,128)} %pad.8.refs_2_.refs_6_, f32[4,16,64,512]{3,2,1,0:T(8,128)} %refs_7_.3, f32[2,16,32,512]{3,2,1,0:T(8,128)} %collective-permute-done.refs_4_.refs_8_, ...), custom_call_target="tpu_custom_call" | custom-call | flops 6442450944 | bytes 8388608 | tf_op jit(solution)/shard_map/spread/pallas_call | solution.py:388
  102.7 19.4 %collective-permute-done.2.refs_4_.refs_9_ = f32[2,16,32,512]{3,2,1,0:T(8,128)S(1)} collective-permute-done((f32[2,16,32,512]{3,2,1,0:T(8,128)}, f32[2,16,32,512]{3,2,1,0:T(8,128)S(1)}, u32[]{:S(2)}, u32[]{:S(2)}) %collective-permute-start.2) | collective-permute-done | bytes 2097184 | tf_op jit(solution)/shard_map/ppermute | solution.py:644
  123.4 5.6 %all-to-all-start.1 = ((f32[8,2,16,32,128]{4,3,2,1,0:T(8,128)}), f32[8,2,16,32,128]{4,3,2,1,0:T(8,128)}, u32[]{:S(2)}, u32[]{:S(2)}) async-start(f32[8,2,16,32,128]{4,3,2,1,0:T(8,128)} %spread.5), calls=%async_computation.1 | async-start | bytes 8388608 | tf_op jit(solution)/shard_map/all_to_all | solution.py:627
  130.2 2.6 collective-permute-start.6
  132.8 4.1 collective-permute-start.5
  136.9 12.2 %spread.6 = f32[8,2,8,32,128]{4,3,2,1,0:T(8,128)} custom-call(f32[4,264,512]{2,1,0:T(8,128)} %bitcast.44, s32[1]{0:T(128)} %bitcast.2.refs_1_.refs_5_, f32[16,8,512]{2,1,0:T(8,128)} %pad.8.refs_2_.refs_6_, f32[4,16,64,512]{3,2,1,0:T(8,128)} %refs_7_.3, f32[2,16,32,512]{3,2,1,0:T(8,128)} %copy-done.1, bf16[1024,1024]{1,0:T(8,128)(2,1)} %constant.49.clone.refs_5_.refs_10_, ...), custom_call_target="tpu_custom_call" | custom-call | flops 3221225472 | bytes 4194304 | tf_op jit(solution)/shard_map/spread/pallas_call | solution.py:388
  149.1 27.5 %all-to-all-done.1.refs_0_ = f32[8,2,16,32,128]{4,3,2,1,0:T(8,128)} async-done(((f32[8,2,16,32,128]{4,3,2,1,0:T(8,128)}), f32[8,2,16,32,128]{4,3,2,1,0:T(8,128)}, u32[]{:S(2)}, u32[]{:S(2)}) %all-to-all-start.1) | async-done | bytes 4194336 | tf_op jit(solution)/shard_map/all_to_all | solution.py:627
  176.6 5.1 all-to-all-start.2
  181.7 2.6 collective-permute-start.4
  184.3 3.0 collective-permute-start.3
  188.1 3.1 select_bitcast_fusion.1
  191.3 2.7 select_bitcast_fusion
  194.1 3.4 fusion.5
  197.4 12.2 %spread.7 = f32[8,2,8,32,128]{4,3,2,1,0:T(8,128)} custom-call(f32[4,264,512]{2,1,0:T(8,128)} %bitcast.45, s32[1]{0:T(128)} %bitcast.2.refs_1_.refs_5_, f32[16,8,512]{2,1,0:T(8,128)} %pad.8.refs_2_.refs_6_, f32[4,16,64,512]{3,2,1,0:T(8,128)} %refs_7_.3, f32[2,16,32,512]{3,2,1,0:T(8,128)} %copy-done.1, bf16[1024,1024]{1,0:T(8,128)(2,1)} %constant.49.clone.refs_5_.refs_10_, ...), custom_call_target="tpu_custom_call" | custom-call | flops 3221225472 | bytes 4194304 | tf_op jit(solution)/shard_map/spread/pallas_call | solution.py:388
  211.0 4.8 all-to-all-start.3
  215.8 8.0 %gather_z.5 = f32[8,64,512]{2,1,0:T(8,128)} custom-call(f32[8,2,16,32,128]{4,3,2,1,0:T(8,128)} %all-to-all-done.1.refs_0_, f32[8,2,8,32,128]{4,3,2,1,0:T(8,128)} %copy-done, f32[4,16,64,512]{3,2,1,0:T(8,128)} %bitcast.34, bf16[512,512]{1,0:T(8,128)(2,1)} %constant.51.clone.refs_3_.refs_2_, bf16[512,512]{1,0:T(8,128)(2,1)} %constant.52.clone.refs_4_.refs_3_), custom_call_target="tpu_custom_call" | custom-call | flops 3221225472 | bytes 8388608 | tf_op jit(solution)/shard_map/gather_z/pallas_call | solution.py:453
  223.8 17.1 %all-to-all-done.3.refs_1_ = f32[8,2,8,32,128]{4,3,2,1,0:T(8,128)} async-done(((f32[8,2,8,32,128]{4,3,2,1,0:T(8,128)}), f32[8,2,8,32,128]{4,3,2,1,0:T(8,128)}, u32[]{:S(2)}, u32[]{:S(2)}) %all-to-all-start.3) | async-done | bytes 2097184 | tf_op jit(solution)/shard_map/all_to_all | solution.py:627
  240.9 8.0 %gather_z.4 = f32[8,64,512]{2,1,0:T(8,128)} custom-call(f32[8,2,16,32,128]{4,3,2,1,0:T(8,128)} %all-to-all-done.1.refs_0_, f32[8,2,8,32,128]{4,3,2,1,0:T(8,128)} %all-to-all-done.3.refs_1_, f32[4,16,64,512]{3,2,1,0:T(8,128)} %bitcast.35, bf16[512,512]{1,0:T(8,128)(2,1)} %constant.51.clone.refs_3_.refs_2_, bf16[512,512]{1,0:T(8,128)(2,1)} %constant.52.clone.refs_4_.refs_3_), custom_call_target="tpu_custom_call" | custom-call | flops 3221225472 | bytes 8388608 | tf_op jit(solution)/shard_map/gather_z/pallas_call | solution.py:453
  250.0 2.6 forward_z.4
  252.6 11.4 %all_to_all.40.data_ref = f32[8,72,128]{2,1,0:T(8,128)} all-to-all(f32[8,72,128]{2,1,0:T(8,128)} %get-tuple-element.70), channel_id=1, replica_groups=mesh['term'=4,'pencil'=8] {'pencil'}, dimensions={0} | all-to-all | bytes 589824 | tf_op jit(solution)/shard_map/all_to_all | solution.py:627
  264.0 3.1 forward_x.4
  267.1 10.4 %reduce-scatter.5.cloned.1.call-done.refs_0_ = f32[2,64,512]{2,1,0:T(8,128)} async-done(((f32[8,64,512]{2,1,0:T(8,128)}), f32[2,64,512]{2,1,0:T(8,128)}) %reduce-scatter.5.cloned.1.call-update) | async-done | bytes 262160 | tf_op jit(solution)/shard_map/reduce_scatter | solution.py:675
  277.5 2.6 forward_z.5
  280.1 10.5 %all_to_all.41.data_ref = f32[8,72,128]{2,1,0:T(8,128)} all-to-all(f32[8,72,128]{2,1,0:T(8,128)} %get-tuple-element.73), channel_id=1, replica_groups=mesh['term'=4,'pencil'=8] {'pencil'}, dimensions={0} | all-to-all | bytes 589824 | tf_op jit(solution)/shard_map/all_to_all | solution.py:627
  290.6 3.1 forward_x.5.refs_1_
  298.1 16.1 %collective-permute-done.9.refs_4_ = f32[136,512]{1,0:T(8,128)S(1)} collective-permute-done((f32[136,512]{1,0:T(8,128)}, f32[136,512]{1,0:T(8,128)S(1)}, u32[]{:S(2)}, u32[]{:S(2)}) %collective-permute-start.9) | collective-permute-done | bytes 278560 | tf_op jit(solution)/shard_map/ppermute | solution.py:663
  314.2 15.5 %collective-permute-done.8.refs_3_ = f32[136,512]{1,0:T(8,128)S(1)} collective-permute-done((f32[136,512]{1,0:T(8,128)}, f32[136,512]{1,0:T(8,128)S(1)}, u32[]{:S(2)}, u32[]{:S(2)}) %collective-permute-start.8) | collective-permute-done | bytes 278560 | tf_op jit(solution)/shard_map/ppermute | solution.py:663
  332.6 18.2 %spread.8 = f32[8,4,8,32,128]{4,3,2,1,0:T(8,128)} custom-call(f32[4,136,512]{2,1,0:T(8,128)} %bitcast.54, f32[136,512]{1,0:T(8,128)} %forward_x.5.refs_1_, f32[136,512]{1,0:T(8,128)} %copy-done.16, f32[136,512]{1,0:T(8,128)} %copy-done.15, f32[136,512]{1,0:T(8,128)} %copy-done.14, s32[1]{0:T(128)} %bitcast.2.refs_1_.refs_5_, ...), custom_call_target="tpu_custom_call" | custom-call | flops 6442450944 | bytes 8388608 | tf_op jit(solution)/shard_map/spread/pallas_call | solution.py:388
  350.7 5.1 all-to-all-start.6
  355.9 18.3 %spread.9 = f32[8,4,8,32,128]{4,3,2,1,0:T(8,128)} custom-call(f32[4,136,512]{2,1,0:T(8,128)} %bitcast.55, f32[136,512]{1,0:T(8,128)} %forward_x.5.refs_1_, f32[136,512]{1,0:T(8,128)} %copy-done.16, f32[136,512]{1,0:T(8,128)} %copy-done.15, f32[136,512]{1,0:T(8,128)} %copy-done.14, s32[1]{0:T(128)} %bitcast.2.refs_1_.refs_5_, ...), custom_call_target="tpu_custom_call" | custom-call | flops 6442450944 | bytes 8388608 | tf_op jit(solution)/shard_map/spread/pallas_call | solution.py:388
  374.2 29.4 %all-to-all-done.6.refs_0_ = f32[8,4,8,32,128]{4,3,2,1,0:T(8,128)} async-done(((f32[8,4,8,32,128]{4,3,2,1,0:T(8,128)}), f32[8,4,8,32,128]{4,3,2,1,0:T(8,128)}, u32[]{:S(2)}, u32[]{:S(2)}) %all-to-all-start.6) | async-done | bytes 4194336 | tf_op jit(solution)/shard_map/all_to_all | solution.py:627
  403.5 6.1 %all-to-all-start.7 = ((f32[8,4,8,32,128]{4,3,2,1,0:T(8,128)}), f32[8,4,8,32,128]{4,3,2,1,0:T(8,128)}, u32[]{:S(2)}, u32[]{:S(2)}) async-start(f32[8,4,8,32,128]{4,3,2,1,0:T(8,128)} %spread.9), calls=%async_computation.10 | async-start | bytes 8388608 | tf_op jit(solution)/shard_map/all_to_all | solution.py:627
  409.6 8.0 %gather_z.6 = f32[8,64,512]{2,1,0:T(8,128)} custom-call(f32[8,4,8,32,128]{4,3,2,1,0:T(8,128)} %all-to-all-done.6.refs_0_, f32[4,16,64,512]{3,2,1,0:T(8,128)} %bitcast.36, bf16[512,512]{1,0:T(8,128)(2,1)} %constant.51.clone.refs_3_.refs_2_, bf16[512,512]{1,0:T(8,128)(2,1)} %constant.52.clone.refs_4_.refs_3_), custom_call_target="tpu_custom_call" | custom-call | flops 3221225472 | bytes 8388608 | tf_op jit(solution)/shard_map/gather_z/pallas_call | solution.py:453
  417.7 39.6 %all-to-all-done.7.refs_0_ = f32[8,4,8,32,128]{4,3,2,1,0:T(8,128)} async-done(((f32[8,4,8,32,128]{4,3,2,1,0:T(8,128)}), f32[8,4,8,32,128]{4,3,2,1,0:T(8,128)}, u32[]{:S(2)}, u32[]{:S(2)}) %all-to-all-start.7) | async-done | bytes 4194336 | tf_op jit(solution)/shard_map/all_to_all | solution.py:627
  457.3 7.9 %gather_z.7 = f32[8,64,512]{2,1,0:T(8,128)} custom-call(f32[8,4,8,32,128]{4,3,2,1,0:T(8,128)} %all-to-all-done.7.refs_0_, f32[4,16,64,512]{3,2,1,0:T(8,128)} %bitcast.37, bf16[512,512]{1,0:T(8,128)(2,1)} %constant.51.clone.refs_3_.refs_2_, bf16[512,512]{1,0:T(8,128)(2,1)} %constant.52.clone.refs_4_.refs_3_), custom_call_target="tpu_custom_call" | custom-call | flops 3221225472 | bytes 8388608 | tf_op jit(solution)/shard_map/gather_z/pallas_call | solution.py:453
  476.3 4.1 collective-permute-start.10
  483.1 8.8 %reduce-scatter.11.cloned.1.call-done.fresh_ref = f32[2,64,512]{2,1,0:T(8,128)} async-done(((f32[8,64,512]{2,1,0:T(8,128)}), f32[2,64,512]{2,1,0:T(8,128)}) %reduce-scatter.11.cloned.1.call-update) | async-done | bytes 262160 | tf_op jit(solution)/shard_map/reduce_scatter | solution.py:675
  495.0 3.9 collective-permute-start.15
  499.7 2.8 collective-permute-start.14
  502.5 3.7 collective-permute-start.13
  509.0 2.7 warm.1
  (104 shorter events, 45.3 us)
Async XLA Ops:
  12.9 13.5 %all-to-all-start = ((f32[8,72,256]{2,1,0:T(8,128)}), f32[8,72,256]{2,1,0:T(8,128)S(1)}, u32[]{:S(2)}, u32[]{:S(2)}) async-start(f32[8,72,256]{2,1,0:T(8,128)} %forward_z.3), calls=%async_computation | async-start | bytes 1179648 | tf_op jit(solution)/shard_map/all_to_all | solution.py:627
  17.5 68.9 %all-gather.5.cloned.1.call-start = ((), (), s32[]{:S(2)}) async-start(), calls=%async_computation.16 | async-start | bytes 2703360 | tf_op jit(solution)/shard_map/all_gather | solution.py:678
  23.7 50.3 %collective-permute-start = (f32[2,16,32,512]{3,2,1,0:T(8,128)}, f32[2,16,32,512]{3,2,1,0:T(8,128)}, u32[]{:S(2)}, u32[]{:S(2)}) collective-permute-start(f32[2,16,32,512]{3,2,1,0:T(8,128)} %mirror.3), channel_id=1, source_target_pairs={{0,7},{1,6},{2,5},{3,4},{4,3},{5,2},{6,1},{7,0},{8,15},{9,14},{10,... | collective-permute-start | bytes 6291464 | tf_op jit(solution)/shard_map/ppermute | solution.py:644
  26.4 0.8 copy-start.3
  31.9 42.1 %collective-permute-start.1 = (f32[4,16,512]{2,0,1:T(4,128)S(1)}, f32[4,16,512]{2,0,1:T(4,128)S(1)}, u32[]{:S(2)}, u32[]{:S(2)}) collective-permute-start(f32[4,16,512]{2,0,1:T(4,128)S(1)} %fusion.8), channel_id=1, source_target_pairs={{1,7},{2,6},{3,5},{5,3},{6,2},{7,1},{9,15},{10,14},{11,13},{13,11}... | collective-permute-start | bytes 393224 | tf_op jit(solution)/shard_map/ppermute | solution.py:646
  74.0 48.1 %collective-permute-start.2 = (f32[2,16,32,512]{3,2,1,0:T(8,128)}, f32[2,16,32,512]{3,2,1,0:T(8,128)S(1)}, u32[]{:S(2)}, u32[]{:S(2)}) collective-permute-start(f32[2,16,32,512]{3,2,1,0:T(8,128)} %mirror.2), channel_id=1, source_target_pairs={{0,7},{1,6},{2,5},{3,4},{4,3},{5,2},{6,1},{7,0},{8,15},{9,14},{10,... | collective-permute-start | bytes 6291464 | tf_op jit(solution)/shard_map/ppermute | solution.py:644
  122.1 1.3 copy-start.1
  123.4 53.2 %all-to-all-start.1 = ((f32[8,2,16,32,128]{4,3,2,1,0:T(8,128)}), f32[8,2,16,32,128]{4,3,2,1,0:T(8,128)}, u32[]{:S(2)}, u32[]{:S(2)}) async-start(f32[8,2,16,32,128]{4,3,2,1,0:T(8,128)} %spread.5), calls=%async_computation.1 | async-start | bytes 8388608 | tf_op jit(solution)/shard_map/all_to_all | solution.py:627
  130.2 63.8 %collective-permute-start.6 = (f32[4,1,512]{2,1,0:T(1,128)S(1)}, f32[4,1,512]{2,1,0:T(1,128)S(1)}, u32[]{:S(2)}, u32[]{:S(2)}) collective-permute-start(f32[4,1,512]{2,1,0:T(1,128)S(1)} %get-tuple-element.113), channel_id=1, source_target_pairs={{1,0},{2,1},{3,2},{4,3},{5,4},{6,5},{7,6},{9,8},{10,9},{11,10},{12... | collective-permute-start | bytes 24584 | tf_op jit(solution)/shard_map/ppermute | solution.py:517
  132.8 61.2 %collective-permute-start.5 = (f32[4,1,512]{2,1,0:T(1,128)S(1)}, f32[4,1,512]{2,1,0:T(1,128)S(1)}, u32[]{:S(2)}, u32[]{:S(2)}) collective-permute-start(f32[4,1,512]{2,1,0:T(1,128)S(1)} %get-tuple-element.114), channel_id=1, source_target_pairs={{0,1},{1,2},{2,3},{3,4},{4,5},{5,6},{6,7},{8,9},{9,10},{10,11},{11... | collective-permute-start | bytes 24584 | tf_op jit(solution)/shard_map/ppermute | solution.py:516
  149.1 38.2 %copy-start.9 = (f32[3,2]{0,1:T(2,128)S(1)}, f32[3,2]{0,1:T(2,128)}, u32[]{:S(2)}) copy-start(f32[3,2]{0,1:T(2,128)} %param.50) | copy-start | bytes 76
  176.6 33.0 %all-to-all-start.2 = ((f32[8,2,8,32,128]{4,3,2,1,0:T(8,128)}), f32[8,2,8,32,128]{4,3,2,1,0:T(8,128)S(1)}, u32[]{:S(2)}, u32[]{:S(2)}) async-start(f32[8,2,8,32,128]{4,3,2,1,0:T(8,128)} %spread.6), calls=%async_computation.2 | async-start | bytes 4194304 | tf_op jit(solution)/shard_map/all_to_all | solution.py:627
  181.7 6.4 %copy-start.6 = (s32[64,4,512]{2,1,0:T(4,128)S(1)}, s32[64,4,512]{2,1,0:T(4,128)}, u32[]{:S(2)}) copy-start(s32[64,4,512]{2,1,0:T(4,128)} %param.49) | copy-start | bytes 1572868
  181.7 12.3 %collective-permute-start.4 = (f32[1,64,512]{2,1,0:T(8,128)S(1)}, f32[1,64,512]{2,1,0:T(8,128)S(1)}, u32[]{:S(2)}, u32[]{:S(2)}) collective-permute-start(f32[1,64,512]{2,1,0:T(8,128)S(1)} %get-tuple-element.117), channel_id=1, source_target_pairs={{8,0},{16,8},{24,16},{9,1},{17,9},{25,17},{10,2},{18,10},{26,18},{... | collective-permute-start | bytes 393224 | tf_op jit(solution)/shard_map/ppermute | solution.py:517
  184.3 9.7 %collective-permute-start.3 = (f32[1,64,512]{2,1,0:T(8,128)S(1)}, f32[1,64,512]{2,1,0:T(8,128)S(1)}, u32[]{:S(2)}, u32[]{:S(2)}) collective-permute-start(f32[1,64,512]{2,1,0:T(8,128)S(1)} %get-tuple-element.118), channel_id=1, source_target_pairs={{0,8},{8,16},{16,24},{1,9},{9,17},{17,25},{2,10},{10,18},{18,26},{... | collective-permute-start | bytes 393224 | tf_op jit(solution)/shard_map/ppermute | solution.py:516
  209.6 1.3 copy-start
  211.0 29.9 %all-to-all-start.3 = ((f32[8,2,8,32,128]{4,3,2,1,0:T(8,128)}), f32[8,2,8,32,128]{4,3,2,1,0:T(8,128)}, u32[]{:S(2)}, u32[]{:S(2)}) async-start(f32[8,2,8,32,128]{4,3,2,1,0:T(8,128)} %spread.7), calls=%async_computation.3 | async-start | bytes 4194304 | tf_op jit(solution)/shard_map/all_to_all | solution.py:627
  215.8 34.3 %reduce-scatter.7.cloned.1.call-start = ((), (), s32[]{:S(2)}) async-start(), calls=%async_computation.13 | async-start | bytes 1310720 | tf_op jit(solution)/shard_map/reduce_scatter | solution.py:675
  223.8 53.7 %reduce-scatter.5.cloned.1.call-start = ((), (), s32[]{:S(2)}) async-start(), calls=%async_computation.12 | async-start | bytes 1310720 | tf_op jit(solution)/shard_map/reduce_scatter | solution.py:675
  248.9 82.9 %all-gather.7.cloned.1.call-start = ((), (), s32[]{:S(2)}) async-start(), calls=%async_computation.17 | async-start | bytes 1392640 | tf_op jit(solution)/shard_map/all_gather | solution.py:661
  293.7 20.5 %collective-permute-start.9 = (f32[136,512]{1,0:T(8,128)}, f32[136,512]{1,0:T(8,128)S(1)}, u32[]{:S(2)}, u32[]{:S(2)}) collective-permute-start(f32[136,512]{1,0:T(8,128)} %forward_x.5.refs_1_), channel_id=1, source_target_pairs={{0,8},{8,16},{16,24},{24,0},{1,9},{9,17},{17,25},{25,1},{2,10},{10... | collective-permute-start | bytes 835592 | tf_op jit(solution)/shard_map/ppermute | solution.py:663
  295.7 34.0 %collective-permute-start.8 = (f32[136,512]{1,0:T(8,128)}, f32[136,512]{1,0:T(8,128)S(1)}, u32[]{:S(2)}, u32[]{:S(2)}) collective-permute-start(f32[136,512]{1,0:T(8,128)} %forward_x.5.refs_1_), channel_id=1, source_target_pairs={{0,16},{8,24},{16,0},{24,8},{1,17},{9,25},{17,1},{25,9},{2,18},{10... | collective-permute-start | bytes 835592 | tf_op jit(solution)/shard_map/ppermute | solution.py:663
  298.1 33.7 %collective-permute-start.7 = (f32[136,512]{1,0:T(8,128)}, f32[136,512]{1,0:T(8,128)S(1)}, u32[]{:S(2)}, u32[]{:S(2)}) collective-permute-start(f32[136,512]{1,0:T(8,128)} %forward_x.5.refs_1_), channel_id=1, source_target_pairs={{0,24},{8,0},{16,8},{24,16},{1,25},{9,1},{17,9},{25,17},{2,26},{10... | collective-permute-start | bytes 835592 | tf_op jit(solution)/shard_map/ppermute | solution.py:663
  314.2 17.6 %copy-start.14 = (f32[136,512]{1,0:T(8,128)}, f32[136,512]{1,0:T(8,128)S(1)}, u32[]{:S(2)}) copy-start(f32[136,512]{1,0:T(8,128)S(1)} %collective-permute-done.9.refs_4_) | copy-start | bytes 835588
  329.7 2.1 copy-start.15
  331.8 0.7 copy-start.16
  350.7 52.8 %all-to-all-start.6 = ((f32[8,4,8,32,128]{4,3,2,1,0:T(8,128)}), f32[8,4,8,32,128]{4,3,2,1,0:T(8,128)}, u32[]{:S(2)}, u32[]{:S(2)}) async-start(f32[8,4,8,32,128]{4,3,2,1,0:T(8,128)} %spread.8), calls=%async_computation.8 | async-start | bytes 8388608 | tf_op jit(solution)/shard_map/all_to_all | solution.py:627
  403.5 53.7 %all-to-all-start.7 = ((f32[8,4,8,32,128]{4,3,2,1,0:T(8,128)}), f32[8,4,8,32,128]{4,3,2,1,0:T(8,128)}, u32[]{:S(2)}, u32[]{:S(2)}) async-start(f32[8,4,8,32,128]{4,3,2,1,0:T(8,128)} %spread.9), calls=%async_computation.10 | async-start | bytes 8388608 | tf_op jit(solution)/shard_map/all_to_all | solution.py:627
  409.6 58.4 %reduce-scatter.9.cloned.1.call-start = ((), (), s32[]{:S(2)}) async-start(), calls=%async_computation.14 | async-start | bytes 1310720 | tf_op jit(solution)/shard_map/reduce_scatter | solution.py:675
  417.6 47.6 %copy-start.2 = (f32[64,4,512]{2,0,1:T(8,128)S(1)}, f32[64,4,512]{2,0,1:T(8,128)}, u32[]{:S(2)}) copy-start(f32[64,4,512]{2,0,1:T(8,128)} %copy.69) | copy-start | bytes 1572868
  417.6 74.2 %reduce-scatter.11.cloned.1.call-start = ((), (), s32[]{:S(2)}) async-start(), calls=%async_computation.15 | async-start | bytes 1310720 | tf_op jit(solution)/shard_map/reduce_scatter | solution.py:675
  465.2 1.2 copy-start.5
  465.2 2.0 copy-start.4
  471.3 11.9 %collective-permute-start.12 = (f32[1,64,512]{2,1,0:T(8,128)S(1)}, f32[1,64,512]{2,1,0:T(8,128)S(1)}, u32[]{:S(2)}, u32[]{:S(2)}) collective-permute-start(f32[1,64,512]{2,1,0:T(8,128)S(1)} %slice.147), channel_id=1, source_target_pairs={{8,0},{16,8},{24,16},{9,1},{17,9},{25,17},{10,2},{18,10},{26,18},{... | collective-permute-start | bytes 393224 | tf_op jit(solution)/shard_map/ppermute | solution.py:582
  474.0 6.5 %collective-permute-start.11 = (f32[2,1,512]{2,1,0:T(1,128)S(1)}, f32[2,1,512]{2,1,0:T(1,128)S(1)}, u32[]{:S(2)}, u32[]{:S(2)}) collective-permute-start(f32[2,1,512]{2,1,0:T(1,128)S(1)} %get-tuple-element.121), channel_id=1, source_target_pairs={{1,0},{2,1},{3,2},{4,3},{5,4},{6,5},{7,6},{9,8},{10,9},{11,10},{12... | collective-permute-start | bytes 12296 | tf_op jit(solution)/shard_map/ppermute | solution.py:517
  476.3 4.9 collective-permute-start.10
  480.4 27.9 %copy-start.10 = (f32[2,1,512]{2,1,0:T(1,128)}, f32[2,1,512]{2,1,0:T(1,128)S(1)}, u32[]{:S(2)}) copy-start(f32[2,1,512]{2,1,0:T(1,128)S(1)} %collective-permute-done.11.refs_6_) | copy-start | bytes 12292
  481.2 27.2 %copy-start.11 = (f32[2,1,512]{2,1,0:T(1,128)}, f32[2,1,512]{2,1,0:T(1,128)S(1)}, u32[]{:S(2)}) copy-start(f32[2,1,512]{2,1,0:T(1,128)S(1)} %collective-permute-done.10.refs_4_) | copy-start | bytes 12292
  483.1 25.3 %copy-start.7 = (f32[1,64,512]{2,1,0:T(8,128)}, f32[1,64,512]{2,1,0:T(8,128)S(1)}, u32[]{:S(2)}) copy-start(f32[1,64,512]{2,1,0:T(8,128)S(1)} %collective-permute-done.12.refs_9_) | copy-start | bytes 393220
  495.0 13.3 %collective-permute-start.15 = (f32[1,64,512]{2,1,0:T(8,128)S(1)}, f32[1,64,512]{2,1,0:T(8,128)S(1)}, u32[]{:S(2)}, u32[]{:S(2)}) collective-permute-start(f32[1,64,512]{2,1,0:T(8,128)S(1)} %slice.153), channel_id=1, source_target_pairs={{0,8},{8,16},{16,24},{1,9},{9,17},{17,25},{2,10},{10,18},{18,26},{... | collective-permute-start | bytes 393224 | tf_op jit(solution)/shard_map/ppermute | solution.py:588
  499.7 8.7 %collective-permute-start.14 = (f32[2,1,512]{2,1,0:T(1,128)S(1)}, f32[2,1,512]{2,1,0:T(1,128)S(1)}, u32[]{:S(2)}, u32[]{:S(2)}) collective-permute-start(f32[2,1,512]{2,1,0:T(1,128)S(1)} %get-tuple-element.119), channel_id=1, source_target_pairs={{1,0},{2,1},{3,2},{4,3},{5,4},{6,5},{7,6},{9,8},{10,9},{11,10},{12... | collective-permute-start | bytes 12296 | tf_op jit(solution)/shard_map/ppermute | solution.py:517
  502.5 5.9 %collective-permute-start.13 = (f32[2,1,512]{2,1,0:T(1,128)S(1)}, f32[2,1,512]{2,1,0:T(1,128)S(1)}, u32[]{:S(2)}, u32[]{:S(2)}) collective-permute-start(f32[2,1,512]{2,1,0:T(1,128)S(1)} %get-tuple-element.120), channel_id=1, source_target_pairs={{0,1},{1,2},{2,3},{3,4},{4,5},{5,6},{6,7},{8,9},{9,10},{10,11},{11... | collective-permute-start | bytes 12296 | tf_op jit(solution)/shard_map/ppermute | solution.py:516
  508.3 0.6 copy-start.12
  508.3 0.6 copy-start.13
  508.4 0.6 copy-start.8
Sparse Core Ops, SparseCore 0:
  31.0 45.0 all-gather.4
  223.9 25.2 reduce-scatter.6
  251.6 25.8 reduce-scatter.4
  278.9 37.3 all-gather.6
  417.7 24.4 reduce-scatter.8
  465.4 26.4 reduce-scatter.10

commit v5 on v4

--- a/solution.py
+++ b/solution.py
@@ -419,20 +419,17 @@
     *data_refs, factor_ref, high_ref, low_ref, out_ref = refs
     blocks, _, wide, half, lanes = data_refs[0].shape
     rows = lanes // 2
-    parts = []
     for y in range(wide):
+        parts = []
         for data_ref in data_refs:
             for t in range(data_ref.shape[1]):
                 turned = data_ref[:, t, y].reshape(blocks * half, lanes).T
                 parts.append(jnp.concatenate([turned[:rows], turned[rows:]], axis=1))
-    high, low = split(jnp.concatenate(parts, axis=0))
-    fields = dot_stacked(jnp.concatenate([high, low], axis=0), high_ref[...], low_ref[...])
-    terms = len(parts) // wide
-    for y in range(wide):
-        total = factor_ref[0, y] * fields[y * terms * rows : (y * terms + 1) * rows]
-        for t in range(1, terms):
-            at = (y * terms + t) * rows
-            total = total + factor_ref[t, y] * fields[at : at + rows]
+        high, low = split(jnp.concatenate(parts, axis=0))
+        fields = dot_stacked(jnp.concatenate([high, low], axis=0), high_ref[...], low_ref[...])
+        total = factor_ref[0, y] * fields[:rows]
+        for t in range(1, len(parts)):
+            total = total + factor_ref[t, y] * fields[t * rows : (t + 1) * rows]
         out_ref[y] = total
 
 
@@ -518,9 +515,13 @@
         yield dim, low, high
 
 
-def heat_step(heat, perfuse):
+def halos_of(heat):
+    return [side for _, low, high in padded_by_one(heat, (("term", 0), ("pencil", 1))) for side in (low, high)]
+
+
+def heat_step(heat, halos, perfuse):
     near = jnp.zeros_like(heat)
-    for dim, low, high in padded_by_one(heat, (("term", 0), ("pencil", 1))):
+    for dim, (low, high) in enumerate(zip(halos[::2], halos[1::2])):
         size = heat.shape[dim]
         near = near + jnp.concatenate([low, lax.slice_in_dim(heat, 0, size - 1, axis=dim)], axis=dim)
         near = near + jnp.concatenate([lax.slice_in_dim(heat, 1, size, axis=dim), high], axis=dim)
@@ -632,15 +633,17 @@
     sent, multiplier = lax.optimization_barrier((sent, spectral_multiplier))
     sent = exchange(sent)
     lowest = spectral_multiplier[:, :, 0, :]
+    thermal = jnp.transpose(thermal_increase, (1, 0, 2))
     others, before = [], None
     for start, end in ((0, middle), (middle, terms)):
         if end > start:
             mirrored = mirror(multiplier, start, end)
             if others:
-                mirrored, before, lowest = lax.optimization_barrier((mirrored, before, lowest))
+                mirrored, before, lowest, *halos = lax.optimization_barrier((mirrored, before, lowest, *halos))
                 others = [(*others[0][:2], before)]
             else:
-                mirrored, lowest = lax.optimization_barrier((mirrored, lowest))
+                mirrored, lowest, thermal = lax.optimization_barrier((mirrored, lowest, thermal))
+                halos = halos_of(thermal)
             before = lax.ppermute(mirrored, "pencil", opposite)
             if not others:
                 lowest = lowest + lax.ppermute(
@@ -730,7 +733,7 @@
         )
         for at in range(2)
     ]
-    heat = heat_step(jnp.transpose(thermal_increase, (1, 0, 2)), perfuse)
+    heat = heat_step(thermal, halos, perfuse)
 
     previous = cut_up(to_brick(prior_acoustic))
     current = cut_up(to_brick(present_acoustic))

time: 521 us -> 527 us (1.012)
  waiting for transfers between devices: 225 us -> 231 us
    all_to_all x6, waiting for transfers between devices: 115 us -> 125 us  [exchange(): return lax.all_to_all(values, 'pencil', 0, 0, tiled=True)]
  transfers between devices with their start and end apart: 28 -> 28, of which waited for: 14 -> 15; matrix products, arithmetic and copies ran while one was open for 7% -> 7% of each run, Pallas kernels for 23% -> 22%
where the time goes in v5:
time: 527 us; the launch traced here: 525 us
  waiting for transfers between devices  231 us (44%)
  Pallas kernels  143 us (27%)
  starting transfers between devices  71.2 us (14%)
  local copies, waits for them, and re-layouts  31.4 us (6%)
  blocking collectives  21.9 us (4%)
  between operations  14.5 us (3%)
  other arithmetic  11.6 us (2%)
    all_to_all x6, waiting for transfers between devices, exchange(): return lax.all_to_all(values, 'pencil', 0, 0, tiled=True)  125 us
    pallas_call x5, Pallas kernels, spread(): pl.pallas_call(functools.partial(spread_kernel, spans=spans, counts=[len(...  77.1 us
    ppermute x3, waiting for transfers between devices, gathered(): lax.ppermute(part, 'term', [(i, (i - d) % term_count) for i in range(term...  33.7 us
    all_to_all x6, starting transfers between devices, exchange(): return lax.all_to_all(values, 'pencil', 0, 0, tiled=True)  32.5 us
    ppermute x1, waiting for transfers between devices, on_device(): lax.ppermute(flip(flip(lowest, 1), 2), 'pencil', [(p, blocks - p) for p i...  31.9 us
    pallas_call x4, Pallas kernels, gather(): pl.pallas_call(gather_kernel, grid=(holders,), in_specs=[chunk_spec(chunk...  30.7 us
    all_to_all x2, blocking collectives, exchange(): return lax.all_to_all(values, 'pencil', 0, 0, tiled=True)  21.9 us
    unnamed x42, local copies, waits for them, and re-layouts  19.9 us
  transfers between devices with their start and end apart: 28, of which 15 were waited for; matrix products, arithmetic and copies ran while one was open for 7% of the time, Pallas kernels for 22%

profile of v5, /device:TPU:11, one launch (start us, length us, event | category | flops | bytes accessed | tf_op | source)
XLA Modules:
  0.0 524.7 jit_solution(10529635950913773499)
XLA Ops:
  9.9 3.1 forward_z.3
  13.0 4.6 all-to-all-start
  19.2 4.8 mirror.3
  27.3 3.6 forward_x.3
  31.0 2.4 collective-permute-start.5
  33.4 4.1 collective-permute-start.4
  42.5 31.9 %collective-permute-done.1 = f32[4,16,512]{2,0,1:T(4,128)S(1)} collective-permute-done((f32[4,16,512]{2,0,1:T(4,128)S(1)}, f32[4,16,512]{2,0,1:T(4,128)S(1)}, u32[]{:S(2)}, u32[]{:S(2)}) %collective-permute-start.1) | collective-permute-done | bytes 131104 | tf_op jit(solution)/shard_map/ppermute | solution.py:649
  74.4 3.5 collective-permute-start.2
  77.9 4.8 mirror.2
  82.9 11.6 %copy.67 = f32[4,64,16,512]{3,1,2,0:T(8,128)} copy(f32[4,64,16,512]{3,2,1,0:T(8,128)} %param.47) | data formatting | bytes 16777216 | tf_op args[2]
  95.2 16.3 %spread.5 = f32[8,2,16,32,128]{4,3,2,1,0:T(8,128)} custom-call(f32[4,264,512]{2,1,0:T(8,128)} %bitcast.43, s32[1]{0:T(128)} %bitcast.2.refs_1_.refs_5_, f32[16,8,512]{2,1,0:T(8,128)} %pad.8.refs_2_.refs_6_, f32[4,16,64,512]{3,2,1,0:T(8,128)} %refs_7_.3, f32[2,16,32,512]{3,2,1,0:T(8,128)} %collective-permute-done.refs_4_.refs_8_, ...), custom_call_target="tpu_custom_call" | custom-call | flops 6442450944 | bytes 8388608 | tf_op jit(solution)/shard_map/spread/pallas_call | solution.py:388
  111.5 19.3 %collective-permute-done.6.refs_4_.refs_9_ = f32[2,16,32,512]{3,2,1,0:T(8,128)S(1)} collective-permute-done((f32[2,16,32,512]{3,2,1,0:T(8,128)}, f32[2,16,32,512]{3,2,1,0:T(8,128)S(1)}, u32[]{:S(2)}, u32[]{:S(2)}) %collective-permute-start.6) | collective-permute-done | bytes 2097184 | tf_op jit(solution)/shard_map/ppermute | solution.py:647
  132.1 5.6 %all-to-all-start.1 = ((f32[8,2,16,32,128]{4,3,2,1,0:T(8,128)}), f32[8,2,16,32,128]{4,3,2,1,0:T(8,128)}, u32[]{:S(2)}, u32[]{:S(2)}) async-start(f32[8,2,16,32,128]{4,3,2,1,0:T(8,128)} %spread.5), calls=%async_computation.1 | async-start | bytes 8388608 | tf_op jit(solution)/shard_map/all_to_all | solution.py:628
  137.7 12.2 %spread.6 = f32[8,2,8,32,128]{4,3,2,1,0:T(8,128)} custom-call(f32[4,264,512]{2,1,0:T(8,128)} %bitcast.44, s32[1]{0:T(128)} %bitcast.2.refs_1_.refs_5_, f32[16,8,512]{2,1,0:T(8,128)} %pad.8.refs_2_.refs_6_, f32[4,16,64,512]{3,2,1,0:T(8,128)} %refs_7_.3, f32[2,16,32,512]{3,2,1,0:T(8,128)} %copy-done.1, bf16[1024,1024]{1,0:T(8,128)(2,1)} %constant.49.clone.refs_5_.refs_10_, ...), custom_call_target="tpu_custom_call" | custom-call | flops 3221225472 | bytes 4194304 | tf_op jit(solution)/shard_map/spread/pallas_call | solution.py:388
  149.9 35.4 %all-to-all-done.1.refs_0_ = f32[8,2,16,32,128]{4,3,2,1,0:T(8,128)} async-done(((f32[8,2,16,32,128]{4,3,2,1,0:T(8,128)}), f32[8,2,16,32,128]{4,3,2,1,0:T(8,128)}, u32[]{:S(2)}, u32[]{:S(2)}) %all-to-all-start.1) | async-done | bytes 4194336 | tf_op jit(solution)/shard_map/all_to_all | solution.py:628
  185.3 5.2 all-to-all-start.2
  191.1 4.1 select_bitcast_fusion.1
  195.3 2.7 select_bitcast_fusion
  198.2 3.4 fusion.5
  201.5 12.2 %spread.7 = f32[8,2,8,32,128]{4,3,2,1,0:T(8,128)} custom-call(f32[4,264,512]{2,1,0:T(8,128)} %bitcast.45, s32[1]{0:T(128)} %bitcast.2.refs_1_.refs_5_, f32[16,8,512]{2,1,0:T(8,128)} %pad.8.refs_2_.refs_6_, f32[4,16,64,512]{3,2,1,0:T(8,128)} %refs_7_.3, f32[2,16,32,512]{3,2,1,0:T(8,128)} %copy-done.1, bf16[1024,1024]{1,0:T(8,128)(2,1)} %constant.49.clone.refs_5_.refs_10_, ...), custom_call_target="tpu_custom_call" | custom-call | flops 3221225472 | bytes 4194304 | tf_op jit(solution)/shard_map/spread/pallas_call | solution.py:388
  216.9 5.8 %all-to-all-start.3 = ((f32[8,2,8,32,128]{4,3,2,1,0:T(8,128)}), f32[8,2,8,32,128]{4,3,2,1,0:T(8,128)}, u32[]{:S(2)}, u32[]{:S(2)}) async-start(f32[8,2,8,32,128]{4,3,2,1,0:T(8,128)} %spread.7), calls=%async_computation.3 | async-start | bytes 4194304 | tf_op jit(solution)/shard_map/all_to_all | solution.py:628
  222.7 7.7 %gather_z.5 = f32[8,64,512]{2,1,0:T(8,128)} custom-call(f32[8,2,16,32,128]{4,3,2,1,0:T(8,128)} %all-to-all-done.1.refs_0_, f32[8,2,8,32,128]{4,3,2,1,0:T(8,128)} %copy-done, f32[4,16,64,512]{3,2,1,0:T(8,128)} %bitcast.34, bf16[512,512]{1,0:T(8,128)(2,1)} %constant.51.clone.refs_3_.refs_2_, bf16[512,512]{1,0:T(8,128)(2,1)} %constant.52.clone.refs_4_.refs_3_), custom_call_target="tpu_custom_call" | custom-call | flops 3221225472 | bytes 8388608 | tf_op jit(solution)/shard_map/gather_z/pallas_call | solution.py:450
  230.5 17.4 %all-to-all-done.3.refs_1_ = f32[8,2,8,32,128]{4,3,2,1,0:T(8,128)} async-done(((f32[8,2,8,32,128]{4,3,2,1,0:T(8,128)}), f32[8,2,8,32,128]{4,3,2,1,0:T(8,128)}, u32[]{:S(2)}, u32[]{:S(2)}) %all-to-all-start.3) | async-done | bytes 2097184 | tf_op jit(solution)/shard_map/all_to_all | solution.py:628
  247.9 7.7 %gather_z.4 = f32[8,64,512]{2,1,0:T(8,128)} custom-call(f32[8,2,16,32,128]{4,3,2,1,0:T(8,128)} %all-to-all-done.1.refs_0_, f32[8,2,8,32,128]{4,3,2,1,0:T(8,128)} %all-to-all-done.3.refs_1_, f32[4,16,64,512]{3,2,1,0:T(8,128)} %bitcast.35, bf16[512,512]{1,0:T(8,128)(2,1)} %constant.51.clone.refs_3_.refs_2_, bf16[512,512]{1,0:T(8,128)(2,1)} %constant.52.clone.refs_4_.refs_3_), custom_call_target="tpu_custom_call" | custom-call | flops 3221225472 | bytes 8388608 | tf_op jit(solution)/shard_map/gather_z/pallas_call | solution.py:450
  256.7 2.6 forward_z.4
  259.3 11.3 %all_to_all.40.data_ref = f32[8,72,128]{2,1,0:T(8,128)} all-to-all(f32[8,72,128]{2,1,0:T(8,128)} %get-tuple-element.80), channel_id=1, replica_groups=mesh['term'=4,'pencil'=8] {'pencil'}, dimensions={0} | all-to-all | bytes 589824 | tf_op jit(solution)/shard_map/all_to_all | solution.py:628
  270.6 3.1 forward_x.4
  273.7 10.2 %reduce-scatter.5.cloned.1.call-done.refs_0_ = f32[2,64,512]{2,1,0:T(8,128)} async-done(((f32[8,64,512]{2,1,0:T(8,128)}), f32[2,64,512]{2,1,0:T(8,128)}) %reduce-scatter.5.cloned.1.call-update) | async-done | bytes 262160 | tf_op jit(solution)/shard_map/reduce_scatter | solution.py:678
  284.0 2.6 forward_z.5
  286.6 10.5 %all_to_all.41.data_ref = f32[8,72,128]{2,1,0:T(8,128)} all-to-all(f32[8,72,128]{2,1,0:T(8,128)} %get-tuple-element.83), channel_id=1, replica_groups=mesh['term'=4,'pencil'=8] {'pencil'}, dimensions={0} | all-to-all | bytes 589824 | tf_op jit(solution)/shard_map/all_to_all | solution.py:628
  297.1 3.1 forward_x.5.refs_1_
  302.2 2.5 collective-permute-start.8
  304.7 16.1 %collective-permute-done.9.refs_4_ = f32[136,512]{1,0:T(8,128)S(1)} collective-permute-done((f32[136,512]{1,0:T(8,128)}, f32[136,512]{1,0:T(8,128)S(1)}, u32[]{:S(2)}, u32[]{:S(2)}) %collective-permute-start.9) | collective-permute-done | bytes 278560 | tf_op jit(solution)/shard_map/ppermute | solution.py:666
  320.7 15.5 %collective-permute-done.8.refs_3_ = f32[136,512]{1,0:T(8,128)S(1)} collective-permute-done((f32[136,512]{1,0:T(8,128)}, f32[136,512]{1,0:T(8,128)S(1)}, u32[]{:S(2)}, u32[]{:S(2)}) %collective-permute-start.8) | collective-permute-done | bytes 278560 | tf_op jit(solution)/shard_map/ppermute | solution.py:666
  339.1 18.2 %spread.8 = f32[8,4,8,32,128]{4,3,2,1,0:T(8,128)} custom-call(f32[4,136,512]{2,1,0:T(8,128)} %bitcast.54, f32[136,512]{1,0:T(8,128)} %forward_x.5.refs_1_, f32[136,512]{1,0:T(8,128)} %copy-done.16, f32[136,512]{1,0:T(8,128)} %copy-done.15, f32[136,512]{1,0:T(8,128)} %copy-done.14, s32[1]{0:T(128)} %bitcast.2.refs_1_.refs_5_, ...), custom_call_target="tpu_custom_call" | custom-call | flops 6442450944 | bytes 8388608 | tf_op jit(solution)/shard_map/spread/pallas_call | solution.py:388
  357.2 5.2 all-to-all-start.6
  362.4 18.3 %spread.9 = f32[8,4,8,32,128]{4,3,2,1,0:T(8,128)} custom-call(f32[4,136,512]{2,1,0:T(8,128)} %bitcast.55, f32[136,512]{1,0:T(8,128)} %forward_x.5.refs_1_, f32[136,512]{1,0:T(8,128)} %copy-done.16, f32[136,512]{1,0:T(8,128)} %copy-done.15, f32[136,512]{1,0:T(8,128)} %copy-done.14, s32[1]{0:T(128)} %bitcast.2.refs_1_.refs_5_, ...), custom_call_target="tpu_custom_call" | custom-call | flops 6442450944 | bytes 8388608 | tf_op jit(solution)/shard_map/spread/pallas_call | solution.py:388
  380.7 29.4 %all-to-all-done.6.refs_0_ = f32[8,4,8,32,128]{4,3,2,1,0:T(8,128)} async-done(((f32[8,4,8,32,128]{4,3,2,1,0:T(8,128)}), f32[8,4,8,32,128]{4,3,2,1,0:T(8,128)}, u32[]{:S(2)}, u32[]{:S(2)}) %all-to-all-start.6) | async-done | bytes 4194336 | tf_op jit(solution)/shard_map/all_to_all | solution.py:628
  410.0 6.1 %all-to-all-start.7 = ((f32[8,4,8,32,128]{4,3,2,1,0:T(8,128)}), f32[8,4,8,32,128]{4,3,2,1,0:T(8,128)}, u32[]{:S(2)}, u32[]{:S(2)}) async-start(f32[8,4,8,32,128]{4,3,2,1,0:T(8,128)} %spread.9), calls=%async_computation.10 | async-start | bytes 8388608 | tf_op jit(solution)/shard_map/all_to_all | solution.py:628
  416.1 7.7 %gather_z.6 = f32[8,64,512]{2,1,0:T(8,128)} custom-call(f32[8,4,8,32,128]{4,3,2,1,0:T(8,128)} %all-to-all-done.6.refs_0_, f32[4,16,64,512]{3,2,1,0:T(8,128)} %bitcast.36, bf16[512,512]{1,0:T(8,128)(2,1)} %constant.51.clone.refs_3_.refs_2_, bf16[512,512]{1,0:T(8,128)(2,1)} %constant.52.clone.refs_4_.refs_3_), custom_call_target="tpu_custom_call" | custom-call | flops 3221225472 | bytes 8388608 | tf_op jit(solution)/shard_map/gather_z/pallas_call | solution.py:450
  423.9 39.9 %all-to-all-done.7.refs_0_ = f32[8,4,8,32,128]{4,3,2,1,0:T(8,128)} async-done(((f32[8,4,8,32,128]{4,3,2,1,0:T(8,128)}), f32[8,4,8,32,128]{4,3,2,1,0:T(8,128)}, u32[]{:S(2)}, u32[]{:S(2)}) %all-to-all-start.7) | async-done | bytes 4194336 | tf_op jit(solution)/shard_map/all_to_all | solution.py:628
  463.8 7.6 %gather_z.7 = f32[8,64,512]{2,1,0:T(8,128)} custom-call(f32[8,4,8,32,128]{4,3,2,1,0:T(8,128)} %all-to-all-done.7.refs_0_, f32[4,16,64,512]{3,2,1,0:T(8,128)} %bitcast.37, bf16[512,512]{1,0:T(8,128)(2,1)} %constant.51.clone.refs_3_.refs_2_, bf16[512,512]{1,0:T(8,128)(2,1)} %constant.52.clone.refs_4_.refs_3_), custom_call_target="tpu_custom_call" | custom-call | flops 3221225472 | bytes 8388608 | tf_op jit(solution)/shard_map/gather_z/pallas_call | solution.py:450
  482.5 4.1 collective-permute-start.10
  489.3 8.7 %reduce-scatter.11.cloned.1.call-done.fresh_ref = f32[2,64,512]{2,1,0:T(8,128)} async-done(((f32[8,64,512]{2,1,0:T(8,128)}), f32[2,64,512]{2,1,0:T(8,128)}) %reduce-scatter.11.cloned.1.call-update) | async-done | bytes 262160 | tf_op jit(solution)/shard_map/reduce_scatter | solution.py:678
  501.2 3.8 collective-permute-start.15
  505.8 2.8 collective-permute-start.14
  508.6 3.6 collective-permute-start.13
  515.2 2.7 warm.1
  (104 shorter events, 45.3 us)
Async XLA Ops:
  9.9 9.0 %copy-start.6 = (f32[64,4,512]{2,1,0:T(4,128)S(1)}, f32[64,4,512]{2,1,0:T(4,128)}, u32[]{:S(2)}) copy-start(f32[64,4,512]{2,1,0:T(4,128)} %param.51) | copy-start | bytes 1572868
  13.0 13.5 %all-to-all-start = ((f32[8,72,256]{2,1,0:T(8,128)}), f32[8,72,256]{2,1,0:T(8,128)S(1)}, u32[]{:S(2)}, u32[]{:S(2)}) async-start(f32[8,72,256]{2,1,0:T(8,128)} %forward_z.3), calls=%async_computation | async-start | bytes 1179648 | tf_op jit(solution)/shard_map/all_to_all | solution.py:628
  17.6 77.6 %all-gather.5.cloned.1.call-start = ((), (), s32[]{:S(2)}) async-start(), calls=%async_computation.16 | async-start | bytes 2703360 | tf_op jit(solution)/shard_map/all_gather | solution.py:681
  24.0 58.8 %collective-permute-start = (f32[2,16,32,512]{3,2,1,0:T(8,128)}, f32[2,16,32,512]{3,2,1,0:T(8,128)}, u32[]{:S(2)}, u32[]{:S(2)}) collective-permute-start(f32[2,16,32,512]{3,2,1,0:T(8,128)} %mirror.3), channel_id=1, source_target_pairs={{0,7},{1,6},{2,5},{3,4},{4,3},{5,2},{6,1},{7,0},{8,15},{9,14},{10,... | collective-permute-start | bytes 6291464 | tf_op jit(solution)/shard_map/ppermute | solution.py:647
  26.5 0.8 copy-start.3
  31.0 51.8 %collective-permute-start.5 = (f32[4,1,512]{2,1,0:T(1,128)S(1)}, f32[4,1,512]{2,1,0:T(1,128)S(1)}, u32[]{:S(2)}, u32[]{:S(2)}) collective-permute-start(f32[4,1,512]{2,1,0:T(1,128)S(1)} %get-tuple-element.125), channel_id=1, source_target_pairs={{1,0},{2,1},{3,2},{4,3},{5,4},{6,5},{7,6},{9,8},{10,9},{11,10},{12... | collective-permute-start | bytes 24584 | tf_op jit(solution)/shard_map/ppermute | solution.py:514
  33.4 49.4 %collective-permute-start.4 = (f32[4,1,512]{2,1,0:T(1,128)S(1)}, f32[4,1,512]{2,1,0:T(1,128)S(1)}, u32[]{:S(2)}, u32[]{:S(2)}) collective-permute-start(f32[4,1,512]{2,1,0:T(1,128)S(1)} %get-tuple-element.126), channel_id=1, source_target_pairs={{0,1},{1,2},{2,3},{3,4},{4,5},{5,6},{6,7},{8,9},{9,10},{10,11},{11... | collective-permute-start | bytes 24584 | tf_op jit(solution)/shard_map/ppermute | solution.py:513
  38.4 35.9 %collective-permute-start.1 = (f32[4,16,512]{2,0,1:T(4,128)S(1)}, f32[4,16,512]{2,0,1:T(4,128)S(1)}, u32[]{:S(2)}, u32[]{:S(2)}) collective-permute-start(f32[4,16,512]{2,0,1:T(4,128)S(1)} %fusion.8), channel_id=1, source_target_pairs={{1,7},{2,6},{3,5},{5,3},{6,2},{7,1},{9,15},{10,14},{11,13},{13,11}... | collective-permute-start | bytes 393224 | tf_op jit(solution)/shard_map/ppermute | solution.py:649
  40.4 42.4 %collective-permute-start.3 = (f32[1,64,512]{2,1,0:T(8,128)S(1)}, f32[1,64,512]{2,1,0:T(8,128)S(1)}, u32[]{:S(2)}, u32[]{:S(2)}) collective-permute-start(f32[1,64,512]{2,1,0:T(8,128)S(1)} %get-tuple-element.127), channel_id=1, source_target_pairs={{8,0},{16,8},{24,16},{9,1},{17,9},{25,17},{10,2},{18,10},{26,18},{... | collective-permute-start | bytes 393224 | tf_op jit(solution)/shard_map/ppermute | solution.py:514
  74.4 8.4 %collective-permute-start.2 = (f32[1,64,512]{2,1,0:T(8,128)S(1)}, f32[1,64,512]{2,1,0:T(8,128)S(1)}, u32[]{:S(2)}, u32[]{:S(2)}) collective-permute-start(f32[1,64,512]{2,1,0:T(8,128)S(1)} %get-tuple-element.128), channel_id=1, source_target_pairs={{0,8},{8,16},{16,24},{1,9},{9,17},{17,25},{2,10},{10,18},{18,26},{... | collective-permute-start | bytes 393224 | tf_op jit(solution)/shard_map/ppermute | solution.py:513
  82.8 48.0 %collective-permute-start.6 = (f32[2,16,32,512]{3,2,1,0:T(8,128)}, f32[2,16,32,512]{3,2,1,0:T(8,128)S(1)}, u32[]{:S(2)}, u32[]{:S(2)}) collective-permute-start(f32[2,16,32,512]{3,2,1,0:T(8,128)} %mirror.2), channel_id=1, source_target_pairs={{0,7},{1,6},{2,5},{3,4},{4,3},{5,2},{6,1},{7,0},{8,15},{9,14},{10,... | collective-permute-start | bytes 6291464 | tf_op jit(solution)/shard_map/ppermute | solution.py:647
  130.8 1.3 copy-start.1
  132.1 53.2 %all-to-all-start.1 = ((f32[8,2,16,32,128]{4,3,2,1,0:T(8,128)}), f32[8,2,16,32,128]{4,3,2,1,0:T(8,128)}, u32[]{:S(2)}, u32[]{:S(2)}) async-start(f32[8,2,16,32,128]{4,3,2,1,0:T(8,128)} %spread.5), calls=%async_computation.1 | async-start | bytes 8388608 | tf_op jit(solution)/shard_map/all_to_all | solution.py:628
  149.9 40.5 %copy-start.9 = (f32[3,2]{0,1:T(2,128)S(1)}, f32[3,2]{0,1:T(2,128)}, u32[]{:S(2)}) copy-start(f32[3,2]{0,1:T(2,128)} %param.50) | copy-start | bytes 76
  185.3 30.2 %all-to-all-start.2 = ((f32[8,2,8,32,128]{4,3,2,1,0:T(8,128)}), f32[8,2,8,32,128]{4,3,2,1,0:T(8,128)S(1)}, u32[]{:S(2)}, u32[]{:S(2)}) async-start(f32[8,2,8,32,128]{4,3,2,1,0:T(8,128)} %spread.6), calls=%async_computation.2 | async-start | bytes 4194304 | tf_op jit(solution)/shard_map/all_to_all | solution.py:628
  215.5 1.3 copy-start
  216.9 31.0 %all-to-all-start.3 = ((f32[8,2,8,32,128]{4,3,2,1,0:T(8,128)}), f32[8,2,8,32,128]{4,3,2,1,0:T(8,128)}, u32[]{:S(2)}, u32[]{:S(2)}) async-start(f32[8,2,8,32,128]{4,3,2,1,0:T(8,128)} %spread.7), calls=%async_computation.3 | async-start | bytes 4194304 | tf_op jit(solution)/shard_map/all_to_all | solution.py:628
  222.7 34.0 %reduce-scatter.7.cloned.1.call-start = ((), (), s32[]{:S(2)}) async-start(), calls=%async_computation.13 | async-start | bytes 1310720 | tf_op jit(solution)/shard_map/reduce_scatter | solution.py:678
  230.4 53.5 %reduce-scatter.5.cloned.1.call-start = ((), (), s32[]{:S(2)}) async-start(), calls=%async_computation.12 | async-start | bytes 1310720 | tf_op jit(solution)/shard_map/reduce_scatter | solution.py:678
  255.6 82.7 %all-gather.7.cloned.1.call-start = ((), (), s32[]{:S(2)}) async-start(), calls=%async_computation.17 | async-start | bytes 1392640 | tf_op jit(solution)/shard_map/all_gather | solution.py:664
  300.2 20.5 %collective-permute-start.9 = (f32[136,512]{1,0:T(8,128)}, f32[136,512]{1,0:T(8,128)S(1)}, u32[]{:S(2)}, u32[]{:S(2)}) collective-permute-start(f32[136,512]{1,0:T(8,128)} %forward_x.5.refs_1_), channel_id=1, source_target_pairs={{0,8},{8,16},{16,24},{24,0},{1,9},{9,17},{17,25},{25,1},{2,10},{10... | collective-permute-start | bytes 835592 | tf_op jit(solution)/shard_map/ppermute | solution.py:666
  302.2 34.1 %collective-permute-start.8 = (f32[136,512]{1,0:T(8,128)}, f32[136,512]{1,0:T(8,128)S(1)}, u32[]{:S(2)}, u32[]{:S(2)}) collective-permute-start(f32[136,512]{1,0:T(8,128)} %forward_x.5.refs_1_), channel_id=1, source_target_pairs={{0,16},{8,24},{16,0},{24,8},{1,17},{9,25},{17,1},{25,9},{2,18},{10... | collective-permute-start | bytes 835592 | tf_op jit(solution)/shard_map/ppermute | solution.py:666
  304.6 33.7 %collective-permute-start.7 = (f32[136,512]{1,0:T(8,128)}, f32[136,512]{1,0:T(8,128)S(1)}, u32[]{:S(2)}, u32[]{:S(2)}) collective-permute-start(f32[136,512]{1,0:T(8,128)} %forward_x.5.refs_1_), channel_id=1, source_target_pairs={{0,24},{8,0},{16,8},{24,16},{1,25},{9,1},{17,9},{25,17},{2,26},{10... | collective-permute-start | bytes 835592 | tf_op jit(solution)/shard_map/ppermute | solution.py:666
  320.7 17.6 %copy-start.14 = (f32[136,512]{1,0:T(8,128)}, f32[136,512]{1,0:T(8,128)S(1)}, u32[]{:S(2)}) copy-start(f32[136,512]{1,0:T(8,128)S(1)} %collective-permute-done.9.refs_4_) | copy-start | bytes 835588
  336.2 2.1 copy-start.15
  338.3 0.7 copy-start.16
  357.2 52.8 %all-to-all-start.6 = ((f32[8,4,8,32,128]{4,3,2,1,0:T(8,128)}), f32[8,4,8,32,128]{4,3,2,1,0:T(8,128)}, u32[]{:S(2)}, u32[]{:S(2)}) async-start(f32[8,4,8,32,128]{4,3,2,1,0:T(8,128)} %spread.8), calls=%async_computation.8 | async-start | bytes 8388608 | tf_op jit(solution)/shard_map/all_to_all | solution.py:628
  410.0 53.7 %all-to-all-start.7 = ((f32[8,4,8,32,128]{4,3,2,1,0:T(8,128)}), f32[8,4,8,32,128]{4,3,2,1,0:T(8,128)}, u32[]{:S(2)}, u32[]{:S(2)}) async-start(f32[8,4,8,32,128]{4,3,2,1,0:T(8,128)} %spread.9), calls=%async_computation.10 | async-start | bytes 8388608 | tf_op jit(solution)/shard_map/all_to_all | solution.py:628
  416.1 58.1 %reduce-scatter.9.cloned.1.call-start = ((), (), s32[]{:S(2)}) async-start(), calls=%async_computation.14 | async-start | bytes 1310720 | tf_op jit(solution)/shard_map/reduce_scatter | solution.py:678
  423.8 47.6 %copy-start.2 = (f32[64,4,512]{2,0,1:T(8,128)S(1)}, f32[64,4,512]{2,0,1:T(8,128)}, u32[]{:S(2)}) copy-start(f32[64,4,512]{2,0,1:T(8,128)} %copy.69) | copy-start | bytes 1572868
  423.8 74.2 %reduce-scatter.11.cloned.1.call-start = ((), (), s32[]{:S(2)}) async-start(), calls=%async_computation.15 | async-start | bytes 1310720 | tf_op jit(solution)/shard_map/reduce_scatter | solution.py:678
  471.4 1.2 copy-start.5
  471.4 2.0 copy-start.4
  477.4 11.9 %collective-permute-start.12 = (f32[1,64,512]{2,1,0:T(8,128)S(1)}, f32[1,64,512]{2,1,0:T(8,128)S(1)}, u32[]{:S(2)}, u32[]{:S(2)}) collective-permute-start(f32[1,64,512]{2,1,0:T(8,128)S(1)} %slice.147), channel_id=1, source_target_pairs={{8,0},{16,8},{24,16},{9,1},{17,9},{25,17},{10,2},{18,10},{26,18},{... | collective-permute-start | bytes 393224 | tf_op jit(solution)/shard_map/ppermute | solution.py:583
  480.2 6.5 %collective-permute-start.11 = (f32[2,1,512]{2,1,0:T(1,128)S(1)}, f32[2,1,512]{2,1,0:T(1,128)S(1)}, u32[]{:S(2)}, u32[]{:S(2)}) collective-permute-start(f32[2,1,512]{2,1,0:T(1,128)S(1)} %get-tuple-element.131), channel_id=1, source_target_pairs={{1,0},{2,1},{3,2},{4,3},{5,4},{6,5},{7,6},{9,8},{10,9},{11,10},{12... | collective-permute-start | bytes 12296 | tf_op jit(solution)/shard_map/ppermute | solution.py:514
  482.5 4.9 collective-permute-start.10
  486.6 27.9 %copy-start.10 = (f32[2,1,512]{2,1,0:T(1,128)}, f32[2,1,512]{2,1,0:T(1,128)S(1)}, u32[]{:S(2)}) copy-start(f32[2,1,512]{2,1,0:T(1,128)S(1)} %collective-permute-done.11.refs_6_) | copy-start | bytes 12292
  487.4 27.2 %copy-start.11 = (f32[2,1,512]{2,1,0:T(1,128)}, f32[2,1,512]{2,1,0:T(1,128)S(1)}, u32[]{:S(2)}) copy-start(f32[2,1,512]{2,1,0:T(1,128)S(1)} %collective-permute-done.10.refs_4_) | copy-start | bytes 12292
  489.3 25.2 %copy-start.7 = (f32[1,64,512]{2,1,0:T(8,128)}, f32[1,64,512]{2,1,0:T(8,128)S(1)}, u32[]{:S(2)}) copy-start(f32[1,64,512]{2,1,0:T(8,128)S(1)} %collective-permute-done.12.refs_9_) | copy-start | bytes 393220
  501.2 13.3 %collective-permute-start.15 = (f32[1,64,512]{2,1,0:T(8,128)S(1)}, f32[1,64,512]{2,1,0:T(8,128)S(1)}, u32[]{:S(2)}, u32[]{:S(2)}) collective-permute-start(f32[1,64,512]{2,1,0:T(8,128)S(1)} %slice.153), channel_id=1, source_target_pairs={{0,8},{8,16},{16,24},{1,9},{9,17},{17,25},{2,10},{10,18},{18,26},{... | collective-permute-start | bytes 393224 | tf_op jit(solution)/shard_map/ppermute | solution.py:589
  505.8 8.7 %collective-permute-start.14 = (f32[2,1,512]{2,1,0:T(1,128)S(1)}, f32[2,1,512]{2,1,0:T(1,128)S(1)}, u32[]{:S(2)}, u32[]{:S(2)}) collective-permute-start(f32[2,1,512]{2,1,0:T(1,128)S(1)} %get-tuple-element.129), channel_id=1, source_target_pairs={{1,0},{2,1},{3,2},{4,3},{5,4},{6,5},{7,6},{9,8},{10,9},{11,10},{12... | collective-permute-start | bytes 12296 | tf_op jit(solution)/shard_map/ppermute | solution.py:514
  508.6 5.9 %collective-permute-start.13 = (f32[2,1,512]{2,1,0:T(1,128)S(1)}, f32[2,1,512]{2,1,0:T(1,128)S(1)}, u32[]{:S(2)}, u32[]{:S(2)}) collective-permute-start(f32[2,1,512]{2,1,0:T(1,128)S(1)} %get-tuple-element.130), channel_id=1, source_target_pairs={{0,1},{1,2},{2,3},{3,4},{4,5},{5,6},{6,7},{8,9},{9,10},{10,11},{11... | collective-permute-start | bytes 12296 | tf_op jit(solution)/shard_map/ppermute | solution.py:513
  514.5 0.6 copy-start.12
  514.5 0.6 copy-start.13
  514.5 0.6 copy-start.8
Sparse Core Ops, SparseCore 0:
  31.1 47.9 all-gather.4
  230.6 25.0 reduce-scatter.6
  258.1 25.7 reduce-scatter.4
  285.4 37.3 all-gather.6
  423.9 24.4 reduce-scatter.8
  471.5 26.4 reduce-scatter.10

commit v6 on v5

--- a/solution.py
+++ b/solution.py
@@ -267,7 +267,7 @@
     others = refs[at + 3 : at + 3 + len(pieces)]
     (
         high_ref, low_ref, out_ref,
-        fk_ref, edge_in_ref, edge_ref, edge_out_ref, u_ref, u_both_ref,
+        fk_ref, edge_in_ref, edge_ref, u_ref, u_both_ref,
     ) = refs[at + 3 + len(pieces) :]
     length_y, _, half, length_x = fk_ref.shape
     lanes_out = out_ref.shape[-1]
@@ -315,9 +315,6 @@
             for n, y in enumerate(wanted):
                 edge_ref[n, :, index * 128 : index * 128 + 128] = values[y][0]
                 edge_ref[n, :, length_x + index * 128 : length_x + index * 128 + 128] = values[y][1]
-        high, low = split(edge_ref[...].reshape(-1, 2 * length_x))
-        edge_out_ref[...] = dot_three(high, low, high_ref[...], low_ref[...])
-
     row_index = lax.broadcasted_iota(jnp.int32, (8, 128), 0)
 
     def weigh(other_ref):
@@ -343,12 +340,18 @@
         for other_ref, (start, end) in zip(others, pieces):
             pl.when(jnp.logical_and(step >= start, step < end))(functools.partial(weigh, other_ref))
 
-    @pl.loop(0, count_y * half // 64)
+    main_rows = count_y * half
+    all_rows = u_ref.shape[0]
+    for n in range(count_y):
+        u_ref[main_rows + n : main_rows + n + 1, :] = edge_ref[n, pl.ds(first_term + step, 1), :]
+    if main_rows + count_y < all_rows:
+        u_ref[main_rows + count_y :, :] = jnp.zeros_like(u_ref[main_rows + count_y :, :])
+
+    @pl.loop(0, all_rows // 16)
     def _(part):
-        rows = pl.ds(pl.multiple_of(part * 64, 64), 64)
-        high, low = split(u_ref[rows, :])
-        u_both_ref[rows, :] = high
-        u_both_ref[pl.ds(pl.multiple_of(count_y * half + part * 64, 64), 64), :] = low
+        high, low = split(u_ref[pl.ds(pl.multiple_of(part * 16, 16), 16), :])
+        u_both_ref[pl.ds(pl.multiple_of(part * 16, 16), 16), :] = high
+        u_both_ref[pl.ds(pl.multiple_of(all_rows + part * 16, 16), 16), :] = low
 
     lane_index = lax.broadcasted_iota(jnp.int32, (8, lanes_out), 1)
     row_index = lax.broadcasted_iota(jnp.int32, (8, lanes_out), 0)
@@ -357,7 +360,7 @@
     for part in range(2 * length_x // 256):
         cols = slice(part * 256, part * 256 + 256)
         result = dot_stacked(u_both_ref[...], high_ref[:, cols], low_ref[:, cols])
-        edges = [edge_out_ref[pl.ds(n * first_ref.shape[1] + step + first_term, 1), cols] for n in range(count_y)]
+        edges = [result[main_rows + n : main_rows + n + 1] for n in range(count_y)]
         for k in range(count):
             q = part * count + k
             inside = slice(k * lanes_out, (k + 1) * lanes_out)
@@ -378,6 +381,7 @@
     high, low = halves(inverse_x_table(blocks, length_x))
     high, low = jnp.asarray(high), jnp.asarray(low)
     rows = count_y * half
+    spare = count_y + -count_y % 16
     others = [each for each in others if each[0] < end_term and each[1] > first_term]
 
     def piece_spec(start, end):
@@ -405,9 +409,8 @@
             pltpu.VMEM((length_y, 2, half, length_x), F32),
             pltpu.VMEM((length_y, 8, length_x), F32),
             pltpu.VMEM((count_y, first.shape[1], 2 * length_x), F32),
-            pltpu.VMEM((count_y * first.shape[1], 2 * length_x), F32),
-            pltpu.VMEM((rows, 2 * length_x), F32),
-            pltpu.VMEM((2 * rows, 2 * length_x), BF16),
+            pltpu.VMEM((rows + spare, 2 * length_x), F32),
+            pltpu.VMEM((2 * (rows + spare), 2 * length_x), BF16),
         ],
         compiler_params=params(1),
         cost_estimate=cost(terms * 24 * rows * length_x * length_x, terms * 16 * rows * length_x),
@@ -515,13 +518,9 @@
         yield dim, low, high
 
 
-def halos_of(heat):
-    return [side for _, low, high in padded_by_one(heat, (("term", 0), ("pencil", 1))) for side in (low, high)]
-
-
-def heat_step(heat, halos, perfuse):
+def heat_step(heat, perfuse):
     near = jnp.zeros_like(heat)
-    for dim, (low, high) in enumerate(zip(halos[::2], halos[1::2])):
+    for dim, low, high in padded_by_one(heat, (("term", 0), ("pencil", 1))):
         size = heat.shape[dim]
         near = near + jnp.concatenate([low, lax.slice_in_dim(heat, 0, size - 1, axis=dim)], axis=dim)
         near = near + jnp.concatenate([lax.slice_in_dim(heat, 1, size, axis=dim), high], axis=dim)
@@ -530,18 +529,29 @@
     return heat + DIFFUSION * (near - 6.0 * heat) - perfuse * heat
 
 
-def update_kernel(fresh_ref, old_ref, dose_ref, heat_ref, absorb_ref, pressure_ref, source_ref, out_ref):
+def update_kernel(
+    fresh_ref, old_ref, dose_ref, heat_ref, absorb_ref,
+    pressure_ref, source_ref, out_ref, low_ref, high_ref, below_ref, above_ref,
+):
+    width, rows, _ = fresh_ref.shape
     field = fresh_ref[...] - old_ref[...]
     source = absorb_ref[...] * (dose_ref[...] + field * field)
+    heat = heat_ref[...] + source
     pressure_ref[...] = field
     source_ref[...] = source
-    out_ref[...] = heat_ref[...] + source
+    out_ref[...] = heat
+    low_ref[...] = heat[:, :1]
+    high_ref[...] = heat[:, rows - 1 :]
+    below_ref[...] = heat[:1]
+    above_ref[...] = heat[width - 1 :]
 
 
 def update(fresh, old, dose, heat, absorb):
+    width, rows, length_z = fresh.shape
+    shapes = [fresh.shape] * 3 + [(width, 1, length_z)] * 2 + [(1, rows, length_z)] * 2
     return pl.pallas_call(
         update_kernel,
-        out_shape=[jax.ShapeDtypeStruct(fresh.shape, F32)] * 3,
+        out_shape=[jax.ShapeDtypeStruct(shape, F32) for shape in shapes],
         compiler_params=params(),
         cost_estimate=cost(5 * fresh.size, 32 * fresh.size),
         name="update",
@@ -575,18 +585,24 @@
             out_ref[w] = fresh
 
 
-def halo(heat, lowest):
-    (_, low, high), = padded_by_one(heat, (("pencil", 1),))
+def edges_of(heat):
+    return heat[:, :1], heat[:, -1:], heat[:1], heat[-1:]
+
+
+def halo(edges, lowest):
+    count = lax.axis_size("pencil")
+    low = lax.ppermute(edges[1], "pencil", [(i, i + 1) for i in range(count - 1)])
+    high = lax.ppermute(edges[0], "pencil", [(i + 1, i) for i in range(count - 1)])
     if not lowest:
         return [low, high]
     backward = [(i + 1, i) for i in range(lax.axis_size("term") - 1)]
-    return [low, high, lax.ppermute(heat[:1], "term", backward)]
-
-
-def warm(heats, sources, sides, perfuse, turned):
+    return [low, high, lax.ppermute(edges[2], "term", backward)]
+
+
+def warm(heats, sources, sides, top, perfuse, turned):
     width, rows, length_z = perfuse.shape
     above = sides[0][2]
-    below = lax.ppermute(heats[-1][-1:], "term", [(i, i + 1) for i in range(lax.axis_size("term") - 1)])
+    below = lax.ppermute(top, "term", [(i, i + 1) for i in range(lax.axis_size("term") - 1)])
     return pl.pallas_call(
         functools.partial(warm_kernel, groups=len(heats), turned=turned),
         out_shape=jax.ShapeDtypeStruct((rows, width, length_z) if turned else perfuse.shape, F32),
@@ -633,17 +649,15 @@
     sent, multiplier = lax.optimization_barrier((sent, spectral_multiplier))
     sent = exchange(sent)
     lowest = spectral_multiplier[:, :, 0, :]
-    thermal = jnp.transpose(thermal_increase, (1, 0, 2))
     others, before = [], None
     for start, end in ((0, middle), (middle, terms)):
         if end > start:
             mirrored = mirror(multiplier, start, end)
             if others:
-                mirrored, before, lowest, *halos = lax.optimization_barrier((mirrored, before, lowest, *halos))
+                mirrored, before, lowest = lax.optimization_barrier((mirrored, before, lowest))
                 others = [(*others[0][:2], before)]
             else:
-                mirrored, lowest, thermal = lax.optimization_barrier((mirrored, lowest, thermal))
-                halos = halos_of(thermal)
+                mirrored, lowest = lax.optimization_barrier((mirrored, lowest))
             before = lax.ppermute(mirrored, "pencil", opposite)
             if not others:
                 lowest = lowest + lax.ppermute(
@@ -733,7 +747,7 @@
         )
         for at in range(2)
     ]
-    heat = heat_step(thermal, halos, perfuse)
+    heat = heat_step(jnp.transpose(thermal_increase, (1, 0, 2)), perfuse)
 
     previous = cut_up(to_brick(prior_acoustic))
     current = cut_up(to_brick(present_acoustic))
@@ -751,15 +765,18 @@
         if ahead:
             sides.append(ahead)
         updated.append(update(fresh, *rest))
-        ahead = halo(updated[-1][2], not sides)
+        ahead = halo(updated[-1][3:], not sides)
     sides.append(ahead)
     pressure = jnp.concatenate([each[0] for each in updated], axis=0)
     sources = [each[1] for each in updated]
     heats = [each[2] for each in updated]
+    top = updated[-1][6]
     for _ in range(HEAT_STEPS - 2):
-        heats = cut_up(warm(heats, sources, sides, perfuse, False))
-        sides = [halo(each, index == 0) for index, each in enumerate(heats)]
-    return jnp.transpose(pressure, (1, 0, 2)), warm(heats, sources, sides, perfuse, True)
+        heats = cut_up(warm(heats, sources, sides, top, perfuse, False))
+        edges = [edges_of(each) for each in heats]
+        sides = [halo(each, index == 0) for index, each in enumerate(edges)]
+        top = edges[-1][3]
+    return jnp.transpose(pressure, (1, 0, 2)), warm(heats, sources, sides, top, perfuse, True)
 
 
 def solution(mesh):

time: 527 us -> 519 us (0.985)
    ppermute x2 -> x6, starting transfers between devices: 5.75 us -> 15.8 us  [the longest x2 6.21 us: halo(): lax.ppermute(edges[1], 'pencil', [(i, i + 1) for i in range(count - 1)])]
    ppermute x4 -> x2, starting transfers between devices: 15.4 us -> 6.89 us  [padded_by_one(): lax.ppermute(lax.slice_in_dim(block, size - 1, size, axis=dim), axis, for...]
    all_to_all x6, waiting for transfers between devices: 125 us -> 117 us  [exchange(): return lax.all_to_all(values, 'pencil', 0, 0, tiled=True)]
  transfers between devices with their start and end apart: 28 -> 28, of which waited for: 15 -> 15; matrix products, arithmetic and copies ran while one was open for 7% -> 6% of each run, Pallas kernels for 22% -> 22%
where the time goes in v6:
time: 519 us; the launch traced here: 516 us
  waiting for transfers between devices  232 us (45%)
  Pallas kernels  141 us (27%)
  starting transfers between devices  67.4 us (13%)
  local copies, waits for them, and re-layouts  29.1 us (6%)
  blocking collectives  21.9 us (4%)
  between operations  14.4 us (3%)
  other arithmetic  10.4 us (2%)
    all_to_all x6, waiting for transfers between devices, exchange(): return lax.all_to_all(values, 'pencil', 0, 0, tiled=True)  117 us
    pallas_call x5, Pallas kernels, spread(): pl.pallas_call(functools.partial(spread_kernel, spans=spans, counts=[len(...  74.9 us
    ppermute x1, waiting for transfers between devices, on_device(): lax.ppermute(flip(flip(lowest, 1), 2), 'pencil', [(p, blocks - p) for p i...  35.2 us
    ppermute x3, waiting for transfers between devices, gathered(): lax.ppermute(part, 'term', [(i, (i - d) % term_count) for i in range(term...  33.6 us
    all_to_all x6, starting transfers between devices, exchange(): return lax.all_to_all(values, 'pencil', 0, 0, tiled=True)  31.5 us
    pallas_call x4, Pallas kernels, gather(): pl.pallas_call(gather_kernel, grid=(holders,), in_specs=[chunk_spec(chunk...  30.7 us
    all_to_all x2, blocking collectives, exchange(): return lax.all_to_all(values, 'pencil', 0, 0, tiled=True)  21.9 us
    unnamed x42, local copies, waits for them, and re-layouts  21 us
  transfers between devices with their start and end apart: 28, of which 15 were waited for; matrix products, arithmetic and copies ran while one was open for 6% of the time, Pallas kernels for 22%

profile of v6, /device:TPU:11, one launch (start us, length us, event | category | flops | bytes accessed | tf_op | source)
XLA Modules:
  0.0 515.5 jit_solution(389147825545626742)
XLA Ops:
  9.9 3.0 forward_z.3
  12.9 4.6 all-to-all-start
  18.9 4.8 mirror.3
  27.2 3.7 forward_x.3
  34.0 4.8 mirror.2
  38.8 35.2 %collective-permute-done.1 = f32[4,16,512]{2,0,1:T(4,128)S(1)} collective-permute-done((f32[4,16,512]{2,0,1:T(4,128)S(1)}, f32[4,16,512]{2,0,1:T(4,128)S(1)}, u32[]{:S(2)}, u32[]{:S(2)}) %collective-permute-start.1) | collective-permute-done | bytes 131104 | tf_op jit(solution)/shard_map/ppermute | solution.py:663
  74.1 11.6 %copy.67 = f32[4,64,16,512]{3,1,2,0:T(8,128)} copy(f32[4,64,16,512]{3,2,1,0:T(8,128)} %param.47) | data formatting | bytes 16777216 | tf_op args[2]
  86.4 16.0 %spread.5 = f32[8,2,16,32,128]{4,3,2,1,0:T(8,128)} custom-call(f32[4,264,512]{2,1,0:T(8,128)} %bitcast.43, s32[1]{0:T(128)} %bitcast.2.refs_1_.refs_5_, f32[16,8,512]{2,1,0:T(8,128)} %pad.8.refs_2_.refs_6_, f32[4,16,64,512]{3,2,1,0:T(8,128)} %refs_7_.3, f32[2,16,32,512]{3,2,1,0:T(8,128)} %collective-permute-done.refs_4_.refs_8_, ...), custom_call_target="tpu_custom_call" | custom-call | flops 6442450944 | bytes 8388608 | tf_op jit(solution)/shard_map/spread/pallas_call | solution.py:392
  102.4 19.7 %collective-permute-done.2.refs_4_.refs_9_ = f32[2,16,32,512]{3,2,1,0:T(8,128)S(1)} collective-permute-done((f32[2,16,32,512]{3,2,1,0:T(8,128)}, f32[2,16,32,512]{3,2,1,0:T(8,128)S(1)}, u32[]{:S(2)}, u32[]{:S(2)}) %collective-permute-start.2) | collective-permute-done | bytes 2097184 | tf_op jit(solution)/shard_map/ppermute | solution.py:661
  123.4 5.6 %all-to-all-start.1 = ((f32[8,2,16,32,128]{4,3,2,1,0:T(8,128)}), f32[8,2,16,32,128]{4,3,2,1,0:T(8,128)}, u32[]{:S(2)}, u32[]{:S(2)}) async-start(f32[8,2,16,32,128]{4,3,2,1,0:T(8,128)} %spread.5), calls=%async_computation.1 | async-start | bytes 8388608 | tf_op jit(solution)/shard_map/all_to_all | solution.py:644
  130.2 2.6 collective-permute-start.6
  132.8 3.8 collective-permute-start.5
  136.7 11.5 %spread.6 = f32[8,2,8,32,128]{4,3,2,1,0:T(8,128)} custom-call(f32[4,264,512]{2,1,0:T(8,128)} %bitcast.44, s32[1]{0:T(128)} %bitcast.2.refs_1_.refs_5_, f32[16,8,512]{2,1,0:T(8,128)} %pad.8.refs_2_.refs_6_, f32[4,16,64,512]{3,2,1,0:T(8,128)} %refs_7_.3, f32[2,16,32,512]{3,2,1,0:T(8,128)} %copy-done.1, bf16[1024,1024]{1,0:T(8,128)(2,1)} %constant.49.clone.refs_5_.refs_10_, ...), custom_call_target="tpu_custom_call" | custom-call | flops 3221225472 | bytes 4194304 | tf_op jit(solution)/shard_map/spread/pallas_call | solution.py:392
  148.2 28.4 %all-to-all-done.1.refs_0_ = f32[8,2,16,32,128]{4,3,2,1,0:T(8,128)} async-done(((f32[8,2,16,32,128]{4,3,2,1,0:T(8,128)}), f32[8,2,16,32,128]{4,3,2,1,0:T(8,128)}, u32[]{:S(2)}, u32[]{:S(2)}) %all-to-all-start.1) | async-done | bytes 4194336 | tf_op jit(solution)/shard_map/all_to_all | solution.py:644
  176.6 5.1 all-to-all-start.2
  181.7 2.5 collective-permute-start.4
  184.3 3.0 collective-permute-start.3
  188.1 2.9 select_bitcast_fusion.1
  191.1 2.8 select_bitcast_fusion
  194.0 3.2 fusion.5
  197.2 11.5 %spread.7 = f32[8,2,8,32,128]{4,3,2,1,0:T(8,128)} custom-call(f32[4,264,512]{2,1,0:T(8,128)} %bitcast.45, s32[1]{0:T(128)} %bitcast.2.refs_1_.refs_5_, f32[16,8,512]{2,1,0:T(8,128)} %pad.8.refs_2_.refs_6_, f32[4,16,64,512]{3,2,1,0:T(8,128)} %refs_7_.3, f32[2,16,32,512]{3,2,1,0:T(8,128)} %copy-done.1, bf16[1024,1024]{1,0:T(8,128)(2,1)} %constant.49.clone.refs_5_.refs_10_, ...), custom_call_target="tpu_custom_call" | custom-call | flops 3221225472 | bytes 4194304 | tf_op jit(solution)/shard_map/spread/pallas_call | solution.py:392
  210.1 5.0 all-to-all-start.3
  215.1 7.7 %gather_z.5 = f32[8,64,512]{2,1,0:T(8,128)} custom-call(f32[8,2,16,32,128]{4,3,2,1,0:T(8,128)} %all-to-all-done.1.refs_0_, f32[8,2,8,32,128]{4,3,2,1,0:T(8,128)} %copy-done, f32[4,16,64,512]{3,2,1,0:T(8,128)} %bitcast.34, bf16[512,512]{1,0:T(8,128)(2,1)} %constant.51.clone.refs_3_.refs_2_, bf16[512,512]{1,0:T(8,128)(2,1)} %constant.52.clone.refs_4_.refs_3_), custom_call_target="tpu_custom_call" | custom-call | flops 3221225472 | bytes 8388608 | tf_op jit(solution)/shard_map/gather_z/pallas_call | solution.py:453
  222.8 17.4 %all-to-all-done.3.refs_1_ = f32[8,2,8,32,128]{4,3,2,1,0:T(8,128)} async-done(((f32[8,2,8,32,128]{4,3,2,1,0:T(8,128)}), f32[8,2,8,32,128]{4,3,2,1,0:T(8,128)}, u32[]{:S(2)}, u32[]{:S(2)}) %all-to-all-start.3) | async-done | bytes 2097184 | tf_op jit(solution)/shard_map/all_to_all | solution.py:644
  240.2 7.7 %gather_z.4 = f32[8,64,512]{2,1,0:T(8,128)} custom-call(f32[8,2,16,32,128]{4,3,2,1,0:T(8,128)} %all-to-all-done.1.refs_0_, f32[8,2,8,32,128]{4,3,2,1,0:T(8,128)} %all-to-all-done.3.refs_1_, f32[4,16,64,512]{3,2,1,0:T(8,128)} %bitcast.35, bf16[512,512]{1,0:T(8,128)(2,1)} %constant.51.clone.refs_3_.refs_2_, bf16[512,512]{1,0:T(8,128)(2,1)} %constant.52.clone.refs_4_.refs_3_), custom_call_target="tpu_custom_call" | custom-call | flops 3221225472 | bytes 8388608 | tf_op jit(solution)/shard_map/gather_z/pallas_call | solution.py:453
  249.1 2.6 forward_z.4
  251.6 11.3 %all_to_all.40.data_ref = f32[8,72,128]{2,1,0:T(8,128)} all-to-all(f32[8,72,128]{2,1,0:T(8,128)} %get-tuple-element.76), channel_id=1, replica_groups=mesh['term'=4,'pencil'=8] {'pencil'}, dimensions={0} | all-to-all | bytes 589824 | tf_op jit(solution)/shard_map/all_to_all | solution.py:644
  263.0 3.1 forward_x.4
  266.1 10.3 %reduce-scatter.5.cloned.1.call-done.refs_0_ = f32[2,64,512]{2,1,0:T(8,128)} async-done(((f32[8,64,512]{2,1,0:T(8,128)}), f32[2,64,512]{2,1,0:T(8,128)}) %reduce-scatter.5.cloned.1.call-update) | async-done | bytes 262160 | tf_op jit(solution)/shard_map/reduce_scatter | solution.py:692
  276.4 2.6 forward_z.5
  279.0 10.6 %all_to_all.41.data_ref = f32[8,72,128]{2,1,0:T(8,128)} all-to-all(f32[8,72,128]{2,1,0:T(8,128)} %get-tuple-element.79), channel_id=1, replica_groups=mesh['term'=4,'pencil'=8] {'pencil'}, dimensions={0} | all-to-all | bytes 589824 | tf_op jit(solution)/shard_map/all_to_all | solution.py:644
  289.6 3.1 forward_x.5.refs_1_
  297.1 16.0 %collective-permute-done.9.refs_4_ = f32[136,512]{1,0:T(8,128)S(1)} collective-permute-done((f32[136,512]{1,0:T(8,128)}, f32[136,512]{1,0:T(8,128)S(1)}, u32[]{:S(2)}, u32[]{:S(2)}) %collective-permute-start.9) | collective-permute-done | bytes 278560 | tf_op jit(solution)/shard_map/ppermute | solution.py:680
  313.2 15.5 %collective-permute-done.8.refs_3_ = f32[136,512]{1,0:T(8,128)S(1)} collective-permute-done((f32[136,512]{1,0:T(8,128)}, f32[136,512]{1,0:T(8,128)S(1)}, u32[]{:S(2)}, u32[]{:S(2)}) %collective-permute-start.8) | collective-permute-done | bytes 278560 | tf_op jit(solution)/shard_map/ppermute | solution.py:680
  331.5 17.9 %spread.8 = f32[8,4,8,32,128]{4,3,2,1,0:T(8,128)} custom-call(f32[4,136,512]{2,1,0:T(8,128)} %bitcast.54, f32[136,512]{1,0:T(8,128)} %forward_x.5.refs_1_, f32[136,512]{1,0:T(8,128)} %copy-done.16, f32[136,512]{1,0:T(8,128)} %copy-done.15, f32[136,512]{1,0:T(8,128)} %copy-done.14, s32[1]{0:T(128)} %bitcast.2.refs_1_.refs_5_, ...), custom_call_target="tpu_custom_call" | custom-call | flops 6442450944 | bytes 8388608 | tf_op jit(solution)/shard_map/spread/pallas_call | solution.py:392
  349.4 5.2 %all-to-all-start.6 = ((f32[8,4,8,32,128]{4,3,2,1,0:T(8,128)}), f32[8,4,8,32,128]{4,3,2,1,0:T(8,128)}, u32[]{:S(2)}, u32[]{:S(2)}) async-start(f32[8,4,8,32,128]{4,3,2,1,0:T(8,128)} %spread.8), calls=%async_computation.8 | async-start | bytes 8388608 | tf_op jit(solution)/shard_map/all_to_all | solution.py:644
  354.6 18.0 %spread.9 = f32[8,4,8,32,128]{4,3,2,1,0:T(8,128)} custom-call(f32[4,136,512]{2,1,0:T(8,128)} %bitcast.55, f32[136,512]{1,0:T(8,128)} %forward_x.5.refs_1_, f32[136,512]{1,0:T(8,128)} %copy-done.16, f32[136,512]{1,0:T(8,128)} %copy-done.15, f32[136,512]{1,0:T(8,128)} %copy-done.14, s32[1]{0:T(128)} %bitcast.2.refs_1_.refs_5_, ...), custom_call_target="tpu_custom_call" | custom-call | flops 6442450944 | bytes 8388608 | tf_op jit(solution)/shard_map/spread/pallas_call | solution.py:392
  372.6 29.6 %all-to-all-done.6.refs_0_ = f32[8,4,8,32,128]{4,3,2,1,0:T(8,128)} async-done(((f32[8,4,8,32,128]{4,3,2,1,0:T(8,128)}), f32[8,4,8,32,128]{4,3,2,1,0:T(8,128)}, u32[]{:S(2)}, u32[]{:S(2)}) %all-to-all-start.6) | async-done | bytes 4194336 | tf_op jit(solution)/shard_map/all_to_all | solution.py:644
  402.2 6.1 %all-to-all-start.7 = ((f32[8,4,8,32,128]{4,3,2,1,0:T(8,128)}), f32[8,4,8,32,128]{4,3,2,1,0:T(8,128)}, u32[]{:S(2)}, u32[]{:S(2)}) async-start(f32[8,4,8,32,128]{4,3,2,1,0:T(8,128)} %spread.9), calls=%async_computation.10 | async-start | bytes 8388608 | tf_op jit(solution)/shard_map/all_to_all | solution.py:644
  408.3 7.7 %gather_z.6 = f32[8,64,512]{2,1,0:T(8,128)} custom-call(f32[8,4,8,32,128]{4,3,2,1,0:T(8,128)} %all-to-all-done.6.refs_0_, f32[4,16,64,512]{3,2,1,0:T(8,128)} %bitcast.36, bf16[512,512]{1,0:T(8,128)(2,1)} %constant.51.clone.refs_3_.refs_2_, bf16[512,512]{1,0:T(8,128)(2,1)} %constant.52.clone.refs_4_.refs_3_), custom_call_target="tpu_custom_call" | custom-call | flops 3221225472 | bytes 8388608 | tf_op jit(solution)/shard_map/gather_z/pallas_call | solution.py:453
  416.1 39.9 %all-to-all-done.7.refs_0_ = f32[8,4,8,32,128]{4,3,2,1,0:T(8,128)} async-done(((f32[8,4,8,32,128]{4,3,2,1,0:T(8,128)}), f32[8,4,8,32,128]{4,3,2,1,0:T(8,128)}, u32[]{:S(2)}, u32[]{:S(2)}) %all-to-all-start.7) | async-done | bytes 4194336 | tf_op jit(solution)/shard_map/all_to_all | solution.py:644
  456.0 7.6 %gather_z.7 = f32[8,64,512]{2,1,0:T(8,128)} custom-call(f32[8,4,8,32,128]{4,3,2,1,0:T(8,128)} %all-to-all-done.7.refs_0_, f32[4,16,64,512]{3,2,1,0:T(8,128)} %bitcast.37, bf16[512,512]{1,0:T(8,128)(2,1)} %constant.51.clone.refs_3_.refs_2_, bf16[512,512]{1,0:T(8,128)(2,1)} %constant.52.clone.refs_4_.refs_3_), custom_call_target="tpu_custom_call" | custom-call | flops 3221225472 | bytes 8388608 | tf_op jit(solution)/shard_map/gather_z/pallas_call | solution.py:453
  470.7 3.5 collective-permute-start.10
  476.2 4.1 collective-permute-done.11.refs_6_
  481.1 9.2 %reduce-scatter.11.cloned.1.call-done.fresh_ref = f32[2,64,512]{2,1,0:T(8,128)} async-done(((f32[8,64,512]{2,1,0:T(8,128)}), f32[2,64,512]{2,1,0:T(8,128)}) %reduce-scatter.11.cloned.1.call-update) | async-done | bytes 262160 | tf_op jit(solution)/shard_map/reduce_scatter | solution.py:692
  492.7 3.8 collective-permute-start.15
  496.5 2.8 collective-permute-start.13
  505.9 2.7 warm.1
  (100 shorter events, 43.7 us)
Async XLA Ops:
  12.9 13.5 %all-to-all-start = ((f32[8,72,256]{2,1,0:T(8,128)}), f32[8,72,256]{2,1,0:T(8,128)S(1)}, u32[]{:S(2)}, u32[]{:S(2)}) async-start(f32[8,72,256]{2,1,0:T(8,128)} %forward_z.3), calls=%async_computation | async-start | bytes 1179648 | tf_op jit(solution)/shard_map/all_to_all | solution.py:644
  17.5 68.9 %all-gather.5.cloned.1.call-start = ((), (), s32[]{:S(2)}) async-start(), calls=%async_computation.16 | async-start | bytes 2703360 | tf_op jit(solution)/shard_map/all_gather | solution.py:695
  23.7 50.3 %collective-permute-start = (f32[2,16,32,512]{3,2,1,0:T(8,128)}, f32[2,16,32,512]{3,2,1,0:T(8,128)}, u32[]{:S(2)}, u32[]{:S(2)}) collective-permute-start(f32[2,16,32,512]{3,2,1,0:T(8,128)} %mirror.3), channel_id=1, source_target_pairs={{0,7},{1,6},{2,5},{3,4},{4,3},{5,2},{6,1},{7,0},{8,15},{9,14},{10,... | collective-permute-start | bytes 6291464 | tf_op jit(solution)/shard_map/ppermute | solution.py:661
  26.4 0.8 copy-start.3
  31.9 42.1 %collective-permute-start.1 = (f32[4,16,512]{2,0,1:T(4,128)S(1)}, f32[4,16,512]{2,0,1:T(4,128)S(1)}, u32[]{:S(2)}, u32[]{:S(2)}) collective-permute-start(f32[4,16,512]{2,0,1:T(4,128)S(1)} %fusion.8), channel_id=1, source_target_pairs={{1,7},{2,6},{3,5},{5,3},{6,2},{7,1},{9,15},{10,14},{11,13},{13,11}... | collective-permute-start | bytes 393224 | tf_op jit(solution)/shard_map/ppermute | solution.py:663
  74.0 48.1 %collective-permute-start.2 = (f32[2,16,32,512]{3,2,1,0:T(8,128)}, f32[2,16,32,512]{3,2,1,0:T(8,128)S(1)}, u32[]{:S(2)}, u32[]{:S(2)}) collective-permute-start(f32[2,16,32,512]{3,2,1,0:T(8,128)} %mirror.2), channel_id=1, source_target_pairs={{0,7},{1,6},{2,5},{3,4},{4,3},{5,2},{6,1},{7,0},{8,15},{9,14},{10,... | collective-permute-start | bytes 6291464 | tf_op jit(solution)/shard_map/ppermute | solution.py:661
  122.1 1.3 copy-start.1
  123.4 53.2 %all-to-all-start.1 = ((f32[8,2,16,32,128]{4,3,2,1,0:T(8,128)}), f32[8,2,16,32,128]{4,3,2,1,0:T(8,128)}, u32[]{:S(2)}, u32[]{:S(2)}) async-start(f32[8,2,16,32,128]{4,3,2,1,0:T(8,128)} %spread.5), calls=%async_computation.1 | async-start | bytes 8388608 | tf_op jit(solution)/shard_map/all_to_all | solution.py:644
  130.2 63.8 %collective-permute-start.6 = (f32[4,1,512]{2,1,0:T(1,128)S(1)}, f32[4,1,512]{2,1,0:T(1,128)S(1)}, u32[]{:S(2)}, u32[]{:S(2)}) collective-permute-start(f32[4,1,512]{2,1,0:T(1,128)S(1)} %get-tuple-element.125), channel_id=1, source_target_pairs={{1,0},{2,1},{3,2},{4,3},{5,4},{6,5},{7,6},{9,8},{10,9},{11,10},{12... | collective-permute-start | bytes 24584 | tf_op jit(solution)/shard_map/ppermute | solution.py:517
  132.8 61.1 %collective-permute-start.5 = (f32[4,1,512]{2,1,0:T(1,128)S(1)}, f32[4,1,512]{2,1,0:T(1,128)S(1)}, u32[]{:S(2)}, u32[]{:S(2)}) collective-permute-start(f32[4,1,512]{2,1,0:T(1,128)S(1)} %get-tuple-element.126), channel_id=1, source_target_pairs={{0,1},{1,2},{2,3},{3,4},{4,5},{5,6},{6,7},{8,9},{9,10},{10,11},{11... | collective-permute-start | bytes 24584 | tf_op jit(solution)/shard_map/ppermute | solution.py:516
  148.2 39.2 %copy-start.9 = (f32[3,2]{0,1:T(2,128)S(1)}, f32[3,2]{0,1:T(2,128)}, u32[]{:S(2)}) copy-start(f32[3,2]{0,1:T(2,128)} %param.50) | copy-start | bytes 76
  176.6 32.2 %all-to-all-start.2 = ((f32[8,2,8,32,128]{4,3,2,1,0:T(8,128)}), f32[8,2,8,32,128]{4,3,2,1,0:T(8,128)S(1)}, u32[]{:S(2)}, u32[]{:S(2)}) async-start(f32[8,2,8,32,128]{4,3,2,1,0:T(8,128)} %spread.6), calls=%async_computation.2 | async-start | bytes 4194304 | tf_op jit(solution)/shard_map/all_to_all | solution.py:644
  181.7 6.4 %copy-start.6 = (s32[64,4,512]{2,1,0:T(4,128)S(1)}, s32[64,4,512]{2,1,0:T(4,128)}, u32[]{:S(2)}) copy-start(s32[64,4,512]{2,1,0:T(4,128)} %param.49) | copy-start | bytes 1572868
  181.7 12.3 %collective-permute-start.4 = (f32[1,64,512]{2,1,0:T(8,128)S(1)}, f32[1,64,512]{2,1,0:T(8,128)S(1)}, u32[]{:S(2)}, u32[]{:S(2)}) collective-permute-start(f32[1,64,512]{2,1,0:T(8,128)S(1)} %get-tuple-element.129), channel_id=1, source_target_pairs={{8,0},{16,8},{24,16},{9,1},{17,9},{25,17},{10,2},{18,10},{26,18},{... | collective-permute-start | bytes 393224 | tf_op jit(solution)/shard_map/ppermute | solution.py:517
  184.3 9.7 %collective-permute-start.3 = (f32[1,64,512]{2,1,0:T(8,128)S(1)}, f32[1,64,512]{2,1,0:T(8,128)S(1)}, u32[]{:S(2)}, u32[]{:S(2)}) collective-permute-start(f32[1,64,512]{2,1,0:T(8,128)S(1)} %get-tuple-element.130), channel_id=1, source_target_pairs={{0,8},{8,16},{16,24},{1,9},{9,17},{17,25},{2,10},{10,18},{18,26},{... | collective-permute-start | bytes 393224 | tf_op jit(solution)/shard_map/ppermute | solution.py:516
  208.7 1.4 copy-start
  210.1 30.1 %all-to-all-start.3 = ((f32[8,2,8,32,128]{4,3,2,1,0:T(8,128)}), f32[8,2,8,32,128]{4,3,2,1,0:T(8,128)}, u32[]{:S(2)}, u32[]{:S(2)}) async-start(f32[8,2,8,32,128]{4,3,2,1,0:T(8,128)} %spread.7), calls=%async_computation.3 | async-start | bytes 4194304 | tf_op jit(solution)/shard_map/all_to_all | solution.py:644
  215.1 34.0 %reduce-scatter.7.cloned.1.call-start = ((), (), s32[]{:S(2)}) async-start(), calls=%async_computation.13 | async-start | bytes 1310720 | tf_op jit(solution)/shard_map/reduce_scatter | solution.py:692
  222.8 53.6 %reduce-scatter.5.cloned.1.call-start = ((), (), s32[]{:S(2)}) async-start(), calls=%async_computation.12 | async-start | bytes 1310720 | tf_op jit(solution)/shard_map/reduce_scatter | solution.py:692
  248.0 82.8 %all-gather.7.cloned.1.call-start = ((), (), s32[]{:S(2)}) async-start(), calls=%async_computation.17 | async-start | bytes 1392640 | tf_op jit(solution)/shard_map/all_gather | solution.py:678
  292.7 20.5 %collective-permute-start.9 = (f32[136,512]{1,0:T(8,128)}, f32[136,512]{1,0:T(8,128)S(1)}, u32[]{:S(2)}, u32[]{:S(2)}) collective-permute-start(f32[136,512]{1,0:T(8,128)} %forward_x.5.refs_1_), channel_id=1, source_target_pairs={{0,8},{8,16},{16,24},{24,0},{1,9},{9,17},{17,25},{25,1},{2,10},{10... | collective-permute-start | bytes 835592 | tf_op jit(solution)/shard_map/ppermute | solution.py:680
  294.6 34.1 %collective-permute-start.8 = (f32[136,512]{1,0:T(8,128)}, f32[136,512]{1,0:T(8,128)S(1)}, u32[]{:S(2)}, u32[]{:S(2)}) collective-permute-start(f32[136,512]{1,0:T(8,128)} %forward_x.5.refs_1_), channel_id=1, source_target_pairs={{0,16},{8,24},{16,0},{24,8},{1,17},{9,25},{17,1},{25,9},{2,18},{10... | collective-permute-start | bytes 835592 | tf_op jit(solution)/shard_map/ppermute | solution.py:680
  297.1 33.7 %collective-permute-start.7 = (f32[136,512]{1,0:T(8,128)}, f32[136,512]{1,0:T(8,128)S(1)}, u32[]{:S(2)}, u32[]{:S(2)}) collective-permute-start(f32[136,512]{1,0:T(8,128)} %forward_x.5.refs_1_), channel_id=1, source_target_pairs={{0,24},{8,0},{16,8},{24,16},{1,25},{9,1},{17,9},{25,17},{2,26},{10... | collective-permute-start | bytes 835592 | tf_op jit(solution)/shard_map/ppermute | solution.py:680
  313.2 17.6 %copy-start.14 = (f32[136,512]{1,0:T(8,128)}, f32[136,512]{1,0:T(8,128)S(1)}, u32[]{:S(2)}) copy-start(f32[136,512]{1,0:T(8,128)S(1)} %collective-permute-done.9.refs_4_) | copy-start | bytes 835588
  328.7 2.1 copy-start.15
  330.8 0.7 copy-start.16
  349.4 52.8 %all-to-all-start.6 = ((f32[8,4,8,32,128]{4,3,2,1,0:T(8,128)}), f32[8,4,8,32,128]{4,3,2,1,0:T(8,128)}, u32[]{:S(2)}, u32[]{:S(2)}) async-start(f32[8,4,8,32,128]{4,3,2,1,0:T(8,128)} %spread.8), calls=%async_computation.8 | async-start | bytes 8388608 | tf_op jit(solution)/shard_map/all_to_all | solution.py:644
  402.2 53.7 %all-to-all-start.7 = ((f32[8,4,8,32,128]{4,3,2,1,0:T(8,128)}), f32[8,4,8,32,128]{4,3,2,1,0:T(8,128)}, u32[]{:S(2)}, u32[]{:S(2)}) async-start(f32[8,4,8,32,128]{4,3,2,1,0:T(8,128)} %spread.9), calls=%async_computation.10 | async-start | bytes 8388608 | tf_op jit(solution)/shard_map/all_to_all | solution.py:644
  408.3 58.2 %reduce-scatter.9.cloned.1.call-start = ((), (), s32[]{:S(2)}) async-start(), calls=%async_computation.14 | async-start | bytes 1310720 | tf_op jit(solution)/shard_map/reduce_scatter | solution.py:692
  416.0 47.6 %copy-start.2 = (f32[64,4,512]{2,0,1:T(8,128)S(1)}, f32[64,4,512]{2,0,1:T(8,128)}, u32[]{:S(2)}) copy-start(f32[64,4,512]{2,0,1:T(8,128)} %copy.69) | copy-start | bytes 1572868
  416.1 74.3 %reduce-scatter.11.cloned.1.call-start = ((), (), s32[]{:S(2)}) async-start(), calls=%async_computation.15 | async-start | bytes 1310720 | tf_op jit(solution)/shard_map/reduce_scatter | solution.py:692
  463.6 1.2 copy-start.5
  463.6 2.0 copy-start.4
  468.8 12.3 %collective-permute-start.12 = (f32[1,64,512]{2,1,0:T(8,128)}, f32[1,64,512]{2,1,0:T(8,128)S(1)}, u32[]{:S(2)}, u32[]{:S(2)}) collective-permute-start(f32[1,64,512]{2,1,0:T(8,128)} %get-tuple-element.95), channel_id=1, source_target_pairs={{8,0},{16,8},{24,16},{9,1},{17,9},{25,17},{10,2},{18,10},{26,18},{... | collective-permute-start | bytes 393224 | tf_op jit(solution)/shard_map/ppermute | solution.py:599
  470.7 5.4 %collective-permute-start.10 = (f32[2,1,512]{2,1,0:T(1,128)}, f32[2,1,512]{2,1,0:T(1,128)S(1)}, u32[]{:S(2)}, u32[]{:S(2)}) collective-permute-start(f32[2,1,512]{2,1,0:T(1,128)} %get-tuple-element.93), channel_id=1, source_target_pairs={{0,1},{1,2},{2,3},{3,4},{4,5},{5,6},{6,7},{8,9},{9,10},{10,11},{11... | collective-permute-start | bytes 12296 | tf_op jit(solution)/shard_map/ppermute | solution.py:594
  474.2 6.0 %collective-permute-start.11 = (f32[2,1,512]{2,1,0:T(1,128)}, f32[2,1,512]{2,1,0:T(1,128)S(1)}, u32[]{:S(2)}, u32[]{:S(2)}) collective-permute-start(f32[2,1,512]{2,1,0:T(1,128)} %get-tuple-element.94), channel_id=1, source_target_pairs={{1,0},{2,1},{3,2},{4,3},{5,4},{6,5},{7,6},{9,8},{10,9},{11,10},{12... | collective-permute-start | bytes 12296 | tf_op jit(solution)/shard_map/ppermute | solution.py:595
  476.1 29.1 %copy-start.10 = (f32[2,1,512]{2,1,0:T(1,128)}, f32[2,1,512]{2,1,0:T(1,128)S(1)}, u32[]{:S(2)}) copy-start(f32[2,1,512]{2,1,0:T(1,128)S(1)} %collective-permute-done.10.refs_4_) | copy-start | bytes 12292
  480.2 25.0 %copy-start.11 = (f32[2,1,512]{2,1,0:T(1,128)}, f32[2,1,512]{2,1,0:T(1,128)S(1)}, u32[]{:S(2)}) copy-start(f32[2,1,512]{2,1,0:T(1,128)S(1)} %collective-permute-done.11.refs_6_) | copy-start | bytes 12292
  481.1 24.1 %copy-start.7 = (f32[1,64,512]{2,1,0:T(8,128)}, f32[1,64,512]{2,1,0:T(8,128)S(1)}, u32[]{:S(2)}) copy-start(f32[1,64,512]{2,1,0:T(8,128)S(1)} %collective-permute-done.12.refs_9_) | copy-start | bytes 393220
  492.7 12.6 %collective-permute-start.15 = (f32[1,64,512]{2,1,0:T(8,128)}, f32[1,64,512]{2,1,0:T(8,128)S(1)}, u32[]{:S(2)}, u32[]{:S(2)}) collective-permute-start(f32[1,64,512]{2,1,0:T(8,128)} %get-tuple-element.107), channel_id=1, source_target_pairs={{0,8},{8,16},{16,24},{1,9},{9,17},{17,25},{2,10},{10,18},{18,26},{... | collective-permute-start | bytes 393224 | tf_op jit(solution)/shard_map/ppermute | solution.py:605
  496.5 6.9 %collective-permute-start.13 = (f32[2,1,512]{2,1,0:T(1,128)}, f32[2,1,512]{2,1,0:T(1,128)S(1)}, u32[]{:S(2)}, u32[]{:S(2)}) collective-permute-start(f32[2,1,512]{2,1,0:T(1,128)} %get-tuple-element.104), channel_id=1, source_target_pairs={{0,1},{1,2},{2,3},{3,4},{4,5},{5,6},{6,7},{8,9},{9,10},{10,11},{11... | collective-permute-start | bytes 12296 | tf_op jit(solution)/shard_map/ppermute | solution.py:594
  499.2 6.0 %collective-permute-start.14 = (f32[2,1,512]{2,1,0:T(1,128)}, f32[2,1,512]{2,1,0:T(1,128)S(1)}, u32[]{:S(2)}, u32[]{:S(2)}) collective-permute-start(f32[2,1,512]{2,1,0:T(1,128)} %get-tuple-element.106), channel_id=1, source_target_pairs={{1,0},{2,1},{3,2},{4,3},{5,4},{6,5},{7,6},{9,8},{10,9},{11,10},{12... | collective-permute-start | bytes 12296 | tf_op jit(solution)/shard_map/ppermute | solution.py:595
  503.4 1.9 copy-start.12
  505.3 0.6 copy-start.13
  505.3 0.6 copy-start.8
Sparse Core Ops, SparseCore 0:
  31.0 45.0 all-gather.4
  222.9 25.2 reduce-scatter.6
  250.6 25.7 reduce-scatter.4
  277.8 37.3 all-gather.6
  416.2 24.4 reduce-scatter.8
  463.8 26.5 reduce-scatter.10

commit v7 on v6

--- a/solution.py
+++ b/solution.py
@@ -518,9 +518,13 @@
         yield dim, low, high
 
 
-def heat_step(heat, perfuse):
+def halos_of(heat):
+    return [side for _, low, high in padded_by_one(heat, (("term", 0), ("pencil", 1))) for side in (low, high)]
+
+
+def heat_step(heat, halos, perfuse):
     near = jnp.zeros_like(heat)
-    for dim, low, high in padded_by_one(heat, (("term", 0), ("pencil", 1))):
+    for dim, (low, high) in enumerate(zip(halos[::2], halos[1::2])):
         size = heat.shape[dim]
         near = near + jnp.concatenate([low, lax.slice_in_dim(heat, 0, size - 1, axis=dim)], axis=dim)
         near = near + jnp.concatenate([lax.slice_in_dim(heat, 1, size, axis=dim), high], axis=dim)
@@ -691,7 +695,7 @@
         partial = gather(chunks, factor, scale, width, group)
         return lax.psum_scatter(partial, "term", scatter_dimension=0, tiled=True)
 
-    def doubled_first(part, tied):
+    def doubled_first(part, halos, warmed):
         parts = [[lax.all_gather(part, "term", axis=0, tiled=False)]]
         shared, chunks, bricks = [], {}, []
         if middle:
@@ -708,9 +712,12 @@
             out = exchange(out)
             before = [out]
             if index == 0:
-                out, *tied = lax.optimization_barrier((out, *tied))
+                out, *halos = lax.optimization_barrier((out, *halos))
+                heat = warmed(halos)
+            if index == len(spans) - 1:
+                out, heat = lax.optimization_barrier((out, heat))
             bricks.append(summed(shared + [out], group))
-        return bricks, tied
+        return bricks, heat
 
     def doubled(parts):
         bricks, before = [], []
@@ -747,12 +754,14 @@
         )
         for at in range(2)
     ]
-    heat = heat_step(jnp.transpose(thermal_increase, (1, 0, 2)), perfuse)
+    thermal = jnp.transpose(thermal_increase, (1, 0, 2))
 
     previous = cut_up(to_brick(prior_acoustic))
     current = cut_up(to_brick(present_acoustic))
     dose = []
-    doubles, (heat, absorb, perfuse) = doubled_first(forward_x(sent, width, half, rows), (heat, absorb, perfuse))
+    doubles, heat = doubled_first(
+        forward_x(sent, width, half, rows), halos_of(thermal), lambda halos: heat_step(thermal, halos, perfuse)
+    )
     for _ in range(WAVE_STEPS - 1):
         parts, states = forward(list(zip(doubles, previous, *dose)))
         previous, current = current, [field for field, _ in states]

time: 519 us -> 517 us (level)
  waiting for transfers between devices: 232 us -> 225 us
    unnamed x42 -> x40, local copies, waits for them, and re-layouts: 21 us -> 21.9 us
where the time goes in v7:
time: 517 us; the launch traced here: 515 us
  waiting for transfers between devices  225 us (44%)
  Pallas kernels  141 us (27%)
  starting transfers between devices  71.2 us (14%)
  local copies, waits for them, and re-layouts  30.6 us (6%)
  blocking collectives  21.8 us (4%)
  between operations  14.4 us (3%)
  other arithmetic  11.3 us (2%)
    all_to_all x6, waiting for transfers between devices, exchange(): return lax.all_to_all(values, 'pencil', 0, 0, tiled=True)  116 us
    pallas_call x5, Pallas kernels, spread(): pl.pallas_call(functools.partial(spread_kernel, spans=spans, counts=[len(...  75 us
    ppermute x1, waiting for transfers between devices, on_device(): lax.ppermute(flip(flip(lowest, 1), 2), 'pencil', [(p, blocks - p) for p i...  35.1 us
    ppermute x3, waiting for transfers between devices, gathered(): lax.ppermute(part, 'term', [(i, (i - d) % term_count) for i in range(term...  31.9 us
    all_to_all x6, starting transfers between devices, exchange(): return lax.all_to_all(values, 'pencil', 0, 0, tiled=True)  31.4 us
    pallas_call x4, Pallas kernels, gather(): pl.pallas_call(gather_kernel, grid=(holders,), in_specs=[chunk_spec(chunk...  30.7 us
    unnamed x40, local copies, waits for them, and re-layouts  21.9 us
    all_to_all x2, blocking collectives, exchange(): return lax.all_to_all(values, 'pencil', 0, 0, tiled=True)  21.8 us
  transfers between devices with their start and end apart: 28, of which 15 were waited for; matrix products, arithmetic and copies ran while one was open for 6% of the time, Pallas kernels for 22%

profile of v7, /device:TPU:11, one launch (start us, length us, event | category | flops | bytes accessed | tf_op | source)
XLA Modules:
  0.0 515.3 jit_solution(10906716766910946893)
XLA Ops:
  9.9 3.0 forward_z.3
  12.9 4.6 all-to-all-start
  18.9 4.8 mirror.3
  27.2 3.6 forward_x.3
  34.0 4.8 mirror.2
  38.8 35.1 %collective-permute-done.1 = f32[4,16,512]{2,0,1:T(4,128)S(1)} collective-permute-done((f32[4,16,512]{2,0,1:T(4,128)S(1)}, f32[4,16,512]{2,0,1:T(4,128)S(1)}, u32[]{:S(2)}, u32[]{:S(2)}) %collective-permute-start.1) | collective-permute-done | bytes 131104 | tf_op jit(solution)/shard_map/ppermute | solution.py:667
  74.1 11.5 %copy.67 = f32[4,64,16,512]{3,1,2,0:T(8,128)} copy(f32[4,64,16,512]{3,2,1,0:T(8,128)} %param.47) | data formatting | bytes 16777216 | tf_op args[2]
  86.3 16.0 %spread.5 = f32[8,2,16,32,128]{4,3,2,1,0:T(8,128)} custom-call(f32[4,264,512]{2,1,0:T(8,128)} %bitcast.43, s32[1]{0:T(128)} %bitcast.2.refs_1_.refs_5_, f32[16,8,512]{2,1,0:T(8,128)} %pad.8.refs_2_.refs_6_, f32[4,16,64,512]{3,2,1,0:T(8,128)} %refs_7_.3, f32[2,16,32,512]{3,2,1,0:T(8,128)} %collective-permute-done.refs_4_.refs_8_, ...), custom_call_target="tpu_custom_call" | custom-call | flops 6442450944 | bytes 8388608 | tf_op jit(solution)/shard_map/spread/pallas_call | solution.py:392
  102.3 19.7 %collective-permute-done.2.refs_4_.refs_9_ = f32[2,16,32,512]{3,2,1,0:T(8,128)S(1)} collective-permute-done((f32[2,16,32,512]{3,2,1,0:T(8,128)}, f32[2,16,32,512]{3,2,1,0:T(8,128)S(1)}, u32[]{:S(2)}, u32[]{:S(2)}) %collective-permute-start.2) | collective-permute-done | bytes 2097184 | tf_op jit(solution)/shard_map/ppermute | solution.py:665
  123.4 5.6 %all-to-all-start.1 = ((f32[8,2,16,32,128]{4,3,2,1,0:T(8,128)}), f32[8,2,16,32,128]{4,3,2,1,0:T(8,128)}, u32[]{:S(2)}, u32[]{:S(2)}) async-start(f32[8,2,16,32,128]{4,3,2,1,0:T(8,128)} %spread.5), calls=%async_computation.1 | async-start | bytes 8388608 | tf_op jit(solution)/shard_map/all_to_all | solution.py:648
  129.0 11.5 %spread.6 = f32[8,2,8,32,128]{4,3,2,1,0:T(8,128)} custom-call(f32[4,264,512]{2,1,0:T(8,128)} %bitcast.44, s32[1]{0:T(128)} %bitcast.2.refs_1_.refs_5_, f32[16,8,512]{2,1,0:T(8,128)} %pad.8.refs_2_.refs_6_, f32[4,16,64,512]{3,2,1,0:T(8,128)} %refs_7_.3, f32[2,16,32,512]{3,2,1,0:T(8,128)} %copy-done.2, bf16[1024,1024]{1,0:T(8,128)(2,1)} %constant.49.clone.refs_5_.refs_10_, ...), custom_call_target="tpu_custom_call" | custom-call | flops 3221225472 | bytes 4194304 | tf_op jit(solution)/shard_map/spread/pallas_call | solution.py:392
  140.5 36.1 %all-to-all-done.1.refs_0_ = f32[8,2,16,32,128]{4,3,2,1,0:T(8,128)} async-done(((f32[8,2,16,32,128]{4,3,2,1,0:T(8,128)}), f32[8,2,16,32,128]{4,3,2,1,0:T(8,128)}, u32[]{:S(2)}, u32[]{:S(2)}) %all-to-all-start.1) | async-done | bytes 4194336 | tf_op jit(solution)/shard_map/all_to_all | solution.py:648
  176.6 5.1 all-to-all-start.2
  183.0 3.6 collective-permute-start.3
  189.3 3.6 collective-permute-start.5
  194.9 11.5 %spread.7 = f32[8,2,8,32,128]{4,3,2,1,0:T(8,128)} custom-call(f32[4,264,512]{2,1,0:T(8,128)} %bitcast.45, s32[1]{0:T(128)} %bitcast.2.refs_1_.refs_5_, f32[16,8,512]{2,1,0:T(8,128)} %pad.8.refs_2_.refs_6_, f32[4,16,64,512]{3,2,1,0:T(8,128)} %refs_7_.3, f32[2,16,32,512]{3,2,1,0:T(8,128)} %copy-done.2, bf16[1024,1024]{1,0:T(8,128)(2,1)} %constant.49.clone.refs_5_.refs_10_, ...), custom_call_target="tpu_custom_call" | custom-call | flops 3221225472 | bytes 4194304 | tf_op jit(solution)/shard_map/spread/pallas_call | solution.py:392
  208.1 5.1 all-to-all-start.3
  213.3 7.7 %gather_z.5 = f32[8,64,512]{2,1,0:T(8,128)} custom-call(f32[8,2,16,32,128]{4,3,2,1,0:T(8,128)} %all-to-all-done.1.refs_0_, f32[8,2,8,32,128]{4,3,2,1,0:T(8,128)} %copy-done.1, f32[4,16,64,512]{3,2,1,0:T(8,128)} %bitcast.34, bf16[512,512]{1,0:T(8,128)(2,1)} %constant.51.clone.refs_3_.refs_2_, bf16[512,512]{1,0:T(8,128)(2,1)} %constant.52.clone.refs_4_.refs_3_), custom_call_target="tpu_custom_call" | custom-call | flops 3221225472 | bytes 8388608 | tf_op jit(solution)/shard_map/gather_z/pallas_call | solution.py:453
  221.8 3.9 select_bitcast_fusion.1
  225.9 4.1 fusion.5
  229.9 8.5 %all-to-all-done.3.refs_1_ = f32[8,2,8,32,128]{4,3,2,1,0:T(8,128)S(1)} async-done(((f32[8,2,8,32,128]{4,3,2,1,0:T(8,128)}), f32[8,2,8,32,128]{4,3,2,1,0:T(8,128)S(1)}, u32[]{:S(2)}, u32[]{:S(2)}) %all-to-all-start.3) | async-done | bytes 2097184 | tf_op jit(solution)/shard_map/all_to_all | solution.py:648
  239.7 7.7 %gather_z.4 = f32[8,64,512]{2,1,0:T(8,128)} custom-call(f32[8,2,16,32,128]{4,3,2,1,0:T(8,128)} %all-to-all-done.1.refs_0_, f32[8,2,8,32,128]{4,3,2,1,0:T(8,128)} %copy-done, f32[4,16,64,512]{3,2,1,0:T(8,128)} %bitcast.35, bf16[512,512]{1,0:T(8,128)(2,1)} %constant.51.clone.refs_3_.refs_2_, bf16[512,512]{1,0:T(8,128)(2,1)} %constant.52.clone.refs_4_.refs_3_), custom_call_target="tpu_custom_call" | custom-call | flops 3221225472 | bytes 8388608 | tf_op jit(solution)/shard_map/gather_z/pallas_call | solution.py:453
  248.5 2.6 forward_z.4
  251.1 11.2 %all_to_all.40.data_ref = f32[8,72,128]{2,1,0:T(8,128)} all-to-all(f32[8,72,128]{2,1,0:T(8,128)} %get-tuple-element.84), channel_id=1, replica_groups=mesh['term'=4,'pencil'=8] {'pencil'}, dimensions={0} | all-to-all | bytes 589824 | tf_op jit(solution)/shard_map/all_to_all | solution.py:648
  262.4 3.1 forward_x.4
  265.4 10.2 %reduce-scatter.5.cloned.1.call-done.refs_0_ = f32[2,64,512]{2,1,0:T(8,128)} async-done(((f32[8,64,512]{2,1,0:T(8,128)}), f32[2,64,512]{2,1,0:T(8,128)}) %reduce-scatter.5.cloned.1.call-update) | async-done | bytes 262160 | tf_op jit(solution)/shard_map/reduce_scatter | solution.py:696
  275.7 2.6 forward_z.5
  278.3 10.6 %all_to_all.41.data_ref = f32[8,72,128]{2,1,0:T(8,128)} all-to-all(f32[8,72,128]{2,1,0:T(8,128)} %get-tuple-element.87), channel_id=1, replica_groups=mesh['term'=4,'pencil'=8] {'pencil'}, dimensions={0} | all-to-all | bytes 589824 | tf_op jit(solution)/shard_map/all_to_all | solution.py:648
  288.9 3.1 forward_x.5.refs_1_
  296.2 18.4 %collective-permute-done.7.refs_2_ = f32[136,512]{1,0:T(8,128)S(1)} collective-permute-done((f32[136,512]{1,0:T(8,128)}, f32[136,512]{1,0:T(8,128)S(1)}, u32[]{:S(2)}, u32[]{:S(2)}) %collective-permute-start.7) | collective-permute-done | bytes 278560 | tf_op jit(solution)/shard_map/ppermute | solution.py:684
  314.6 7.6 %collective-permute-done.8.refs_3_ = f32[136,512]{1,0:T(8,128)S(1)} collective-permute-done((f32[136,512]{1,0:T(8,128)}, f32[136,512]{1,0:T(8,128)S(1)}, u32[]{:S(2)}, u32[]{:S(2)}) %collective-permute-start.8) | collective-permute-done | bytes 278560 | tf_op jit(solution)/shard_map/ppermute | solution.py:684
  322.1 6.0 %collective-permute-done.9.refs_4_ = f32[136,512]{1,0:T(8,128)S(1)} collective-permute-done((f32[136,512]{1,0:T(8,128)}, f32[136,512]{1,0:T(8,128)S(1)}, u32[]{:S(2)}, u32[]{:S(2)}) %collective-permute-start.9) | collective-permute-done | bytes 278560 | tf_op jit(solution)/shard_map/ppermute | solution.py:684
  328.8 17.9 %spread.8 = f32[8,4,8,32,128]{4,3,2,1,0:T(8,128)} custom-call(f32[4,136,512]{2,1,0:T(8,128)} %bitcast.54, f32[136,512]{1,0:T(8,128)} %forward_x.5.refs_1_, f32[136,512]{1,0:T(8,128)} %copy-done.13, f32[136,512]{1,0:T(8,128)} %copy-done.14, f32[136,512]{1,0:T(8,128)} %copy-done.15, s32[1]{0:T(128)} %bitcast.2.refs_1_.refs_5_, ...), custom_call_target="tpu_custom_call" | custom-call | flops 6442450944 | bytes 8388608 | tf_op jit(solution)/shard_map/spread/pallas_call | solution.py:392
  346.7 4.9 all-to-all-start.6
  351.6 18.1 %spread.9 = f32[8,4,8,32,128]{4,3,2,1,0:T(8,128)} custom-call(f32[4,136,512]{2,1,0:T(8,128)} %bitcast.55, f32[136,512]{1,0:T(8,128)} %forward_x.5.refs_1_, f32[136,512]{1,0:T(8,128)} %copy-done.13, f32[136,512]{1,0:T(8,128)} %copy-done.14, f32[136,512]{1,0:T(8,128)} %copy-done.15, s32[1]{0:T(128)} %bitcast.2.refs_1_.refs_5_, ...), custom_call_target="tpu_custom_call" | custom-call | flops 6442450944 | bytes 8388608 | tf_op jit(solution)/shard_map/spread/pallas_call | solution.py:392
  369.7 29.6 %all-to-all-done.6.refs_0_ = f32[8,4,8,32,128]{4,3,2,1,0:T(8,128)} async-done(((f32[8,4,8,32,128]{4,3,2,1,0:T(8,128)}), f32[8,4,8,32,128]{4,3,2,1,0:T(8,128)}, u32[]{:S(2)}, u32[]{:S(2)}) %all-to-all-start.6) | async-done | bytes 4194336 | tf_op jit(solution)/shard_map/all_to_all | solution.py:648
  399.3 6.0 %all-to-all-start.7 = ((f32[8,4,8,32,128]{4,3,2,1,0:T(8,128)}), f32[8,4,8,32,128]{4,3,2,1,0:T(8,128)}, u32[]{:S(2)}, u32[]{:S(2)}) async-start(f32[8,4,8,32,128]{4,3,2,1,0:T(8,128)} %spread.9), calls=%async_computation.10 | async-start | bytes 8388608 | tf_op jit(solution)/shard_map/all_to_all | solution.py:648
  405.3 7.7 %gather_z.6 = f32[8,64,512]{2,1,0:T(8,128)} custom-call(f32[8,4,8,32,128]{4,3,2,1,0:T(8,128)} %all-to-all-done.6.refs_0_, f32[4,16,64,512]{3,2,1,0:T(8,128)} %bitcast.36, bf16[512,512]{1,0:T(8,128)(2,1)} %constant.51.clone.refs_3_.refs_2_, bf16[512,512]{1,0:T(8,128)(2,1)} %constant.52.clone.refs_4_.refs_3_), custom_call_target="tpu_custom_call" | custom-call | flops 3221225472 | bytes 8388608 | tf_op jit(solution)/shard_map/gather_z/pallas_call | solution.py:453
  413.1 39.9 %all-to-all-done.7.refs_0_ = f32[8,4,8,32,128]{4,3,2,1,0:T(8,128)} async-done(((f32[8,4,8,32,128]{4,3,2,1,0:T(8,128)}), f32[8,4,8,32,128]{4,3,2,1,0:T(8,128)}, u32[]{:S(2)}, u32[]{:S(2)}) %all-to-all-start.7) | async-done | bytes 4194336 | tf_op jit(solution)/shard_map/all_to_all | solution.py:648
  453.0 7.6 %gather_z.7 = f32[8,64,512]{2,1,0:T(8,128)} custom-call(f32[8,4,8,32,128]{4,3,2,1,0:T(8,128)} %all-to-all-done.7.refs_0_, f32[4,16,64,512]{3,2,1,0:T(8,128)} %bitcast.37, bf16[512,512]{1,0:T(8,128)(2,1)} %constant.51.clone.refs_3_.refs_2_, bf16[512,512]{1,0:T(8,128)(2,1)} %constant.52.clone.refs_4_.refs_3_), custom_call_target="tpu_custom_call" | custom-call | flops 3221225472 | bytes 8388608 | tf_op jit(solution)/shard_map/gather_z/pallas_call | solution.py:453
  467.5 5.4 %collective-permute-start.12 = (f32[1,64,512]{2,1,0:T(8,128)}, f32[1,64,512]{2,1,0:T(8,128)S(1)}, u32[]{:S(2)}, u32[]{:S(2)}) collective-permute-start(f32[1,64,512]{2,1,0:T(8,128)} %get-tuple-element.102), channel_id=1, source_target_pairs={{8,0},{16,8},{24,16},{9,1},{17,9},{25,17},{10,2},{18,10},{26,18},{... | collective-permute-start | bytes 393224 | tf_op jit(solution)/shard_map/ppermute | solution.py:603
  472.9 3.7 collective-permute-start.10
  478.5 4.1 collective-permute-done.11.refs_6_
  482.6 6.4 %reduce-scatter.11.cloned.1.call-done.fresh_ref = f32[2,64,512]{2,1,0:T(8,128)} async-done(((f32[8,64,512]{2,1,0:T(8,128)}), f32[2,64,512]{2,1,0:T(8,128)}) %reduce-scatter.11.cloned.1.call-update) | async-done | bytes 262160 | tf_op jit(solution)/shard_map/reduce_scatter | solution.py:696
  489.1 2.3 update.3
  491.4 3.8 collective-permute-start.15
  495.2 3.9 collective-permute-start.13
  505.8 2.7 warm.1
  (98 shorter events, 44.2 us)
Async XLA Ops:
  12.9 13.5 %all-to-all-start = ((f32[8,72,256]{2,1,0:T(8,128)}), f32[8,72,256]{2,1,0:T(8,128)S(1)}, u32[]{:S(2)}, u32[]{:S(2)}) async-start(f32[8,72,256]{2,1,0:T(8,128)} %forward_z.3), calls=%async_computation | async-start | bytes 1179648 | tf_op jit(solution)/shard_map/all_to_all | solution.py:648
  17.5 68.8 %all-gather.5.cloned.1.call-start = ((), (), s32[]{:S(2)}) async-start(), calls=%async_computation.16 | async-start | bytes 2703360 | tf_op jit(solution)/shard_map/all_gather | solution.py:699
  23.7 50.3 %collective-permute-start = (f32[2,16,32,512]{3,2,1,0:T(8,128)}, f32[2,16,32,512]{3,2,1,0:T(8,128)}, u32[]{:S(2)}, u32[]{:S(2)}) collective-permute-start(f32[2,16,32,512]{3,2,1,0:T(8,128)} %mirror.3), channel_id=1, source_target_pairs={{0,7},{1,6},{2,5},{3,4},{4,3},{5,2},{6,1},{7,0},{8,15},{9,14},{10,... | collective-permute-start | bytes 6291464 | tf_op jit(solution)/shard_map/ppermute | solution.py:665
  26.4 0.8 copy-start.4
  31.9 42.1 %collective-permute-start.1 = (f32[4,16,512]{2,0,1:T(4,128)S(1)}, f32[4,16,512]{2,0,1:T(4,128)S(1)}, u32[]{:S(2)}, u32[]{:S(2)}) collective-permute-start(f32[4,16,512]{2,0,1:T(4,128)S(1)} %fusion.8), channel_id=1, source_target_pairs={{1,7},{2,6},{3,5},{5,3},{6,2},{7,1},{9,15},{10,14},{11,13},{13,11}... | collective-permute-start | bytes 393224 | tf_op jit(solution)/shard_map/ppermute | solution.py:667
  74.0 48.1 %collective-permute-start.2 = (f32[2,16,32,512]{3,2,1,0:T(8,128)}, f32[2,16,32,512]{3,2,1,0:T(8,128)S(1)}, u32[]{:S(2)}, u32[]{:S(2)}) collective-permute-start(f32[2,16,32,512]{3,2,1,0:T(8,128)} %mirror.2), channel_id=1, source_target_pairs={{0,7},{1,6},{2,5},{3,4},{4,3},{5,2},{6,1},{7,0},{8,15},{9,14},{10,... | collective-permute-start | bytes 6291464 | tf_op jit(solution)/shard_map/ppermute | solution.py:665
  122.1 1.4 copy-start.2
  123.4 53.2 %all-to-all-start.1 = ((f32[8,2,16,32,128]{4,3,2,1,0:T(8,128)}), f32[8,2,16,32,128]{4,3,2,1,0:T(8,128)}, u32[]{:S(2)}, u32[]{:S(2)}) async-start(f32[8,2,16,32,128]{4,3,2,1,0:T(8,128)} %spread.5), calls=%async_computation.1 | async-start | bytes 8388608 | tf_op jit(solution)/shard_map/all_to_all | solution.py:648
  176.6 30.2 %all-to-all-start.2 = ((f32[8,2,8,32,128]{4,3,2,1,0:T(8,128)}), f32[8,2,8,32,128]{4,3,2,1,0:T(8,128)S(1)}, u32[]{:S(2)}, u32[]{:S(2)}) async-start(f32[8,2,8,32,128]{4,3,2,1,0:T(8,128)} %spread.6), calls=%async_computation.2 | async-start | bytes 4194304 | tf_op jit(solution)/shard_map/all_to_all | solution.py:648
  183.0 30.3 %collective-permute-start.3 = (f32[1,64,512]{2,1,0:T(8,128)S(1)}, f32[1,64,512]{2,1,0:T(8,128)S(1)}, u32[]{:S(2)}, u32[]{:S(2)}) collective-permute-start(f32[1,64,512]{2,1,0:T(8,128)S(1)} %get-tuple-element.136), channel_id=1, source_target_pairs={{0,8},{8,16},{16,24},{1,9},{9,17},{17,25},{2,10},{10,18},{18,26},{... | collective-permute-start | bytes 393224 | tf_op jit(solution)/shard_map/ppermute | solution.py:516
  186.6 26.7 %collective-permute-start.4 = (f32[1,64,512]{2,1,0:T(8,128)S(1)}, f32[1,64,512]{2,1,0:T(8,128)}, u32[]{:S(2)}, u32[]{:S(2)}) collective-permute-start(f32[1,64,512]{2,1,0:T(8,128)S(1)} %get-tuple-element.135), channel_id=1, source_target_pairs={{8,0},{16,8},{24,16},{9,1},{17,9},{25,17},{10,2},{18,10},{26,18},{... | collective-permute-start | bytes 393224 | tf_op jit(solution)/shard_map/ppermute | solution.py:517
  189.3 23.9 %collective-permute-start.5 = (f32[4,1,512]{2,1,0:T(1,128)}, f32[4,1,512]{2,1,0:T(1,128)S(1)}, u32[]{:S(2)}, u32[]{:S(2)}) collective-permute-start(f32[4,1,512]{2,1,0:T(1,128)} %get-tuple-element.134), channel_id=1, source_target_pairs={{0,1},{1,2},{2,3},{3,4},{4,5},{5,6},{6,7},{8,9},{9,10},{10,11},{11... | collective-permute-start | bytes 24584 | tf_op jit(solution)/shard_map/ppermute | solution.py:516
  193.0 20.3 %collective-permute-start.6 = (f32[4,1,512]{2,1,0:T(1,128)}, f32[4,1,512]{2,1,0:T(1,128)}, u32[]{:S(2)}, u32[]{:S(2)}) collective-permute-start(f32[4,1,512]{2,1,0:T(1,128)} %get-tuple-element.133), channel_id=1, source_target_pairs={{1,0},{2,1},{3,2},{4,3},{5,4},{6,5},{7,6},{9,8},{10,9},{11,10},{12... | collective-permute-start | bytes 24584 | tf_op jit(solution)/shard_map/ppermute | solution.py:517
  206.8 1.3 copy-start.1
  208.1 30.3 %all-to-all-start.3 = ((f32[8,2,8,32,128]{4,3,2,1,0:T(8,128)}), f32[8,2,8,32,128]{4,3,2,1,0:T(8,128)S(1)}, u32[]{:S(2)}, u32[]{:S(2)}) async-start(f32[8,2,8,32,128]{4,3,2,1,0:T(8,128)} %spread.7), calls=%async_computation.3 | async-start | bytes 4194304 | tf_op jit(solution)/shard_map/all_to_all | solution.py:648
  213.2 7.8 %copy-start.8 = (f32[3,2]{0,1:T(2,128)S(1)}, f32[3,2]{0,1:T(2,128)}, u32[]{:S(2)}) copy-start(f32[3,2]{0,1:T(2,128)} %param.50) | copy-start | bytes 76
  213.3 35.3 %reduce-scatter.7.cloned.1.call-start = ((), (), s32[]{:S(2)}) async-start(), calls=%async_computation.13 | async-start | bytes 1310720 | tf_op jit(solution)/shard_map/reduce_scatter | solution.py:696
  221.0 54.7 %reduce-scatter.5.cloned.1.call-start = ((), (), s32[]{:S(2)}) async-start(), calls=%async_computation.12 | async-start | bytes 1310720 | tf_op jit(solution)/shard_map/reduce_scatter | solution.py:696
  238.4 1.3 copy-start
  247.5 80.7 %all-gather.7.cloned.1.call-start = ((), (), s32[]{:S(2)}) async-start(), calls=%async_computation.17 | async-start | bytes 1392640 | tf_op jit(solution)/shard_map/all_gather | solution.py:682
  291.9 22.6 %collective-permute-start.7 = (f32[136,512]{1,0:T(8,128)}, f32[136,512]{1,0:T(8,128)S(1)}, u32[]{:S(2)}, u32[]{:S(2)}) collective-permute-start(f32[136,512]{1,0:T(8,128)} %forward_x.5.refs_1_), channel_id=1, source_target_pairs={{0,24},{8,0},{16,8},{24,16},{1,25},{9,1},{17,9},{25,17},{2,26},{10... | collective-permute-start | bytes 835592 | tf_op jit(solution)/shard_map/ppermute | solution.py:684
  294.2 27.9 %collective-permute-start.8 = (f32[136,512]{1,0:T(8,128)}, f32[136,512]{1,0:T(8,128)S(1)}, u32[]{:S(2)}, u32[]{:S(2)}) collective-permute-start(f32[136,512]{1,0:T(8,128)} %forward_x.5.refs_1_), channel_id=1, source_target_pairs={{0,16},{8,24},{16,0},{24,8},{1,17},{9,25},{17,1},{25,9},{2,18},{10... | collective-permute-start | bytes 835592 | tf_op jit(solution)/shard_map/ppermute | solution.py:684
  295.0 33.1 %collective-permute-start.9 = (f32[136,512]{1,0:T(8,128)}, f32[136,512]{1,0:T(8,128)S(1)}, u32[]{:S(2)}, u32[]{:S(2)}) collective-permute-start(f32[136,512]{1,0:T(8,128)} %forward_x.5.refs_1_), channel_id=1, source_target_pairs={{0,8},{8,16},{16,24},{24,0},{1,9},{9,17},{17,25},{25,1},{2,10},{10... | collective-permute-start | bytes 835592 | tf_op jit(solution)/shard_map/ppermute | solution.py:684
  314.6 13.5 %copy-start.13 = (f32[136,512]{1,0:T(8,128)}, f32[136,512]{1,0:T(8,128)S(1)}, u32[]{:S(2)}) copy-start(f32[136,512]{1,0:T(8,128)S(1)} %collective-permute-done.7.refs_2_) | copy-start | bytes 835588
  322.1 6.0 %copy-start.14 = (f32[136,512]{1,0:T(8,128)}, f32[136,512]{1,0:T(8,128)S(1)}, u32[]{:S(2)}) copy-start(f32[136,512]{1,0:T(8,128)S(1)} %collective-permute-done.8.refs_3_) | copy-start | bytes 835588
  328.1 0.7 copy-start.15
  346.7 52.6 %all-to-all-start.6 = ((f32[8,4,8,32,128]{4,3,2,1,0:T(8,128)}), f32[8,4,8,32,128]{4,3,2,1,0:T(8,128)}, u32[]{:S(2)}, u32[]{:S(2)}) async-start(f32[8,4,8,32,128]{4,3,2,1,0:T(8,128)} %spread.8), calls=%async_computation.8 | async-start | bytes 8388608 | tf_op jit(solution)/shard_map/all_to_all | solution.py:648
  399.3 53.7 %all-to-all-start.7 = ((f32[8,4,8,32,128]{4,3,2,1,0:T(8,128)}), f32[8,4,8,32,128]{4,3,2,1,0:T(8,128)}, u32[]{:S(2)}, u32[]{:S(2)}) async-start(f32[8,4,8,32,128]{4,3,2,1,0:T(8,128)} %spread.9), calls=%async_computation.10 | async-start | bytes 8388608 | tf_op jit(solution)/shard_map/all_to_all | solution.py:648
  405.3 59.8 %reduce-scatter.9.cloned.1.call-start = ((), (), s32[]{:S(2)}) async-start(), calls=%async_computation.14 | async-start | bytes 1310720 | tf_op jit(solution)/shard_map/reduce_scatter | solution.py:696
  413.0 47.6 %copy-start.3 = (f32[64,4,512]{2,0,1:T(8,128)S(1)}, f32[64,4,512]{2,0,1:T(8,128)}, u32[]{:S(2)}) copy-start(f32[64,4,512]{2,0,1:T(8,128)} %copy.69) | copy-start | bytes 1572868
  413.1 76.0 %reduce-scatter.11.cloned.1.call-start = ((), (), s32[]{:S(2)}) async-start(), calls=%async_computation.15 | async-start | bytes 1310720 | tf_op jit(solution)/shard_map/reduce_scatter | solution.py:696
  460.6 3.7 copy-start.5
  467.5 15.2 %collective-permute-start.12 = (f32[1,64,512]{2,1,0:T(8,128)}, f32[1,64,512]{2,1,0:T(8,128)S(1)}, u32[]{:S(2)}, u32[]{:S(2)}) collective-permute-start(f32[1,64,512]{2,1,0:T(8,128)} %get-tuple-element.102), channel_id=1, source_target_pairs={{8,0},{16,8},{24,16},{9,1},{17,9},{25,17},{10,2},{18,10},{26,18},{... | collective-permute-start | bytes 393224 | tf_op jit(solution)/shard_map/ppermute | solution.py:603
  472.9 5.7 %collective-permute-start.10 = (f32[2,1,512]{2,1,0:T(1,128)}, f32[2,1,512]{2,1,0:T(1,128)S(1)}, u32[]{:S(2)}, u32[]{:S(2)}) collective-permute-start(f32[2,1,512]{2,1,0:T(1,128)} %get-tuple-element.100), channel_id=1, source_target_pairs={{0,1},{1,2},{2,3},{3,4},{4,5},{5,6},{6,7},{8,9},{9,10},{10,11},{11... | collective-permute-start | bytes 12296 | tf_op jit(solution)/shard_map/ppermute | solution.py:598
  476.6 6.0 %collective-permute-start.11 = (f32[2,1,512]{2,1,0:T(1,128)}, f32[2,1,512]{2,1,0:T(1,128)S(1)}, u32[]{:S(2)}, u32[]{:S(2)}) collective-permute-start(f32[2,1,512]{2,1,0:T(1,128)} %get-tuple-element.101), channel_id=1, source_target_pairs={{1,0},{2,1},{3,2},{4,3},{5,4},{6,5},{7,6},{9,8},{10,9},{11,10},{12... | collective-permute-start | bytes 12296 | tf_op jit(solution)/shard_map/ppermute | solution.py:599
  478.5 26.6 %copy-start.9 = (f32[2,1,512]{2,1,0:T(1,128)}, f32[2,1,512]{2,1,0:T(1,128)S(1)}, u32[]{:S(2)}) copy-start(f32[2,1,512]{2,1,0:T(1,128)S(1)} %collective-permute-done.10.refs_4_) | copy-start | bytes 12292
  482.6 22.5 %copy-start.10 = (f32[2,1,512]{2,1,0:T(1,128)}, f32[2,1,512]{2,1,0:T(1,128)S(1)}, u32[]{:S(2)}) copy-start(f32[2,1,512]{2,1,0:T(1,128)S(1)} %collective-permute-done.11.refs_6_) | copy-start | bytes 12292
  482.6 22.5 %copy-start.6 = (f32[1,64,512]{2,1,0:T(8,128)}, f32[1,64,512]{2,1,0:T(8,128)S(1)}, u32[]{:S(2)}) copy-start(f32[1,64,512]{2,1,0:T(8,128)S(1)} %collective-permute-done.12.refs_9_) | copy-start | bytes 393220
  491.4 13.7 %collective-permute-start.15 = (f32[1,64,512]{2,1,0:T(8,128)}, f32[1,64,512]{2,1,0:T(8,128)S(1)}, u32[]{:S(2)}, u32[]{:S(2)}) collective-permute-start(f32[1,64,512]{2,1,0:T(8,128)} %get-tuple-element.114), channel_id=1, source_target_pairs={{0,8},{8,16},{16,24},{1,9},{9,17},{17,25},{2,10},{10,18},{18,26},{... | collective-permute-start | bytes 393224 | tf_op jit(solution)/shard_map/ppermute | solution.py:609
  495.2 8.0 %collective-permute-start.13 = (f32[2,1,512]{2,1,0:T(1,128)}, f32[2,1,512]{2,1,0:T(1,128)S(1)}, u32[]{:S(2)}, u32[]{:S(2)}) collective-permute-start(f32[2,1,512]{2,1,0:T(1,128)} %get-tuple-element.111), channel_id=1, source_target_pairs={{0,1},{1,2},{2,3},{3,4},{4,5},{5,6},{6,7},{8,9},{9,10},{10,11},{11... | collective-permute-start | bytes 12296 | tf_op jit(solution)/shard_map/ppermute | solution.py:598
  499.1 6.0 %collective-permute-start.14 = (f32[2,1,512]{2,1,0:T(1,128)}, f32[2,1,512]{2,1,0:T(1,128)S(1)}, u32[]{:S(2)}, u32[]{:S(2)}) collective-permute-start(f32[2,1,512]{2,1,0:T(1,128)} %get-tuple-element.113), channel_id=1, source_target_pairs={{1,0},{2,1},{3,2},{4,3},{5,4},{6,5},{7,6},{9,8},{10,9},{11,10},{12... | collective-permute-start | bytes 12296 | tf_op jit(solution)/shard_map/ppermute | solution.py:599
  503.2 1.9 copy-start.11
  505.1 0.6 copy-start.12
  505.1 0.7 copy-start.7
Sparse Core Ops, SparseCore 0:
  31.0 45.0 all-gather.4
  221.1 26.2 reduce-scatter.6
  249.9 25.7 reduce-scatter.4
  277.1 43.5 all-gather.6
  413.2 26.2 reduce-scatter.8
  460.8 28.2 reduce-scatter.10
